TPU v7x, 32 devices: a whole 2x2x4 slice. The times are simulated.
32 devices in a mesh: dp: 4 (over z), fsdp: 8 (over y, x, core).
Axes of the slice: x: 2, y: 2, z: 4, core: 2. Of those that a mesh axis runs over, the one named last changes fastest.
Arguments:
- inputs: float32 [32768, 768], P(('dp', 'fsdp')), may hold values from -6 to 6
- lengths: int32 [64], P(('dp', 'fsdp')), may hold values from 1 to 512, as said below
- query_weight: bfloat16 [768, 768], P(('dp', 'fsdp')), may hold values from -0.21875 to 0.21875
- key_weight: bfloat16 [768, 768], P(('dp', 'fsdp')), may hold values from -0.21875 to 0.21875
- value_weight: bfloat16 [768, 768], P(('dp', 'fsdp')), may hold values from -0.21875 to 0.21875
- out_weight: bfloat16 [768, 768], P(('dp', 'fsdp')), may hold values from -1.75 to 1.75
- query_bias: bfloat16 [768], P(('dp', 'fsdp')), may hold values from -1.5 to 1.5
- value_bias: bfloat16 [768], P(('dp', 'fsdp')), may hold values from -1.5 to 1.5
- out_bias: bfloat16 [768], P(('dp', 'fsdp')), may hold values from -1.5 to 1.5
- first_gain: bfloat16 [768], P(('dp', 'fsdp')), may hold values from 0.5 to 1.5
- first_shift: bfloat16 [768], P(('dp', 'fsdp')), may hold values from -1.5 to 1.5
- inner_weight: bfloat16 [768, 3072], P(('dp', 'fsdp')), may hold values from -0.21875 to 0.21875
- inner_bias: bfloat16 [3072], P(('dp', 'fsdp')), may hold values from -1.5 to 1.5
- down_weight: bfloat16 [3072, 768], P(('dp', 'fsdp')), may hold values from -0.109375 to 0.109375
- down_bias: bfloat16 [768], P(('dp', 'fsdp')), may hold values from -1.5 to 1.5
- second_gain: bfloat16 [768], P(('dp', 'fsdp')), may hold values from 0.5 to 1.5
- second_shift: bfloat16 [768], P(('dp', 'fsdp')), may hold values from -1.5 to 1.5
- cotangent: float32 [32768, 768], P(('dp', 'fsdp')), may hold values from -6 to 6
Outputs:
- output: float32 [32768, 768], P(('dp', 'fsdp'))
- grad_input: float32 [32768, 768], P(('dp', 'fsdp'))
- grad_query_weight: float32 [768, 768], P(('dp', 'fsdp'))
- grad_key_weight: float32 [768, 768], P(('dp', 'fsdp'))
- grad_value_weight: float32 [768, 768], P(('dp', 'fsdp'))
- grad_out_weight: float32 [768, 768], P(('dp', 'fsdp'))
- grad_query_bias: float32 [768], P(('dp', 'fsdp'))
- grad_value_bias: float32 [768], P(('dp', 'fsdp'))
- grad_out_bias: float32 [768], P(('dp', 'fsdp'))
- grad_first_gain: float32 [768], P(('dp', 'fsdp'))
- grad_first_shift: float32 [768], P(('dp', 'fsdp'))
- grad_inner_weight: float32 [768, 3072], P(('dp', 'fsdp'))
- grad_inner_bias: float32 [3072], P(('dp', 'fsdp'))
- grad_down_weight: float32 [3072, 768], P(('dp', 'fsdp'))
- grad_down_bias: float32 [768], P(('dp', 'fsdp'))
- grad_second_gain: float32 [768], P(('dp', 'fsdp'))
- grad_second_shift: float32 [768], P(('dp', 'fsdp'))
Inputs may be any that keep to these rules, and one draw needn't show every extreme that they name: `lengths`: positions of a pair below its entry are tokens, the rest padding; some pair has all 512 positions valid.
All inputs are finite; a program needn't handle non-finite values.
Results may differ from a plain program's by a relative error of at most 0.014.
The roundings to bfloat16 on the way count: a program that leaves them out, or rounds other values in their place, can miss the bound.
Values may be sent and summed in bfloat16 or wider, within the bound.
No kernel may reach another device: no remote copies, remote signals or barrier semaphores. Data moves between devices by JAX's collectives and lax.ppermute only.
A program may use at most 192 MiB of HBM per device.

v0:
```python
import functools
import math

import jax
import jax.numpy as jnp
import numpy as np
from jax import lax
from jax.experimental import pallas as pl
from jax.experimental.pallas import tpu as pltpu
from jax.sharding import PartitionSpec as P

D = 768
H = 12
DH = 64
FF = 3072
SLABS = 32
SLAB = D // SLABS
CHIPS = SLABS // 2
PAIR_ROWS = 2 * SLAB
NORM_EPSILON = 1e-12
MASKED_SCORE = -1000000000.0
GAUSS_DENSITY = 0.3989422804014327
LOG2E = 1.4426950408889634
MIB = 1 << 20
VMEM = 62 * MIB
ALL_VMEM = 127 * MIB // 2
LITTLE = 16 * MIB

QKV_HALF = 3 * D // 2
QKV_BLOCK = QKV_HALF + 128
OUT_HALF = D // 2
PROJ_BLOCK = QKV_BLOCK + OUT_HALF
INNER_HALF = FF // 2
INNER_BLOCK = OUT_HALF + INNER_HALF
DOWN_BLOCK = 2 * D

SLOT_BITS = ((8, 4, 1, 2), (4, 8, 2, 1))
SLOT_CHIPS = tuple(
    tuple(sum(bit for i, bit in enumerate(bits) if slot >> i & 1) for slot in range(CHIPS)) for bits in SLOT_BITS
)

bf16 = jnp.bfloat16
f32 = jnp.float32
ANY = pl.BlockSpec(memory_space=pl.ANY)
SMEM = pl.BlockSpec(memory_space=pltpu.SMEM)


def dot(a, b):
    return lax.dot_general(a, b, (((1,), (0,)), ((), ())), preferred_element_type=f32)


def dot_t(a, b):
    return lax.dot_general(a, b, (((1,), (1,)), ((), ())), preferred_element_type=f32)


def dot_l(a, b):
    return lax.dot_general(a, b, (((0,), (0,)), ((), ())), preferred_element_type=f32)


def call(kernel, operands, deps, in_specs, **options):
    count = len(operands)

    def body(*refs):
        kernel(*refs[:count], *refs[count + len(deps) :])

    in_specs = in_specs + [whole(8, 128) if v.shape == (8, 128) else ANY for v in deps]
    return pl.pallas_call(body, in_specs=in_specs, **options)(*operands, *deps)


def aligned(start, size, unit):
    return pl.ds(pl.multiple_of(start, unit), size)


def chip_of(slot, half):
    return jnp.where(half == 0, SLOT_CHIPS[0][slot], SLOT_CHIPS[1][slot])


def slot_of(chip, half):
    bits = SLOT_BITS[half]
    return sum(jnp.where((chip & bit) != 0, 1 << i, 0) for i, bit in enumerate(bits))


def blocks_of(place, pieces):
    for ref, (first, other) in pieces:
        half = 1 - place[1] if other else place[1]
        for i in range(ref.shape[0]):
            yield ref, i, place[0] ^ chip_of(first + i, half), half


def proj_blocks(place, pieces, weights, sem):
    for ref, i, chip, half in blocks_of(place, pieces):
        rows = aligned(chip * PAIR_ROWS, PAIR_ROWS, 16)
        yield pltpu.make_async_copy(ref.at[i], weights.at[rows, aligned(half * PROJ_BLOCK, PROJ_BLOCK, 128)], sem)


def inner_blocks(place, pieces, inner_w, sem):
    for ref, i, chip, half in blocks_of(place, pieces):
        rows = aligned(chip * PAIR_ROWS, PAIR_ROWS, 16)
        yield pltpu.make_async_copy(
            ref.at[i, :, pl.ds(0, INNER_HALF)],
            inner_w.at[rows, aligned(half * INNER_HALF, INNER_HALF, 128)],
            sem,
        )


def down_blocks(place, pieces, down_w, sem):
    for ref, i, chip, half in blocks_of(place, pieces):
        for k in range(2):
            at = (chip * 2 + half) * (2 * PAIR_ROWS) + k * PAIR_ROWS
            yield pltpu.make_async_copy(
                ref.at[i, :, pl.ds(INNER_HALF + k * D, D)], down_w.at[aligned(at, PAIR_ROWS, 16), :], sem
            )


def start_all(copies):
    for c in copies:
        c.start()


def whole(*shape):
    return pl.BlockSpec(shape, lambda *s: (0,) * len(shape))


def fold_rows(v):
    return jnp.sum(v.reshape(v.shape[0] // 8, 8, v.shape[1]), axis=0)


def hand_over(place, chip, half, keep, send, pairs, sem):
    slot = slot_of(chip ^ place[0], half)
    for mine, out in ((True, keep), (False, send)):

        @pl.when((place[1] == half) == mine)
        def _():
            for source, lanes in pairs:
                pltpu.make_async_copy(source, out.at[slot, :, lanes], sem).start()


def wait_whole(ref, sem):
    pltpu.make_async_copy(ref, ref, sem).wait()


def lane_masks():
    low = (lax.broadcasted_iota(jnp.int32, (1, 128), 1) < DH).astype(f32)
    return low.astype(bf16), (1.0 - low).astype(bf16)


def attend_kernel(meta, n_pieces, place, lengths, x_ref, *refs):
    piece_refs = refs[:n_pieces]
    qkv_ref, att_ref, stat_ref, weights, vectors = refs[n_pieces : n_pieces + 5]
    sem = refs[-1]
    seq = pl.program_id(0)
    rows = x_ref.shape[0]

    @pl.when(seq == 0)
    def _():
        start_all(proj_blocks(place, zip(piece_refs, meta), weights, sem))
        wait_whole(weights, sem)
        small = weights[:, QKV_HALF:QKV_BLOCK].astype(f32)
        vectors[...] = small.T[0:16, :]

    lowered = x_ref[...].astype(bf16)
    first = dot(lowered, weights[:, 0:QKV_HALF])
    qkv_ref[:, 0:D] = (first[:, 0:D] + vectors[0:1, :]).astype(bf16)
    qkv_ref[:, D:QKV_HALF] = first[:, D:QKV_HALF].astype(bf16)
    second = dot(lowered, weights[:, PROJ_BLOCK : PROJ_BLOCK + QKV_HALF])
    qkv_ref[:, QKV_HALF : 2 * D] = second[:, 0 : D // 2].astype(bf16)
    qkv_ref[:, 2 * D :] = (second[:, D // 2 :] + vectors[1:2, :]).astype(bf16)

    low, high = lane_masks()
    lane = lax.broadcasted_iota(jnp.int32, (1, 128), 1)
    key_at = lax.broadcasted_iota(jnp.int32, (1, rows), 1)
    hidden_keys = jnp.where(key_at < lengths[seq], 0.0, MASKED_SCORE).astype(f32)
    chunk = 256
    ones = jnp.ones((rows, 128), bf16)
    stats = [jnp.zeros((chunk, 128), f32) for _ in range(rows // chunk)]
    for pair in range(H // 2):
        at = pair * 128
        keys = qkv_ref[:, D + at : D + at + 128]
        values = jnp.concatenate([qkv_ref[:, 2 * D + at : 2 * D + at + 128], ones], axis=1)
        keys_of = (keys * low, keys * high)
        for c in range(rows // chunk):
            span = pl.ds(c * chunk, chunk)
            queries = qkv_ref[span, at : at + 128]
            outs = []
            for i in range(2):
                scores = dot_t(queries, keys_of[i]) * (0.125 * LOG2E) + hidden_keys
                peak = jnp.max(scores, axis=-1, keepdims=True)
                weight = jnp.exp2(scores - peak).astype(bf16)
                both = dot(weight, values)
                total = both[:, 128:]
                outs.append(both[:, :128] / total)
                log_total = peak + jnp.log2(total)
                stats[c] = jnp.where(lane == 2 * pair + i, log_total, stats[c])
            att_ref[span, at : at + 128] = jnp.where(lane < DH, outs[0], outs[1]).astype(bf16)
    for c in range(rows // chunk):
        stat_ref[0, :, c * chunk : (c + 1) * chunk] = stats[c].T[0:16, :]


def attend(place, lengths, x, pieces, meta):
    rows = x.shape[0] // lengths.shape[0]
    seqs = lengths.shape[0]
    return pl.pallas_call(
        functools.partial(attend_kernel, meta, len(pieces)),
        grid=(seqs,),
        in_specs=[SMEM, SMEM, pl.BlockSpec((rows, D), lambda s: (s, 0))] + [ANY] * len(pieces),
        out_specs=[
            pl.BlockSpec((rows, 3 * D), lambda s: (s, 0)),
            pl.BlockSpec((rows, D), lambda s: (s, 0)),
            pl.BlockSpec((1, 16, rows), lambda s: (s, 0, 0)),
            whole(D, 2 * PROJ_BLOCK),
            whole(16, D),
        ],
        out_shape=[
            jax.ShapeDtypeStruct((seqs * rows, 3 * D), bf16),
            jax.ShapeDtypeStruct((seqs * rows, D), bf16),
            jax.ShapeDtypeStruct((seqs, 16, rows), f32),
            jax.ShapeDtypeStruct((D, 2 * PROJ_BLOCK), bf16),
            jax.ShapeDtypeStruct((16, D), f32),
        ],
        scratch_shapes=[pltpu.SemaphoreType.DMA],
        compiler_params=pltpu.CompilerParams(vmem_limit_bytes=VMEM),
        cost_estimate=pl.CostEstimate(flops=18_000_000_000, bytes_accessed=20 * MIB, transcendentals=0),
        name="attend",
    )(place, lengths, x, *pieces)


def gelu_parts(u):
    size = jnp.abs(u)
    bell = jnp.exp2(u * u * (-0.5 * LOG2E))
    t = 1.0 / (1.0 + (0.3275911 * math.sqrt(0.5)) * size)
    poly = t * (0.127414796 + t * (-0.142248368 + t * (0.7107068705 + t * (-0.7265760135 + t * 0.5307027145))))
    tail = poly * bell
    below = jnp.where(u < 0.0, tail, 1.0 - tail)
    return below, bell


def mean_rows(v):
    return jnp.sum(v, axis=-1, keepdims=True) * (1.0 / D)


def norm_rows(total):
    center = total - mean_rows(total)
    rstd = lax.rsqrt(mean_rows(center * center) + NORM_EPSILON)
    return center * rstd, rstd


def norm_back(upstream, normed, rstd, gain):
    scaled = upstream * gain
    return rstd * (scaled - mean_rows(scaled) - normed * mean_rows(scaled * normed))


BLOCK = 256
WIDTH = 768
DOWN_STEPS = 8


def out_weight_copies(proj_w, out_w, sem):
    for half in range(2):
        lanes = pl.ds(half * PROJ_BLOCK + QKV_BLOCK, OUT_HALF)
        yield pltpu.make_async_copy(proj_w.at[:, lanes], out_w.at[:, pl.ds(half * OUT_HALF, OUT_HALF)], sem)


def probs_kernel(seq, lengths, q_ref, k_ref, stat_ref, *refs):
    prob_ref = refs[-1]
    pair = pl.program_id(0)
    rows = q_ref.shape[0]
    chunk = 256
    key_at = lax.broadcasted_iota(jnp.int32, (rows, 1), 0)
    hidden_keys = jnp.where(key_at < lengths[seq], 0.0, MASKED_SCORE).astype(f32)
    for i, mask in enumerate(lane_masks()):
        own_keys = k_ref[...] * mask
        for c in range(rows // chunk):
            span = slice(c * chunk, (c + 1) * chunk)
            log_total = stat_ref[0, pl.ds(2 * pair + i, 1), span]
            scores = dot_t(own_keys, q_ref[span, :]) * (0.125 * LOG2E) + hidden_keys
            prob_ref[i, :, span] = jnp.exp2(scores - log_total).astype(bf16)


def probs_specs(seq, rows):
    pairs = H // 2
    lane = lambda kind: pl.BlockSpec((rows, 128), lambda s: (seq, kind * pairs + s))
    specs = [SMEM, lane(0), lane(1), pl.BlockSpec((1, 16, rows), lambda s: (seq, 0, 0))]
    return specs, pl.BlockSpec((2, rows, rows), lambda s: (seq * pairs + s, 0, 0))


def probs(seq, lengths, qkv, stats, deps=()):
    seqs, _, rows = stats.shape
    specs, out = probs_specs(seq, rows)
    return call(
        functools.partial(probs_kernel, seq),
        (lengths, qkv, qkv, stats),
        deps,
        grid=(H // 2,),
        in_specs=specs,
        out_specs=out,
        out_shape=jax.ShapeDtypeStruct((seqs * H, rows, rows), bf16),
        compiler_params=pltpu.CompilerParams(vmem_limit_bytes=VMEM),
        cost_estimate=pl.CostEstimate(flops=8_000_000_000, bytes_accessed=MIB, transcendentals=0),
        name="probs",
    )


def window_kernel(seq, blocks, lengths, q_ref, k_ref, stat_ref, _, x_ref, att_ref, vec_ref, proj_w, *refs):
    prob_ref, normed_ref, rstd_ref, hid_ref, x_t, att_t, hid_t, out_w, sem = refs
    g = pl.program_id(0)

    @pl.when(g == 0)
    def _():
        start_all(out_weight_copies(proj_w, out_w, sem))

    probs_kernel(seq, lengths, q_ref, k_ref, stat_ref, prob_ref)

    @pl.when(g == 0)
    def _():
        wait_whole(out_w, sem)

    @pl.when(g < blocks)
    def _():
        x, attended = x_ref[...], att_ref[...]
        normed, rstd = norm_rows(x + dot(attended, out_w[...]) + vec_ref[2:3, :])
        normed_ref[...] = normed
        rstd_ref[...] = jnp.broadcast_to(rstd, rstd_ref.shape)
        hidden = normed * vec_ref[3:4, :] + vec_ref[4:5, :]
        hid_ref[...] = hidden.astype(bf16)
        x_t[...] = x.T.astype(bf16)
        att_t[...] = attended.astype(f32).T.astype(bf16)
        hid_t[...] = hidden.T.astype(bf16)


def window(seq, lengths, x, qkv, attended, stats, weights, vectors, prob, deps=()):
    count = x.shape[0]
    _, _, rows = stats.shape
    blocks = count // BLOCK
    block = lambda s: jnp.minimum(s, blocks - 1)
    token = lambda width: pl.BlockSpec((BLOCK, width), lambda s: (block(s), 0))
    turned = pl.BlockSpec((D, BLOCK), lambda s: (0, block(s)))
    specs, out = probs_specs(seq, rows)
    return call(
        functools.partial(window_kernel, seq, blocks),
        (lengths, qkv, qkv, stats, prob, x, attended, vectors, weights),
        deps,
        grid=(H // 2,),
        in_specs=specs + [ANY, token(D), token(D), whole(16, D), ANY],
        out_specs=[out, token(D), token(128), token(D)] + [turned] * 3,
        out_shape=[
            jax.ShapeDtypeStruct(prob.shape, bf16),
            jax.ShapeDtypeStruct((count, D), f32),
            jax.ShapeDtypeStruct((count, 128), f32),
            jax.ShapeDtypeStruct((count, D), bf16),
        ]
        + [jax.ShapeDtypeStruct((D, count), bf16)] * 3,
        input_output_aliases={4: 0},
        scratch_shapes=[pltpu.VMEM((D, D), bf16), pltpu.SemaphoreType.DMA],
        compiler_params=pltpu.CompilerParams(vmem_limit_bytes=VMEM),
        cost_estimate=pl.CostEstimate(flops=14_000_000_000, bytes_accessed=MIB, transcendentals=0),
        name="window",
    )


def ffn_kernel(meta, pieces, blocks, place, normed_ref, rstd_ref, hid_ref, cot_ref, vec_ref, b1_ref, proj_w, *refs):
    piece_refs = refs[:pieces]
    (out_ref, fb_ref, ab_ref, ib_ref, branch_ref, small_ref, db1_ref, keep, send) = refs[pieces : pieces + 9]
    (out_w, inner_w, down_w, act, down_back, sem, wsem) = refs[pieces + 9 :]
    step = pl.program_id(0)

    @pl.when(step == 0)
    def _():
        start_all(inner_blocks(place, zip(piece_refs, meta), inner_w, sem.at[0]))
        start_all(down_blocks(place, zip(piece_refs, meta), down_w, sem.at[1]))
        start_all(out_weight_copies(proj_w, out_w, sem.at[2]))
        small_ref[...] = jnp.zeros_like(small_ref)
        db1_ref[...] = jnp.zeros_like(db1_ref)
        wait_whole(inner_w, sem.at[0])
        wait_whole(down_w, sem.at[1])
        wait_whole(out_w, sem.at[2])

    @pl.when(step < blocks)
    def _():
        rows = aligned(step * BLOCK, BLOCK, BLOCK)
        first_gain, first_shift = vec_ref[3:4, :], vec_ref[4:5, :]
        second_gain, second_shift = vec_ref[6:7, :], vec_ref[7:8, :]
        first_normed = normed_ref[...]
        hidden_low = hid_ref[...]
        total = first_normed * first_gain + first_shift + vec_ref[5:6, :]
        slopes = []
        for c in range(FF // WIDTH):
            cols = pl.ds(c * WIDTH, WIDTH)
            u = dot(hidden_low, inner_w[:, cols]) + b1_ref[:, cols]
            below, bell = gelu_parts(u)
            active = (u * below).astype(bf16)
            act[rows, cols] = active
            slopes.append(below + u * bell * GAUSS_DENSITY)
            total = total + dot(active, down_w[cols, :])
        second_normed, second_rstd = norm_rows(total)
        out_ref[...] = second_normed * second_gain + second_shift
        cot = cot_ref[...]
        second_back = norm_back(cot, second_normed, second_rstd, second_gain)
        back_low = second_back.astype(bf16)
        down_back[rows, :] = back_low
        hidden_back = second_back
        for c in range(FF // WIDTH):
            cols = pl.ds(c * WIDTH, WIDTH)
            ib = (dot_t(back_low, down_w[cols, :]) * slopes[c]).astype(bf16)
            ib_ref[:, cols] = ib
            db1_ref[:, cols] += fold_rows(ib.astype(f32))
            hidden_back = hidden_back + dot_t(ib, inner_w[:, cols])
        first_back = norm_back(hidden_back, first_normed, rstd_ref[:, 0:1], first_gain)
        fb_ref[...] = first_back
        branch_low = first_back.astype(bf16)
        branch_ref[...] = branch_low
        ab_ref[...] = dot_t(branch_low, out_w[...]).astype(bf16)
        sums = (
            branch_low.astype(f32),
            hidden_back * first_normed,
            hidden_back,
            back_low.astype(f32),
            cot * second_normed,
            cot,
        )
        for i, v in enumerate(sums):
            small_ref[i] += fold_rows(v)

    @pl.when(step >= blocks)
    def _():
        chunk = step - blocks
        width = FF // DOWN_STEPS
        rows = aligned(chunk * width, width, 128)
        down_w[rows, :] = dot_l(act[:, rows], down_back[...]).astype(bf16)
        for i in range(CHIPS // DOWN_STEPS):
            chip = chunk * (CHIPS // DOWN_STEPS) + i
            for half in range(2):
                at = (chip * 2 + half) * (2 * PAIR_ROWS)
                pairs = [
                    (down_w.at[aligned(at + k * PAIR_ROWS, PAIR_ROWS, 16)], pl.ds(k * D, D)) for k in range(2)
                ]
                hand_over(place, chip, half, keep, send, pairs, wsem)

    @pl.when(step == blocks + DOWN_STEPS - 1)
    def _():
        wait_whole(keep, wsem)
        wait_whole(send, wsem)


def feed_forward(place, normed, rstd, hid, cotangent, vectors, inner_bias, weights, pieces, meta):
    count = normed.shape[0]
    blocks = count // BLOCK
    token = lambda width: pl.BlockSpec((BLOCK, width), lambda s: (jnp.minimum(s, blocks - 1), 0))
    return pl.pallas_call(
        functools.partial(ffn_kernel, meta, len(pieces), blocks),
        grid=(blocks + DOWN_STEPS,),
        in_specs=[SMEM, token(D), token(128), token(D), token(D), whole(16, D), whole(1, FF), ANY]
        + [ANY] * len(pieces),
        out_specs=[token(D), token(D), token(D), token(FF), token(D), whole(6, 8, D), whole(8, FF), ANY, ANY],
        out_shape=[
            jax.ShapeDtypeStruct((count, D), f32),
            jax.ShapeDtypeStruct((count, D), f32),
            jax.ShapeDtypeStruct((count, D), bf16),
            jax.ShapeDtypeStruct((count, FF), bf16),
            jax.ShapeDtypeStruct((count, D), bf16),
            jax.ShapeDtypeStruct((6, 8, D), f32),
            jax.ShapeDtypeStruct((8, FF), f32),
            jax.ShapeDtypeStruct((CHIPS, PAIR_ROWS, DOWN_BLOCK), bf16),
            jax.ShapeDtypeStruct((CHIPS, PAIR_ROWS, DOWN_BLOCK), bf16),
        ],
        scratch_shapes=[
            pltpu.VMEM((D, D), bf16),
            pltpu.VMEM((D, FF), bf16),
            pltpu.VMEM((FF, D), bf16),
            pltpu.VMEM((count, FF), bf16),
            pltpu.VMEM((count, D), bf16),
            pltpu.SemaphoreType.DMA((3,)),
            pltpu.SemaphoreType.DMA,
        ],
        compiler_params=pltpu.CompilerParams(vmem_limit_bytes=ALL_VMEM),
        cost_estimate=pl.CostEstimate(flops=52_000_000_000, bytes_accessed=40 * MIB, transcendentals=0),
        name="feed_forward",
    )(place, normed, rstd, hid, cotangent, vectors, inner_bias, weights, *pieces)


def inner_grads_kernel(hid_t, ib_ref, place, att_in, branch_in, keep, send, att_t, branch, out_g, inner_g, sem, wsem):
    step = pl.program_id(0)
    steps = FF // D
    later = [pltpu.make_async_copy(att_in, att_t, sem.at[0]), pltpu.make_async_copy(branch_in, branch, sem.at[1])]

    @pl.when(step == 0)
    def _():
        start_all(later)

    def give(grads, half, width, lane):
        for chip in range(CHIPS):
            block = grads.at[pl.ds(chip * PAIR_ROWS, PAIR_ROWS), pl.ds(half * width, width)]
            hand_over(place, chip, half, keep, send, [(block, pl.ds(lane, width))], wsem)

    @pl.when(step < steps)
    def _():
        cols = aligned(step * D, D, 128)
        inner_g[:, cols] = dot(hid_t[...], ib_ref[...]).astype(bf16)
        for half in range(2):

            @pl.when(step == (half + 1) * (steps // 2) - 1)
            def _():
                give(inner_g, half, INNER_HALF, OUT_HALF)

    @pl.when(step == steps)
    def _():
        for copy in later:
            copy.wait()
        out_g[...] = dot(att_t[...], branch[...]).astype(bf16)
        for half in range(2):
            give(out_g, half, OUT_HALF, 0)
        wait_whole(keep, wsem)
        wait_whole(send, wsem)


def inner_grads(place, hid_t, inner_back, att_t, branch):
    count = hid_t.shape[1]
    steps = FF // D
    return pl.pallas_call(
        inner_grads_kernel,
        grid=(steps + 1,),
        in_specs=[
            whole(D, count),
            pl.BlockSpec((count, D), lambda s: (0, jnp.minimum(s, steps - 1))),
            SMEM,
            ANY,
            ANY,
        ],
        out_specs=[ANY, ANY],
        out_shape=[jax.ShapeDtypeStruct((CHIPS, PAIR_ROWS, INNER_BLOCK), bf16)] * 2,
        scratch_shapes=[
            pltpu.VMEM((D, count), bf16),
            pltpu.VMEM((count, D), bf16),
            pltpu.VMEM((D, D), bf16),
            pltpu.VMEM((D, FF), bf16),
            pltpu.SemaphoreType.DMA((2,)),
            pltpu.SemaphoreType.DMA,
        ],
        compiler_params=pltpu.CompilerParams(vmem_limit_bytes=ALL_VMEM),
        cost_estimate=pl.CostEstimate(flops=4_000_000_000, bytes_accessed=MIB, transcendentals=0),
        name="inner_grads",
    )(hid_t, inner_back, place, att_t, branch)


def attend_back_pair(queries, keys, values, upstream, prob_ref, dq_ref, dk_ref, dv_ref):
    lows, backs = [], []
    masks = lane_masks()
    for i, mask in enumerate(masks):
        low = prob_ref[i]
        weight = low.astype(f32)
        weight_back = dot_t(values * mask, upstream)
        mean = jnp.sum(weight * weight_back, axis=0, keepdims=True)
        lows.append(low)
        backs.append((weight * (weight_back - mean)).astype(bf16))
    each = lambda v: jnp.concatenate([v * mask for mask in masks], axis=0)
    dv_ref[...] = dot(jnp.concatenate(lows, axis=1), each(upstream)).astype(bf16)
    dk_ref[...] = (dot(jnp.concatenate(backs, axis=1), each(queries)) * 0.125).astype(bf16)
    dq_ref[...] = (dot_l(jnp.concatenate(backs, axis=0), each(keys)) * 0.125).astype(bf16)


def attend_back_kernel(q_ref, k_ref, v_ref, up_ref, prob_ref, *refs):
    attend_back_pair(q_ref[...], k_ref[...], v_ref[...], up_ref[...], prob_ref, *refs[-3:])


def pair_specs(rows, first, last):
    pairs = H // 2
    pair = lambda s: jnp.minimum(first + s, last)
    lane = lambda kind: pl.BlockSpec((rows, 128), lambda s: (pair(s) // pairs, kind * pairs + pair(s) % pairs))
    return [lane(0), lane(1), lane(2), lane(0), pl.BlockSpec((2, rows, rows), lambda s: (pair(s), 0, 0))]


def attend_back(first, count, qkv, back, prob, grads=(), deps=()):
    specs = pair_specs(prob.shape[1], first, first + count - 1)
    return call(
        attend_back_kernel,
        (qkv, qkv, qkv, back, prob, *grads),
        deps,
        grid=(count,),
        in_specs=specs + [ANY] * len(grads),
        out_specs=[specs[0]] * 3,
        out_shape=[jax.ShapeDtypeStruct(back.shape, bf16)] * 3,
        input_output_aliases={5 + i: i for i in range(len(grads))},
        compiler_params=pltpu.CompilerParams(vmem_limit_bytes=ALL_VMEM),
        cost_estimate=pl.CostEstimate(flops=3_000_000_000, bytes_accessed=MIB, transcendentals=0),
        name=f"attend_back_{first}",
    )


def proj_grads_kernel(place, turned, small_ref, db1_ref, dq, dk, dv, keep, send, grads, packed, bias, sem, wsem):
    step = pl.program_id(0)
    copies = [pltpu.make_async_copy(v, grads.at[i], sem.at[i]) for i, v in enumerate((dq, dk, dv))]

    @pl.when(step == 0)
    def _():
        start_all([copies[1], copies[2], copies[0]])

    for turn, which in enumerate((1, 2, 0)):

        @pl.when(step == turn)
        def _():
            copies[which].wait()
            g = dot(turned[...], grads[which]).astype(bf16)
            if which == 1:
                packed[:, D:QKV_HALF] = g[:, : D // 2]
                packed[:, QKV_BLOCK : QKV_BLOCK + D // 2] = g[:, D // 2 :]
            else:
                at = 0 if which == 0 else QKV_BLOCK + D // 2
                packed[:, at : at + D] = g
                bias[which // 2] = fold_rows(grads[which].astype(f32))

    @pl.when(step == 0)
    def _():
        owner = lax.broadcasted_iota(jnp.int32, (SLABS, FF), 1) // (4 * SLAB)
        one = lax.broadcasted_iota(jnp.int32, (SLABS, FF), 0)
        mine = jnp.where(owner == one, jnp.sum(db1_ref[...], axis=0, keepdims=True), 0.0)
        place_of = lax.broadcasted_iota(jnp.int32, (FF, 128), 0) % (4 * SLAB)
        pick = (place_of == lax.broadcasted_iota(jnp.int32, (FF, 128), 1)).astype(f32)
        table = lax.dot_general(
            mine, pick, (((1,), (0,)), ((), ())), precision=lax.Precision.HIGHEST, preferred_element_type=f32
        )
        spread = jnp.broadcast_to(table[:, None, :], (SLABS, SLAB, 128)).reshape(D, 128)
        packed[:, QKV_BLOCK + QKV_HALF :] = spread.astype(bf16)

    def give(half):
        for chip in range(CHIPS):
            block = packed.at[pl.ds(chip * PAIR_ROWS, PAIR_ROWS), pl.ds(half * QKV_BLOCK, QKV_BLOCK)]
            hand_over(place, chip, half, keep, send, [(block, pl.ds(0, QKV_BLOCK))], wsem)

    @pl.when(step == 1)
    def _():
        give(1)

    @pl.when(step == 2)
    def _():
        rows_of = [bias[...], small_ref[...], jnp.zeros((120, 8, D), f32)]
        packed[:, QKV_HALF:QKV_BLOCK] = jnp.sum(jnp.concatenate(rows_of, axis=0), axis=1).T.astype(bf16)
        give(0)
        wait_whole(keep, wsem)
        wait_whole(send, wsem)


def proj_grads(place, turned, small, inner_bias_grad, grads, deps=()):
    count = turned.shape[1]
    return call(
        proj_grads_kernel,
        (place, turned, small, inner_bias_grad, *grads),
        deps,
        grid=(3,),
        in_specs=[SMEM, whole(D, count), whole(6, 8, D), whole(8, FF), ANY, ANY, ANY],
        out_specs=[ANY, ANY],
        out_shape=[jax.ShapeDtypeStruct((CHIPS, PAIR_ROWS, QKV_BLOCK), bf16)] * 2,
        scratch_shapes=[
            pltpu.VMEM((3, count, D), bf16),
            pltpu.VMEM((D, 2 * QKV_BLOCK), bf16),
            pltpu.VMEM((2, 8, D), f32),
            pltpu.SemaphoreType.DMA((3,)),
            pltpu.SemaphoreType.DMA,
        ],
        compiler_params=pltpu.CompilerParams(vmem_limit_bytes=ALL_VMEM),
        cost_estimate=pl.CostEstimate(flops=4_000_000_000, bytes_accessed=MIB, transcendentals=0),
        name="proj_grads",
    )


def input_back_kernel(fb_ref, dq_ref, dk_ref, dv_ref, w_ref, *refs):
    half = D // 2
    total = fb_ref[...] + dot_t(dq_ref[...], w_ref[:, 0:D])
    total = total + dot_t(dk_ref[:, :half], w_ref[:, D:QKV_HALF])
    total = total + dot_t(dk_ref[:, half:], w_ref[:, PROJ_BLOCK : PROJ_BLOCK + half])
    out_ref, small_ref = refs[-2:]
    small_ref[...] = total[0:8, 0:128]
    out_ref[...] = total + dot_t(dv_ref[...], w_ref[:, PROJ_BLOCK + half : PROJ_BLOCK + QKV_HALF])


def input_back(first, blocks, first_back, grads, weights, given=(), deps=()):
    token = pl.BlockSpec((BLOCK, D), lambda s: (first + s, 0))
    return call(
        input_back_kernel,
        (first_back, *grads, weights, *given),
        deps,
        grid=(blocks,),
        in_specs=[token] * 4 + [whole(D, 2 * PROJ_BLOCK)] + [ANY] * len(given),
        out_specs=[token, whole(8, 128)],
        out_shape=[jax.ShapeDtypeStruct(first_back.shape, f32), jax.ShapeDtypeStruct((8, 128), f32)],
        input_output_aliases={5: 0} if given else {},
        compiler_params=pltpu.CompilerParams(vmem_limit_bytes=ALL_VMEM),
        cost_estimate=pl.CostEstimate(flops=10_000_000_000, bytes_accessed=MIB, transcendentals=0),
        name=f"input_back_{first}",
    )


def add_up_kernel(jobs, passed, place, *refs):
    refs[len(refs) - 1][...] = refs[0][0, 0:8, 0:128].astype(f32)
    first, out = 0, sum(count for count, _ in jobs) + passed
    for count, kind in jobs:
        terms = refs[first : first + count]
        first += count

        def total(slot):
            return sum((ref[slot].astype(f32) for ref in terms[1:]), terms[0][slot].astype(f32))

        slots = terms[0].shape[0]
        if kind == "upper":

            def one(i, _, total=total, ready=refs[out]):
                ready[i] = total(i).astype(bf16)
                return 0

            lax.fori_loop(0, slots, one, 0)
            out += 1
        elif kind == "both":
            half = slots // 2

            def one(i, _, total=total, ready=refs[out], rest=refs[out + 1], half=half):
                rest[i] = total(i)
                ready[i] = total(half + i).astype(bf16)
                return 0

            lax.fori_loop(0, half, one, 0)
            out += 2
        elif kind == "down":
            whole_sum = total(0)
            refs[out][0:PAIR_ROWS, :] = whole_sum[:, :D]
            refs[out][PAIR_ROWS:, :] = whole_sum[:, D:]
            out += 1
        else:
            whole_sum = total(0)
            low_core = place[1] == 0
            low, high = whole_sum[:SLAB], whole_sum[SLAB:]
            refs[out][...] = jnp.where(low_core, low, high)
            refs[out + 1][...] = jnp.where(low_core, high, low)
            out += 2


def add_up(place, *groups, passed=(), deps=(), vmem=ALL_VMEM):
    operands, specs, out_specs, shapes, jobs = [], [], [], [], []
    steps = 3 if any(size == CHIPS for size, _ in groups) else 1
    one_step = all(size > 1 for size, _ in groups)
    steps = steps if one_step else 1
    for size, terms in groups:
        _, rows, lanes = terms[0].shape
        half, block = size // 2, rows // steps
        kind = "upper" if size == CHIPS else "both" if size > 1 else "down" if lanes == DOWN_BLOCK else "halves"
        operands += terms
        take = (half, 1) if kind == "upper" else (size, 0)
        specs += [pl.BlockSpec((take[0], block, lanes), lambda s, at=take[1]: (at, s, 0))] * len(terms)
        if size > 1:
            kinds = [bf16] if kind == "upper" else [bf16, f32]
            out_specs += [pl.BlockSpec((half, block, lanes), lambda s: (0, s, 0))] * len(kinds)
            shapes += [jax.ShapeDtypeStruct((half, rows, lanes), dtype) for dtype in kinds]
        else:
            ends = [(2 * PAIR_ROWS, D)] if kind == "down" else [(SLAB, lanes)] * 2
            out_specs += [whole(*end) for end in ends]
            shapes += [jax.ShapeDtypeStruct(end, f32) for end in ends]
        jobs.append((len(terms), kind))
    return call(
        lambda *refs: add_up_kernel(jobs, len(passed), refs[0], *refs[1:]),
        [place] + operands + list(passed),
        deps,
        grid=(steps,),
        in_specs=[SMEM] + specs + [ANY] * len(passed),
        out_specs=out_specs + [ANY] * len(passed) + [whole(8, 128)],
        out_shape=shapes
        + [jax.ShapeDtypeStruct(v.shape, v.dtype) for v in passed]
        + [jax.ShapeDtypeStruct((8, 128), f32)],
        input_output_aliases={1 + len(operands) + i: len(shapes) + i for i in range(len(passed))},
        compiler_params=pltpu.CompilerParams(vmem_limit_bytes=vmem),
        cost_estimate=pl.CostEstimate(flops=1000, bytes_accessed=1000, transcendentals=0),
        name="add_up",
    )


def finish_inner_kernel(place, mine, other, out_g, inner_g, small):
    low_core = place[1] == 0
    low = jnp.where(low_core, mine[...], other[...])
    high = jnp.where(low_core, other[...], mine[...])
    out_g[:, :OUT_HALF], out_g[:, OUT_HALF:] = low[:, :OUT_HALF], high[:, :OUT_HALF]
    inner_g[:, :INNER_HALF], inner_g[:, INNER_HALF:] = low[:, OUT_HALF:], high[:, OUT_HALF:]
    small[...] = low[0:8, 0:128]


def finish_proj_kernel(place, mine, other, dq, dk, dv, bias, *vectors):
    low_core = place[1] == 0
    low = jnp.where(low_core, mine[...], other[...])
    high = jnp.where(low_core, other[...], mine[...])
    half = D // 2
    dq[...] = low[:, :D]
    dk[:, :half], dk[:, half:] = low[:, D:QKV_HALF], high[:, :half]
    dv[...] = high[:, half:QKV_HALF]
    bias[...] = high[0, QKV_HALF : QKV_HALF + 4 * SLAB]
    rows = low[:, QKV_HALF:].T
    for i, out in enumerate(vectors):
        out[...] = rows[i, 0:SLAB]


def finish(kernel, place, mine, other, shapes, name, deps=()):
    at = lambda shape: pl.BlockSpec(shape, lambda s: (0,) * len(shape))
    return call(
        kernel,
        (place, mine, other),
        deps,
        grid=(1,),
        in_specs=[SMEM, at(mine.shape), at(mine.shape)],
        out_specs=[at(shape) for shape in shapes],
        out_shape=[jax.ShapeDtypeStruct(shape, f32) for shape in shapes],
        compiler_params=pltpu.CompilerParams(vmem_limit_bytes=LITTLE),
        cost_estimate=pl.CostEstimate(flops=1000, bytes_accessed=1000, transcendentals=0),
        name=name,
    )


def finish_inner(place, mine, other):
    return finish(finish_inner_kernel, place, mine, other, [(SLAB, D), (SLAB, FF), (8, 128)], "finish_inner")


def finish_proj(place, mine, other, deps=()):
    shapes = [(SLAB, D)] * 3 + [(4 * SLAB,)] + [(SLAB,)] * 8
    return finish(finish_proj_kernel, place, mine, other, shapes, "finish_proj", deps)


AXES = ("dp", "fsdp")


CORE = (1, 1)
ALONG_Z_FIRST, ALONG_Z_THEN, ALONG_Z_BOTH, ALONG_XY_FIRST, ALONG_XY_THEN = (16, 8), (8, 16), (24, 24), (2, 4), (4, 2)
FAST_SHAPE = {"dp": 4, "fsdp": 8}


def move(v, masks):
    return lax.ppermute(v, AXES, [(i, i ^ masks[i & 1]) for i in range(SLABS)])


SUM_STEPS = (ALONG_XY_THEN, ALONG_XY_FIRST, ALONG_Z_THEN, ALONG_Z_FIRST)


def after(*values):
    return lax.optimization_barrier(values)


class Sums:
    def __init__(self, keep, got):
        self.size, self.terms, self.step = CHIPS, [keep, got], 0

    def job(self):
        return self.size, self.terms

    def send(self, outs):
        ready = outs.pop(0)
        if self.size < CHIPS:
            self.terms = [outs.pop(0)]
        self.size //= 2
        self.terms = self.terms + [move(ready, SUM_STEPS[self.step])]
        self.step += 1


def add_and_send(place, *groups, **options):
    outs = list(add_up(place, *[g.job() for g in groups], **options))
    for g in groups:
        if g.size > 1:
            g.send(outs)
    return outs


def fast_blocks(shards, core):
    (qw, kw, vw, ow, qb, vb, ob, fg, fs, iw, ib, dw, db, sg, ss) = shards
    vectors = jnp.pad(jnp.stack([qb, vb, ob, fg, fs, db, sg, ss], axis=1), ((0, 0), (0, 120)))
    inner_bias = jnp.pad(ib.reshape(1, 4 * SLAB), ((0, SLAB - 1), (0, 128 - 4 * SLAB)))
    half = D // 2
    halves = [
        jnp.concatenate([qw, kw[:, :half], vectors, ow[:, :half], iw[:, :INNER_HALF]], axis=1),
        jnp.concatenate([kw[:, half:], vw, inner_bias, ow[:, half:], iw[:, INNER_HALF:]], axis=1),
    ]
    low_core = core == 0
    own = jnp.where(low_core, halves[0], halves[1])
    other = move(jnp.where(low_core, halves[1], halves[0]), CORE)
    rows = jnp.concatenate([jnp.where(low_core, own, other), jnp.where(low_core, other, own)], axis=0)
    return rows[:, :PROJ_BLOCK], rows[:, PROJ_BLOCK:], jnp.concatenate([dw[:PAIR_ROWS], dw[PAIR_ROWS:]], axis=1)


def gather_plain(shards):
    (qw, kw, vw, ow, qb, vb, ob, fg, fs, iw, ib, dw, db, sg, ss) = [
        lax.all_gather(v, AXES, axis=0, tiled=True) for v in shards
    ]
    vectors = jnp.pad(jnp.stack([qb, vb, ob, fg, fs, db, sg, ss], axis=1), ((0, 0), (0, 120)))
    inner_bias = jnp.pad(ib.reshape(SLABS, 1, 4 * SLAB), ((0, 0), (0, SLAB - 1), (0, 128 - 4 * SLAB))).reshape(D, 128)
    half = D // 2
    chips = lambda v: v.reshape(CHIPS, PAIR_ROWS, -1)
    down = dw.reshape(CHIPS, 2, 2, PAIR_ROWS, D)
    first = [
        chips(jnp.concatenate([qw, kw[:, :half], vectors, ow[:, :half]], axis=1)),
        chips(jnp.concatenate([kw[:, half:], vw, inner_bias, ow[:, half:]], axis=1)),
    ]
    second = [
        jnp.concatenate([chips(iw[:, c * INNER_HALF : (c + 1) * INNER_HALF]), down[:, c, 0], down[:, c, 1]], axis=2)
        for c in range(2)
    ]
    slots = lambda halves: [v[np.array(SLOT_CHIPS[c])] for c, v in enumerate(halves)]
    return slots(first), slots(second)


def local(fast, inputs, lengths, *rest):
    shards, cotangent = rest[:15], rest[15]
    both = lambda v, came: jnp.concatenate([v, came])
    if fast:
        linear = lax.axis_index(AXES)
        core = linear & 1
        place = jnp.stack([linear >> 1, core]).astype(jnp.int32)
        first, inner, down = fast_blocks(shards, core)
        first = first[None]
        first = both(first, move(first, ALONG_Z_FIRST))
        first, second = after(first, jnp.concatenate([inner, down], axis=1)[None])
        second = jnp.concatenate([second] + [move(second, steps) for steps in (ALONG_Z_FIRST, ALONG_Z_THEN, ALONG_Z_BOTH)])
        first = both(first, move(first, ALONG_Z_THEN))
        first_then, first_core = move(first, ALONG_XY_THEN), move(first, CORE)
        first_came = move(first, ALONG_XY_FIRST)
        first_last, came_core = move(first_came, ALONG_XY_THEN), move(first_came, CORE)
        first_then, first_last, second = after(first_then, first_last, second)
        first = [first, first_came, first_then, first_last]
        first += [first_core, came_core, move(first_then, CORE), move(first_last, CORE)]
        second_came, second_then, second_core = move(second, ALONG_XY_FIRST), move(second, ALONG_XY_THEN), move(second, CORE)
        meta = tuple((at, other) for other in (False, True) for at in range(0, CHIPS, 4))
    else:
        place = jnp.zeros((2,), jnp.int32)
        first, second = gather_plain(shards)
        meta = ((0, False), (0, True))
    qkv, attended, stats, weights, vectors = attend(place, lengths, inputs, first, meta)
    prob = probs(0, lengths, qkv, stats)
    if fast:
        second_came, prob = after(second_came, prob)
        second_last, came_core = move(second_came, ALONG_XY_THEN), move(second_came, CORE)
    prob, normed, rstd, hid, inputs_t, attended_t, hid_t = window(
        1, lengths, inputs, qkv, attended, stats, weights, vectors, prob
    )
    bias_at = PROJ_BLOCK + QKV_HALF
    inner_bias = weights[::SLAB, bias_at : bias_at + 4 * SLAB].reshape(1, FF).astype(f32)
    if fast:
        second_then, second_last, normed, inner_bias = after(second_then, second_last, normed, inner_bias)
        second = [second, second_came, second_then, second_last]
        second += [second_core, came_core, move(second_then, CORE), move(second_last, CORE)]
    output, first_back, back, inner_back, branch, small, db1, down_keep, down_send = feed_forward(
        place, normed, rstd, hid, cotangent, vectors, inner_bias, weights, second, meta
    )
    inner_keep, inner_send = inner_grads(place, hid_t, inner_back, attended_t, branch)
    pairs = lengths.shape[0] * (H // 2)
    third = pairs // 3
    deps = []
    if fast:
        down = Sums(down_keep, move(down_send, CORE))
        inner_send, *deps = add_and_send(place, down, passed=[inner_send], deps=[inner_keep])
        inner = Sums(inner_keep, move(inner_send, CORE))
    grads = attend_back(0, third, qkv, back, prob, deps=deps)
    if fast:
        deps = add_and_send(place, inner, deps=grads[:1])
    grads = attend_back(third, third, qkv, back, prob, grads, deps=deps)
    if fast:
        deps = add_and_send(place, down, deps=grads[:1])
    grads = attend_back(2 * third, pairs - 2 * third, qkv, back, prob, grads, deps=deps)
    if fast:
        deps = add_and_send(place, inner, down, deps=grads[:1])
    proj_keep, proj_send = proj_grads(place, inputs_t, small, db1, grads, deps=deps)
    blocks = inputs.shape[0] // BLOCK
    early = 1
    if fast:
        proj_send, *deps = add_and_send(place, inner, down, passed=[proj_send], deps=[proj_keep])
        proj = Sums(proj_keep, move(proj_send, CORE))
        grad_input, *deps = input_back(0, early, first_back, grads, weights, deps=deps)
        down_grad, *deps = add_and_send(place, proj, down, deps=deps)
        grad_input, *deps = input_back(early, blocks - early, first_back, grads, weights, [grad_input], deps=deps)
        deps = add_and_send(place, proj, inner, deps=deps, vmem=LITTLE)
        mine, other, *deps = add_and_send(place, proj, inner, deps=deps, vmem=LITTLE)
        out_grad, inner_grad, *deps = finish_inner(place, mine, move(other, CORE))
        add_and_send(place, proj, deps=deps, vmem=LITTLE)
        mine, other, _ = add_and_send(place, proj, vmem=LITTLE)
        *square, bias, v0, v1, v2, v3, v4, v5, v6, v7 = finish_proj(place, mine, move(other, CORE))
        vectors = [v0, v1, v2, v3, v4, v5, v6, v7]
    else:
        grad_input, _ = input_back(0, blocks, first_back, grads, weights)
        shard = lambda *v: lax.psum_scatter(jnp.concatenate(v, axis=1), AXES, scatter_dimension=0, tiled=True)
        by_chip = lambda pair: [v[np.argsort(np.array(SLOT_CHIPS[c]))].astype(f32) for c, v in enumerate(pair)]
        low, high = (v.reshape(D, -1) for v in by_chip((inner_keep, inner_send)))
        out_grad, inner_grad = shard(low[:, :OUT_HALF], high[:, :OUT_HALF]), shard(low[:, OUT_HALF:], high[:, OUT_HALF:])
        parts = [jnp.stack([v[:, :, :D], v[:, :, D:]], axis=1) for v in by_chip((down_keep, down_send))]
        down_grad = shard(jnp.stack(parts, axis=1).reshape(FF, D))
        low, high = (v.reshape(D, -1) for v in by_chip((proj_keep, proj_send)))
        half = D // 2
        square = shard(low[:, :D]), shard(low[:, D:QKV_HALF], high[:, :half]), shard(high[:, half:QKV_HALF])
        columns = shard(low[:, QKV_HALF:])
        vectors = [columns[:, i] for i in range(8)]
        bias = shard(high[::SLAB, QKV_HALF : QKV_HALF + 4 * SLAB].reshape(FF, 1))[:, 0]
    return (
        output,
        grad_input,
        *square,
        out_grad,
        *vectors[:5],
        inner_grad,
        bias,
        down_grad,
        *vectors[5:],
    )


def solution(mesh):
    rows, flat = P(AXES, None), P(AXES)
    params = (rows,) * 4 + (flat,) * 5 + (rows, flat, rows, flat, flat, flat)
    return jax.shard_map(
        functools.partial(local, dict(mesh.shape) == FAST_SHAPE),
        mesh=mesh,
        in_specs=(rows, flat) + params + (rows,),
        out_specs=(rows, rows) + params,
        check_vma=False,
    )
```

profile of v0, /device:TPU:0, one launch (start us, length us, event | category | flops | bytes accessed | tf_op | source)
XLA Modules:
  0.0 291.8 jit_solution(6548517274880568552)
XLA Ops:
  7.8 4.0 %collective-permute-start.1 = (bf16[1,48,1664]{2,1,0:T(8,128)(2,1)S(1)}, bf16[1,48,1664]{2,1,0:T(8,128)(2,1)S(1)}, u32[]{:S(2)}, u32[]{:S(2)}) collective-permute-start(bf16[1,48,1664]{2,1,0:T(8,128)(2,1)S(1)} %fusion.4), channel_id=1, source_target_pairs={{0,16},{1,9},{2,18},{3,11},{4,20},{5,13},{6,22},{7,15},{8,24},{9,1... | collective-permute-start | bytes 479240 | tf_op jit(solution)/shard_map/ppermute | solution.py:829
  11.9 3.7 %collective-permute-done.1 = bf16[1,48,1664]{2,1,0:T(8,128)(2,1)S(1)} collective-permute-done((bf16[1,48,1664]{2,1,0:T(8,128)(2,1)S(1)}, bf16[1,48,1664]{2,1,0:T(8,128)(2,1)S(1)}, u32[]{:S(2)}, u32[]{:S(2)}) %collective-permute-start.1) | collective-permute-done | bytes 159776 | tf_op jit(solution)/shard_map/ppermute | solution.py:829
  15.6 2.5 collective-permute-start.2
  18.1 8.3 %collective-permute-done.2 = bf16[2,48,1664]{2,1,0:T(8,128)(2,1)S(1)} collective-permute-done((bf16[2,48,1664]{2,1,0:T(8,128)(2,1)S(1)}, bf16[2,48,1664]{2,1,0:T(8,128)(2,1)S(1)}, u32[]{:S(2)}, u32[]{:S(2)}) %collective-permute-start.2) | collective-permute-done | bytes 319520 | tf_op jit(solution)/shard_map/ppermute | solution.py:829
  28.2 2.9 collective-permute-start.8
  34.1 7.3 %collective-permute-done.4.refs_1_ = bf16[4,48,1664]{2,1,0:T(8,128)(2,1)S(1)} collective-permute-done((bf16[4,48,1664]{2,1,0:T(8,128)(2,1)S(1)}, bf16[4,48,1664]{2,1,0:T(8,128)(2,1)S(1)}, u32[]{:S(2)}, u32[]{:S(2)}) %collective-permute-start.4) | collective-permute-done | bytes 639008 | tf_op jit(solution)/shard_map/ppermute | solution.py:829
  41.4 2.9 %collective-permute-start.5 = (bf16[4,48,1664]{2,1,0:T(8,128)(2,1)S(1)}, bf16[4,48,1664]{2,1,0:T(8,128)(2,1)}, u32[]{:S(2)}, u32[]{:S(2)}) collective-permute-start(bf16[4,48,1664]{2,1,0:T(8,128)(2,1)S(1)} %collective-permute-done.4.refs_1_), channel_id=1, source_target_pairs={{0,4},{1,3},{2,6},{3,1},{4,0},{5,7},{6,2},{7,5},{8,12},{9,11},{10,... | collective-permute-start | bytes 1916936 | tf_op jit(solution)/shard_map/ppermute | solution.py:829
  45.0 8.7 %collective-permute-done.6 = bf16[1,48,3072]{2,1,0:T(8,128)(2,1)S(1)} collective-permute-done((bf16[1,48,3072]{2,1,0:T(8,128)(2,1)S(1)}, bf16[1,48,3072]{2,1,0:T(8,128)(2,1)S(1)}, u32[]{:S(2)}, u32[]{:S(2)}) %collective-permute-start.6) | collective-permute-done | bytes 294944 | tf_op jit(solution)/shard_map/ppermute | solution.py:829
  58.9 17.4 %attend.1 = (bf16[1024,2304]{1,0:T(8,128)(2,1)}, bf16[1024,768]{1,0:T(8,128)(2,1)}, f32[2,16,512]{2,1,0:T(8,128)}, bf16[768,3328]{1,0:T(8,128)(2,1)}, f32[16,768]{1,0:T(8,128)}) custom-call(s32[2]{0:T(128)} %pad_add_fusion.place.refs_0_, s32[2]{0:T(128)} %refs_0_.3, f32[1024,768]{1,0:T(8,128)} %refs_5_.1, bf16[4,48,1664]{2,1,0:T(8,128)(2,1)} %copy-done.6, ...), custom_call_target="tpu_custom_call" | custom-call | flops 17999998976 | bytes 20971520 | tf_op jit(solution)/shard_map/attend/pallas_call | solution.py:202
  77.9 6.9 %probs.1.refs_4_ = bf16[24,512,512]{2,1,0:T(8,128)(2,1)} custom-call(s32[2]{0:T(128)} %refs_0_.3, bf16[1024,2304]{1,0:T(8,128)(2,1)} %get-tuple-element.121.refs_1_.refs_2_.refs_0_, bf16[1024,2304]{1,0:T(8,128)(2,1)} %get-tuple-element.121.refs_1_.refs_2_.refs_0_, f32[2,16,512]{2,1,0:T(8,128)} %get-tuple-element.122.refs_3_), custom_call_target="tpu_custom_call" | custom-call | flops 8000000000 | bytes 1048576 | tf_op jit(solution)/shard_map/probs/pallas_call | solution.py:67
  86.0 13.1 %window.1 = (bf16[24,512,512]{2,1,0:T(8,128)(2,1)}, f32[1024,768]{1,0:T(8,128)}, f32[1024,128]{1,0:T(8,128)}, bf16[1024,768]{1,0:T(8,128)(2,1)}, bf16[768,1024]{...) custom-call(s32[2]{0:T(128)} %refs_0_.3, ...), custom_call_target="tpu_custom_call", output_to_operand_aliasing={{0}: (4, {})} | custom-call | flops 14000000000 | bytes 1048576 | tf_op jit(solution)/shard_map/window/pallas_call | solution.py:67
  99.2 2.6 collective-permute-done.15.refs_3_
  102.3 2.7 collective-permute-done.18.refs_6_
  106.7 49.0 %feed_forward.1 = (f32[1024,768]{1,0:T(8,128)}, f32[1024,768]{1,0:T(8,128)}, bf16[1024,768]{1,0:T(8,128)(2,1)}, bf16[1024,3072]{1,0:T(8,128)(2,1)}, bf16[1024,76...) custom-call(s32[2]{0:T(128)} %pad_add_fusion.place.refs_0_, ...), custom_call_target="tpu_custom_call" | custom-call | flops 51999997952 | bytes 41943040 | tf_op jit(solution)/shard_map/feed_forward/pallas_call | solution.py:448
  155.9 11.0 %inner_grads.1 = (bf16[16,48,1920]{2,1,0:T(8,128)(2,1)}, bf16[16,48,1920]{2,1,0:T(8,128)(2,1)}) custom-call(bf16[768,1024]{1,0:T(8,128)(2,1)} %get-tuple-element.141.hid_t, bf16[1024,3072]{1,0:T(8,128)(2,1)} %get-tuple-element.142.ib_ref, s32[2]{0:T(128)} %pad_add_fusion.place.refs_0_, bf16[768,1024]{1,0:T(8,128)(2,1)} %get-tuple-element.143.att_in, ...), custom_call_target="tpu_custom_call" | custom-call | flops 4000000000 | bytes 1048576 | tf_op jit(solution)/shard_map/inner_grads/pallas_call | solution.py:518
  166.9 3.6 %add_up.10 = (bf16[8,48,1536]{2,1,0:T(8,128)(2,1)}, bf16[16,48,1920]{2,1,0:T(8,128)(2,1)}, f32[8,128]{1,0:T(8,128)}) custom-call(s32[2]{0:T(128)} %pad_add_fusion.place.refs_0_, bf16[16,48,1536]{2,1,0:T(8,128)(2,1)} %get-tuple-element.139.refs_1_, bf16[16,48,1536]{2,1,0:T(8,128)(2,1)} %collective-permute-done.20.refs_2_, ...), custom_call_target="tpu_custom_call", output_to_operand_aliasing={{1}: (3, {})} | custom-call | flops 1000 | bytes 1000 | tf_op jit(solution)/shard_map/add_up/pallas_call | solution.py:67
  171.6 8.5 %attend_back_0.1 = (bf16[1024,768]{1,0:T(8,128)(2,1)}, bf16[1024,768]{1,0:T(8,128)(2,1)}, bf16[1024,768]{1,0:T(8,128)(2,1)}) custom-call(bf16[1024,2304]{1,0:T(8,128)(2,1)} %get-tuple-element.121.refs_1_.refs_2_.refs_0_, bf16[1024,2304]{1,0:T(8,128)(2,1)} %get-tuple-element.121.refs_1_.refs_2_.refs_0_, ...), custom_call_target="tpu_custom_call" | custom-call | flops 3000000000 | bytes 1048576 | tf_op jit(solution)/shard_map/attend_back_0/pallas_call | solution.py:67
  180.1 3.9 %add_up.11 = (bf16[8,48,1920]{2,1,0:T(8,128)(2,1)}, f32[8,128]{1,0:T(8,128)}) custom-call(s32[2]{0:T(128)} %pad_add_fusion.place.refs_0_, bf16[16,48,1920]{2,1,0:T(8,128)(2,1)} %get-tuple-element.146.refs_4_.refs_1_, bf16[16,48,1920]{2,1,0:T(8,128)(2,1)} %collective-permute-done.21.refs_2_, bf16[1024,768]{1,0:T(8,128)(2,1)} %get-tuple-element.148.refs_3_.refs_5_), custom_call_target="tpu_custom_call" | custom-call | flops 1000 | bytes 1000 | tf_op jit(solution)/shard_map/add_up/pallas_call | solution.py:67
  185.3 8.4 %attend_back_4.1 = (bf16[1024,768]{1,0:T(8,128)(2,1)}, bf16[1024,768]{1,0:T(8,128)(2,1)}, bf16[1024,768]{1,0:T(8,128)(2,1)}) custom-call(bf16[1024,2304]{1,0:T(8,128)(2,1)} %get-tuple-element.121.refs_1_.refs_2_.refs_0_, bf16[1024,2304]{1,0:T(8,128)(2,1)} %get-tuple-element.121.refs_1_.refs_2_.refs_0_, ...), custom_call_target="tpu_custom_call", output_to_operand_aliasing={{0}: (5, {}), {1}: (6, {}), {2}: (7, {})} | custom-call | flops 3000000000 | bytes 1048576 | tf_op jit(solution)/shard_map/attend_back_4/pallas_call | solution.py:67
  193.7 3.6 %add_up.12 = (bf16[4,48,1536]{2,1,0:T(8,128)(2,1)}, f32[4,48,1536]{2,1,0:T(8,128)}, f32[8,128]{1,0:T(8,128)}) custom-call(s32[2]{0:T(128)} %pad_add_fusion.place.refs_0_, bf16[16,48,1536]{2,1,0:T(8,128)(2,1)} %get-tuple-element.139.refs_1_, bf16[16,48,1536]{2,1,0:T(8,128)(2,1)} %collective-permute-done.20.refs_2_, ...), custom_call_target="tpu_custom_call" | custom-call | flops 1000 | bytes 1000 | tf_op jit(solution)/shard_map/add_up/pallas_call | solution.py:67
  198.5 8.4 %attend_back_8.1 = (bf16[1024,768]{1,0:T(8,128)(2,1)}, bf16[1024,768]{1,0:T(8,128)(2,1)}, bf16[1024,768]{1,0:T(8,128)(2,1)}) custom-call(bf16[1024,2304]{1,0:T(8,128)(2,1)} %get-tuple-element.121.refs_1_.refs_2_.refs_0_, bf16[1024,2304]{1,0:T(8,128)(2,1)} %get-tuple-element.121.refs_1_.refs_2_.refs_0_, ...), custom_call_target="tpu_custom_call", output_to_operand_aliasing={{0}: (5, {}), {1}: (6, {}), {2}: (7, {})} | custom-call | flops 3000000000 | bytes 1048576 | tf_op jit(solution)/shard_map/attend_back_8/pallas_call | solution.py:67
  209.4 5.0 %add_up.13 = (bf16[4,48,1920]{2,1,0:T(8,128)(2,1)}, f32[4,48,1920]{2,1,0:T(8,128)}, bf16[2,48,1536]{2,1,0:T(8,128)(2,1)}, f32[2,48,1536]{2,1,0:T(8,128)}, f32[8,128]{1,0:T(8,128)}) custom-call(s32[2]{0:T(128)} %pad_add_fusion.place.refs_0_, bf16[16,48,1920]{2,1,0:T(8,128)(2,1)} %get-tuple-element.146.refs_4_.refs_1_, ...), custom_call_target="tpu_custom_call" | custom-call | flops 1000 | bytes 1000 | tf_op jit(solution)/shard_map/add_up/pallas_call | solution.py:67
  215.2 10.3 %proj_grads.1 = (bf16[16,48,1280]{2,1,0:T(8,128)(2,1)}, bf16[16,48,1280]{2,1,0:T(8,128)(2,1)}) custom-call(s32[2]{0:T(128)} %pad_add_fusion.place.refs_0_, bf16[768,1024]{1,0:T(8,128)(2,1)} %get-tuple-element.168.refs_1_, f32[6,8,768]{2,1,0:T(8,128)} %get-tuple-element.169.refs_2_, f32[8,3072]{1,0:T(8,128)} %get-tuple-element.170.refs_3_, ...), custom_call_target="tpu_custom_call" | custom-call | flops 4000000000 | bytes 1048576 | tf_op jit(solution)/shard_map/proj_grads/pallas_call | solution.py:67
  226.3 3.1 %add_up.14 = (bf16[2,48,1920]{2,1,0:T(8,128)(2,1)}, f32[2,48,1920]{2,1,0:T(8,128)}, bf16[1,48,1536]{2,1,0:T(8,128)(2,1)}, f32[1,48,1536]{2,1,0:T(8,128)}, bf16[1...) custom-call(s32[2]{0:T(128)} %pad_add_fusion.place.refs_0_, ...), custom_call_target="tpu_custom_call", output_to_operand_aliasing={{4}: (5, {})} | custom-call | flops 1000 | bytes 1000 | tf_op jit(solution)/shard_map/add_up/pallas_call | solution.py:67
  230.0 2.6 collective-permute-start.28
  232.7 5.2 %input_back_0.1 = (f32[1024,768]{1,0:T(8,128)}, f32[8,128]{1,0:T(8,128)}) custom-call(f32[1024,768]{1,0:T(8,128)} %get-tuple-element.136.refs_0_, bf16[1024,768]{1,0:T(8,128)(2,1)} %get-tuple-element.158.refs_6_.refs_4_.refs_1_, bf16[1024,768]{1,0:T(8,128)(2,1)} %get-tuple-element.159.refs_5_.refs_2_, bf16[1024,768]{1,0:T(8,128)(2,1)} %get-tuple-element.160.refs_6_.refs_3_, ...), custom_call_target="tpu_custom_call" | custom-call | flops 10000000000 | bytes 1048576 | tf_op jit(solution)/shard_map/input_back_0/pallas_call | solution.py:67
  238.5 2.9 add_up.15
  243.5 8.3 %input_back_1.1 = (f32[1024,768]{1,0:T(8,128)}, f32[8,128]{1,0:T(8,128)}) custom-call(f32[1024,768]{1,0:T(8,128)} %get-tuple-element.136.refs_0_, bf16[1024,768]{1,0:T(8,128)(2,1)} %get-tuple-element.158.refs_6_.refs_4_.refs_1_, bf16[1024,768]{1,0:T(8,128)(2,1)} %get-tuple-element.159.refs_5_.refs_2_, ...), custom_call_target="tpu_custom_call", output_to_operand_aliasing={{0}: (5, {})} | custom-call | flops 10000000000 | bytes 1048576 | tf_op jit(solution)/shard_map/input_back_1/pallas_call | solution.py:67
  252.5 3.3 %collective-permute-done.29.refs_3_ = bf16[8,48,1280]{2,1,0:T(8,128)(2,1)} collective-permute-done((bf16[8,48,1280]{2,1,0:T(8,128)(2,1)}, bf16[8,48,1280]{2,1,0:T(8,128)(2,1)}, u32[]{:S(2)}, u32[]{:S(2)}) %collective-permute-start.29) | collective-permute-done | bytes 983072 | tf_op jit(solution)/shard_map/ppermute | solution.py:829
  264.4 6.4 %collective-permute-done.32.refs_4_ = bf16[1,48,1920]{2,1,0:T(8,128)(2,1)S(1)} collective-permute-done((bf16[1,48,1920]{2,1,0:T(8,128)(2,1)S(1)}, bf16[1,48,1920]{2,1,0:T(8,128)(2,1)S(1)}, u32[]{:S(2)}, u32[]{:S(2)}) %collective-permute-start.32) | collective-permute-done | bytes 184352 | tf_op jit(solution)/shard_map/ppermute | solution.py:829
  275.2 5.5 %collective-permute-done.33.refs_2_ = bf16[2,48,1280]{2,1,0:T(8,128)(2,1)S(1)} collective-permute-done((bf16[2,48,1280]{2,1,0:T(8,128)(2,1)S(1)}, bf16[2,48,1280]{2,1,0:T(8,128)(2,1)S(1)}, u32[]{:S(2)}, u32[]{:S(2)}) %collective-permute-start.33) | collective-permute-done | bytes 245792 | tf_op jit(solution)/shard_map/ppermute | solution.py:829
  281.9 6.1 %collective-permute-done.35.refs_2_ = bf16[1,48,1280]{2,1,0:T(8,128)(2,1)S(1)} collective-permute-done((bf16[1,48,1280]{2,1,0:T(8,128)(2,1)S(1)}, bf16[1,48,1280]{2,1,0:T(8,128)(2,1)S(1)}, u32[]{:S(2)}, u32[]{:S(2)}) %collective-permute-start.35) | collective-permute-done | bytes 122912 | tf_op jit(solution)/shard_map/ppermute | solution.py:829
  (105 shorter events, 52.6 us)
Async XLA Ops:
  7.8 7.8 %collective-permute-start.1 = (bf16[1,48,1664]{2,1,0:T(8,128)(2,1)S(1)}, bf16[1,48,1664]{2,1,0:T(8,128)(2,1)S(1)}, u32[]{:S(2)}, u32[]{:S(2)}) collective-permute-start(bf16[1,48,1664]{2,1,0:T(8,128)(2,1)S(1)} %fusion.4), channel_id=1, source_target_pairs={{0,16},{1,9},{2,18},{3,11},{4,20},{5,13},{6,22},{7,15},{8,24},{9,1... | collective-permute-start | bytes 479240 | tf_op jit(solution)/shard_map/ppermute | solution.py:829
  15.6 10.8 %collective-permute-start.2 = (bf16[2,48,1664]{2,1,0:T(8,128)(2,1)S(1)}, bf16[2,48,1664]{2,1,0:T(8,128)(2,1)S(1)}, u32[]{:S(2)}, u32[]{:S(2)}) collective-permute-start(bf16[2,48,1664]{2,1,0:T(8,128)(2,1)S(1)} %pad_maximum_fusion.1), channel_id=1, source_target_pairs={{0,8},{1,17},{2,10},{3,19},{4,12},{5,21},{6,14},{7,23},{8,0},{9,25... | collective-permute-start | bytes 958472 | tf_op jit(solution)/shard_map/ppermute | solution.py:829
  26.4 14.9 %collective-permute-start.4 = (bf16[4,48,1664]{2,1,0:T(8,128)(2,1)S(1)}, bf16[4,48,1664]{2,1,0:T(8,128)(2,1)S(1)}, u32[]{:S(2)}, u32[]{:S(2)}) collective-permute-start(bf16[4,48,1664]{2,1,0:T(8,128)(2,1)S(1)} %constant_dynamic-update-slice_fusion.8.refs_0_), channel_id=1, source_target_pairs={{0,2},{1,5},{2,0},{3,7},{4,6},{5,1},{6,4},{7,3},{8,10},{9,13},{10,... | collective-permute-start | bytes 1916936 | tf_op jit(solution)/shard_map/ppermute | solution.py:829
  28.2 16.1 %collective-permute-start.8 = (bf16[1,48,3072]{2,1,0:T(8,128)(2,1)S(1)}, bf16[1,48,3072]{2,1,0:T(8,128)(2,1)S(1)}, u32[]{:S(2)}, u32[]{:S(2)}) collective-permute-start(bf16[1,48,3072]{2,1,0:T(8,128)(2,1)S(1)} %fusion.2), channel_id=1, source_target_pairs={{0,24},{1,25},{2,26},{3,27},{4,28},{5,29},{6,30},{7,31},{8,16},{9,... | collective-permute-start | bytes 884744 | tf_op jit(solution)/shard_map/ppermute | solution.py:829
  31.1 13.9 %collective-permute-start.7 = (bf16[1,48,3072]{2,1,0:T(8,128)(2,1)S(1)}, bf16[1,48,3072]{2,1,0:T(8,128)(2,1)S(1)}, u32[]{:S(2)}, u32[]{:S(2)}) collective-permute-start(bf16[1,48,3072]{2,1,0:T(8,128)(2,1)S(1)} %fusion.2), channel_id=1, source_target_pairs={{0,8},{1,17},{2,10},{3,19},{4,12},{5,21},{6,14},{7,23},{8,0},{9,25... | collective-permute-start | bytes 884744 | tf_op jit(solution)/shard_map/ppermute | solution.py:829
  31.1 22.6 %collective-permute-start.6 = (bf16[1,48,3072]{2,1,0:T(8,128)(2,1)S(1)}, bf16[1,48,3072]{2,1,0:T(8,128)(2,1)S(1)}, u32[]{:S(2)}, u32[]{:S(2)}) collective-permute-start(bf16[1,48,3072]{2,1,0:T(8,128)(2,1)S(1)} %fusion.2), channel_id=1, source_target_pairs={{0,16},{1,9},{2,18},{3,11},{4,20},{5,13},{6,22},{7,15},{8,24},{9,1... | collective-permute-start | bytes 884744 | tf_op jit(solution)/shard_map/ppermute | solution.py:829
  32.6 21.9 %collective-permute-start.3 = (bf16[4,48,1664]{2,1,0:T(8,128)(2,1)S(1)}, bf16[4,48,1664]{2,1,0:T(8,128)(2,1)S(1)}, u32[]{:S(2)}, u32[]{:S(2)}) collective-permute-start(bf16[4,48,1664]{2,1,0:T(8,128)(2,1)S(1)} %constant_dynamic-update-slice_fusion.8.refs_0_), channel_id=1, source_target_pairs={{0,4},{1,3},{2,6},{3,1},{4,0},{5,7},{6,2},{7,5},{8,12},{9,11},{10,... | collective-permute-start | bytes 1916936 | tf_op jit(solution)/shard_map/ppermute | solution.py:829
  41.4 13.1 %collective-permute-start.5 = (bf16[4,48,1664]{2,1,0:T(8,128)(2,1)S(1)}, bf16[4,48,1664]{2,1,0:T(8,128)(2,1)}, u32[]{:S(2)}, u32[]{:S(2)}) collective-permute-start(bf16[4,48,1664]{2,1,0:T(8,128)(2,1)S(1)} %collective-permute-done.4.refs_1_), channel_id=1, source_target_pairs={{0,4},{1,3},{2,6},{3,1},{4,0},{5,7},{6,2},{7,5},{8,12},{9,11},{10,... | collective-permute-start | bytes 1916936 | tf_op jit(solution)/shard_map/ppermute | solution.py:829
  53.9 4.0 %collective-permute-start.12 = (bf16[4,48,1664]{2,1,0:T(8,128)(2,1)S(1)}, bf16[4,48,1664]{2,1,0:T(8,128)(2,1)}, u32[]{:S(2)}, u32[]{:S(2)}) collective-permute-start(bf16[4,48,1664]{2,1,0:T(8,128)(2,1)S(1)} %collective-permute-done.4.refs_1_), channel_id=1, source_target_pairs={{0,1},{1,0},{2,3},{3,2},{4,5},{5,4},{6,7},{7,6},{8,9},{9,8},{10,11... | collective-permute-start | bytes 1916936 | tf_op jit(solution)/shard_map/ppermute | solution.py:829
  54.4 4.4 %collective-permute-start.13 = (bf16[4,48,1664]{2,1,0:T(8,128)(2,1)S(1)}, bf16[4,48,1664]{2,1,0:T(8,128)(2,1)}, u32[]{:S(2)}, u32[]{:S(2)}) collective-permute-start(bf16[4,48,1664]{2,1,0:T(8,128)(2,1)S(1)} %collective-permute-done.3.refs_2_), channel_id=1, source_target_pairs={{0,1},{1,0},{2,3},{3,2},{4,5},{5,4},{6,7},{7,6},{8,9},{9,8},{10,11... | collective-permute-start | bytes 1916936 | tf_op jit(solution)/shard_map/ppermute | solution.py:829
  54.6 4.3 %collective-permute-start.14 = (bf16[4,48,1664]{2,1,0:T(8,128)(2,1)}, bf16[4,48,1664]{2,1,0:T(8,128)(2,1)}, u32[]{:S(2)}, u32[]{:S(2)}) collective-permute-start(bf16[4,48,1664]{2,1,0:T(8,128)(2,1)} %collective-permute-done.5.refs_3_), channel_id=1, source_target_pairs={{0,1},{1,0},{2,3},{3,2},{4,5},{5,4},{6,7},{7,6},{8,9},{9,8},{10,11... | collective-permute-start | bytes 1916936 | tf_op jit(solution)/shard_map/ppermute | solution.py:829
  55.6 46.7 %collective-permute-start.16 = (bf16[4,48,3072]{2,1,0:T(8,128)(2,1)S(1)}, bf16[4,48,3072]{2,1,0:T(8,128)(2,1)}, u32[]{:S(2)}, u32[]{:S(2)}) collective-permute-start(bf16[4,48,3072]{2,1,0:T(8,128)(2,1)S(1)} %pad_maximum_fusion.refs_0_), channel_id=1, source_target_pairs={{0,1},{1,0},{2,3},{3,2},{4,5},{5,4},{6,7},{7,6},{8,9},{9,8},{10,11... | collective-permute-start | bytes 3538952 | tf_op jit(solution)/shard_map/ppermute | solution.py:829
  56.1 28.7 %collective-permute-start.10 = (bf16[4,48,3072]{2,1,0:T(8,128)(2,1)S(1)}, bf16[4,48,3072]{2,1,0:T(8,128)(2,1)}, u32[]{:S(2)}, u32[]{:S(2)}) collective-permute-start(bf16[4,48,3072]{2,1,0:T(8,128)(2,1)S(1)} %pad_maximum_fusion.refs_0_), channel_id=1, source_target_pairs={{0,2},{1,5},{2,0},{3,7},{4,6},{5,1},{6,4},{7,3},{8,10},{9,13},{10,... | collective-permute-start | bytes 3538952 | tf_op jit(solution)/shard_map/ppermute | solution.py:829
  57.9 41.2 %collective-permute-start.9 = (bf16[4,48,3072]{2,1,0:T(8,128)(2,1)S(1)}, bf16[4,48,3072]{2,1,0:T(8,128)(2,1)}, u32[]{:S(2)}, u32[]{:S(2)}) collective-permute-start(bf16[4,48,3072]{2,1,0:T(8,128)(2,1)S(1)} %pad_maximum_fusion.refs_0_), channel_id=1, source_target_pairs={{0,4},{1,3},{2,6},{3,1},{4,0},{5,7},{6,2},{7,5},{8,12},{9,11},{10,... | collective-permute-start | bytes 3538952 | tf_op jit(solution)/shard_map/ppermute | solution.py:829
  84.8 17.5 %collective-permute-start.17 = (bf16[4,48,3072]{2,1,0:T(8,128)(2,1)}, bf16[4,48,3072]{2,1,0:T(8,128)(2,1)}, u32[]{:S(2)}, u32[]{:S(2)}) collective-permute-start(bf16[4,48,3072]{2,1,0:T(8,128)(2,1)} %collective-permute-done.10.refs_1_), channel_id=1, source_target_pairs={{0,1},{1,0},{2,3},{3,2},{4,5},{5,4},{6,7},{7,6},{8,9},{9,8},{10,11... | collective-permute-start | bytes 3538952 | tf_op jit(solution)/shard_map/ppermute | solution.py:829
  85.3 16.5 %collective-permute-start.15 = (bf16[4,48,3072]{2,1,0:T(8,128)(2,1)}, bf16[4,48,3072]{2,1,0:T(8,128)(2,1)}, u32[]{:S(2)}, u32[]{:S(2)}) collective-permute-start(bf16[4,48,3072]{2,1,0:T(8,128)(2,1)} %collective-permute-done.10.refs_1_), channel_id=1, source_target_pairs={{0,4},{1,3},{2,6},{3,1},{4,0},{5,7},{6,2},{7,5},{8,12},{9,11},{10,... | collective-permute-start | bytes 3538952 | tf_op jit(solution)/shard_map/ppermute | solution.py:829
  101.8 4.9 %collective-permute-start.19 = (bf16[4,48,3072]{2,1,0:T(8,128)(2,1)}, bf16[4,48,3072]{2,1,0:T(8,128)(2,1)}, u32[]{:S(2)}, u32[]{:S(2)}) collective-permute-start(bf16[4,48,3072]{2,1,0:T(8,128)(2,1)} %collective-permute-done.15.refs_3_), channel_id=1, source_target_pairs={{0,1},{1,0},{2,3},{3,2},{4,5},{5,4},{6,7},{7,6},{8,9},{9,8},{10,11... | collective-permute-start | bytes 3538952 | tf_op jit(solution)/shard_map/ppermute | solution.py:829
  155.7 11.2 %collective-permute-start.20 = (bf16[16,48,1536]{2,1,0:T(8,128)(2,1)}, bf16[16,48,1536]{2,1,0:T(8,128)(2,1)}, u32[]{:S(2)}, u32[]{:S(2)}) collective-permute-start(bf16[16,48,1536]{2,1,0:T(8,128)(2,1)} %get-tuple-element.140), channel_id=1, source_target_pairs={{0,1},{1,0},{2,3},{3,2},{4,5},{5,4},{6,7},{7,6},{8,9},{9,8},{10,11... | collective-permute-start | bytes 7077896 | tf_op jit(solution)/shard_map/ppermute | solution.py:829
  170.5 9.6 %collective-permute-start.21 = (bf16[16,48,1920]{2,1,0:T(8,128)(2,1)}, bf16[16,48,1920]{2,1,0:T(8,128)(2,1)}, u32[]{:S(2)}, u32[]{:S(2)}) collective-permute-start(bf16[16,48,1920]{2,1,0:T(8,128)(2,1)} %get-tuple-element.151), channel_id=1, source_target_pairs={{0,1},{1,0},{2,3},{3,2},{4,5},{5,4},{6,7},{7,6},{8,9},{9,8},{10,11... | collective-permute-start | bytes 8847368 | tf_op jit(solution)/shard_map/ppermute | solution.py:829
  170.9 22.8 %collective-permute-start.22 = (bf16[8,48,1536]{2,1,0:T(8,128)(2,1)}, bf16[8,48,1536]{2,1,0:T(8,128)(2,1)}, u32[]{:S(2)}, u32[]{:S(2)}) collective-permute-start(bf16[8,48,1536]{2,1,0:T(8,128)(2,1)} %get-tuple-element.156), channel_id=1, source_target_pairs={{0,4},{1,3},{2,6},{3,1},{4,0},{5,7},{6,2},{7,5},{8,12},{9,11},{10,... | collective-permute-start | bytes 3538952 | tf_op jit(solution)/shard_map/ppermute | solution.py:829
  184.0 25.4 %collective-permute-start.23 = (bf16[8,48,1920]{2,1,0:T(8,128)(2,1)}, bf16[8,48,1920]{2,1,0:T(8,128)(2,1)}, u32[]{:S(2)}, u32[]{:S(2)}) collective-permute-start(bf16[8,48,1920]{2,1,0:T(8,128)(2,1)} %get-tuple-element.161), channel_id=1, source_target_pairs={{0,4},{1,3},{2,6},{3,1},{4,0},{5,7},{6,2},{7,5},{8,12},{9,11},{10,... | collective-permute-start | bytes 4423688 | tf_op jit(solution)/shard_map/ppermute | solution.py:829
  197.3 12.1 %collective-permute-start.24 = (bf16[4,48,1536]{2,1,0:T(8,128)(2,1)}, bf16[4,48,1536]{2,1,0:T(8,128)(2,1)}, u32[]{:S(2)}, u32[]{:S(2)}) collective-permute-start(bf16[4,48,1536]{2,1,0:T(8,128)(2,1)} %get-tuple-element.163), channel_id=1, source_target_pairs={{0,2},{1,5},{2,0},{3,7},{4,6},{5,1},{6,4},{7,3},{8,10},{9,13},{10,... | collective-permute-start | bytes 1769480 | tf_op jit(solution)/shard_map/ppermute | solution.py:829
  214.4 11.8 %collective-permute-start.25 = (bf16[4,48,1920]{2,1,0:T(8,128)(2,1)}, bf16[4,48,1920]{2,1,0:T(8,128)(2,1)}, u32[]{:S(2)}, u32[]{:S(2)}) collective-permute-start(bf16[4,48,1920]{2,1,0:T(8,128)(2,1)} %get-tuple-element.165), channel_id=1, source_target_pairs={{0,2},{1,5},{2,0},{3,7},{4,6},{5,1},{6,4},{7,3},{8,10},{9,13},{10,... | collective-permute-start | bytes 2211848 | tf_op jit(solution)/shard_map/ppermute | solution.py:829
  215.2 10.4 %collective-permute-start.26 = (bf16[2,48,1536]{2,1,0:T(8,128)(2,1)}, bf16[2,48,1536]{2,1,0:T(8,128)(2,1)S(1)}, u32[]{:S(2)}, u32[]{:S(2)}) collective-permute-start(bf16[2,48,1536]{2,1,0:T(8,128)(2,1)} %get-tuple-element.167), channel_id=1, source_target_pairs={{0,8},{1,17},{2,10},{3,19},{4,12},{5,21},{6,14},{7,23},{8,0},{9,25... | collective-permute-start | bytes 884744 | tf_op jit(solution)/shard_map/ppermute | solution.py:829
  229.4 8.5 %collective-permute-start.27 = (bf16[16,48,1280]{2,1,0:T(8,128)(2,1)}, bf16[16,48,1280]{2,1,0:T(8,128)(2,1)}, u32[]{:S(2)}, u32[]{:S(2)}) collective-permute-start(bf16[16,48,1280]{2,1,0:T(8,128)(2,1)} %get-tuple-element.176), channel_id=1, source_target_pairs={{0,1},{1,0},{2,3},{3,2},{4,5},{5,4},{6,7},{7,6},{8,9},{9,8},{10,11... | collective-permute-start | bytes 5898248 | tf_op jit(solution)/shard_map/ppermute | solution.py:829
  230.0 7.8 %collective-permute-start.28 = (bf16[1,48,1536]{2,1,0:T(8,128)(2,1)}, bf16[1,48,1536]{2,1,0:T(8,128)(2,1)S(1)}, u32[]{:S(2)}, u32[]{:S(2)}) collective-permute-start(bf16[1,48,1536]{2,1,0:T(8,128)(2,1)} %get-tuple-element.178), channel_id=1, source_target_pairs={{0,16},{1,9},{2,18},{3,11},{4,20},{5,13},{6,22},{7,15},{8,24},{9,1... | collective-permute-start | bytes 442376 | tf_op jit(solution)/shard_map/ppermute | solution.py:829
  241.4 14.4 %collective-permute-start.29 = (bf16[8,48,1280]{2,1,0:T(8,128)(2,1)}, bf16[8,48,1280]{2,1,0:T(8,128)(2,1)}, u32[]{:S(2)}, u32[]{:S(2)}) collective-permute-start(bf16[8,48,1280]{2,1,0:T(8,128)(2,1)} %get-tuple-element.182), channel_id=1, source_target_pairs={{0,4},{1,3},{2,6},{3,1},{4,0},{5,7},{6,2},{7,5},{8,12},{9,11},{10,... | collective-permute-start | bytes 2949128 | tf_op jit(solution)/shard_map/ppermute | solution.py:829
  242.2 10.4 %collective-permute-start.30 = (bf16[2,48,1920]{2,1,0:T(8,128)(2,1)}, bf16[2,48,1920]{2,1,0:T(8,128)(2,1)S(1)}, u32[]{:S(2)}, u32[]{:S(2)}) collective-permute-start(bf16[2,48,1920]{2,1,0:T(8,128)(2,1)} %get-tuple-element.184), channel_id=1, source_target_pairs={{0,8},{1,17},{2,10},{3,19},{4,12},{5,21},{6,14},{7,23},{8,0},{9,25... | collective-permute-start | bytes 1105928 | tf_op jit(solution)/shard_map/ppermute | solution.py:829
  261.1 9.7 %collective-permute-start.31 = (bf16[4,48,1280]{2,1,0:T(8,128)(2,1)S(1)}, bf16[4,48,1280]{2,1,0:T(8,128)(2,1)S(1)}, u32[]{:S(2)}, u32[]{:S(2)}) collective-permute-start(bf16[4,48,1280]{2,1,0:T(8,128)(2,1)S(1)} %get-tuple-element.187), channel_id=1, source_target_pairs={{0,2},{1,5},{2,0},{3,7},{4,6},{5,1},{6,4},{7,3},{8,10},{9,13},{10,... | collective-permute-start | bytes 1474568 | tf_op jit(solution)/shard_map/ppermute | solution.py:829
  262.4 8.4 %collective-permute-start.32 = (bf16[1,48,1920]{2,1,0:T(8,128)(2,1)S(1)}, bf16[1,48,1920]{2,1,0:T(8,128)(2,1)S(1)}, u32[]{:S(2)}, u32[]{:S(2)}) collective-permute-start(bf16[1,48,1920]{2,1,0:T(8,128)(2,1)S(1)} %get-tuple-element.189), channel_id=1, source_target_pairs={{0,16},{1,9},{2,18},{3,11},{4,20},{5,13},{6,22},{7,15},{8,24},{9,1... | collective-permute-start | bytes 552968 | tf_op jit(solution)/shard_map/ppermute | solution.py:829
  272.0 8.7 %collective-permute-start.33 = (bf16[2,48,1280]{2,1,0:T(8,128)(2,1)S(1)}, bf16[2,48,1280]{2,1,0:T(8,128)(2,1)S(1)}, u32[]{:S(2)}, u32[]{:S(2)}) collective-permute-start(bf16[2,48,1280]{2,1,0:T(8,128)(2,1)S(1)} %get-tuple-element.192), channel_id=1, source_target_pairs={{0,8},{1,17},{2,10},{3,19},{4,12},{5,21},{6,14},{7,23},{8,0},{9,25... | collective-permute-start | bytes 737288 | tf_op jit(solution)/shard_map/ppermute | solution.py:829
  281.9 6.1 %collective-permute-start.35 = (bf16[1,48,1280]{2,1,0:T(8,128)(2,1)S(1)}, bf16[1,48,1280]{2,1,0:T(8,128)(2,1)S(1)}, u32[]{:S(2)}, u32[]{:S(2)}) collective-permute-start(bf16[1,48,1280]{2,1,0:T(8,128)(2,1)S(1)} %get-tuple-element.197), channel_id=1, source_target_pairs={{0,16},{1,9},{2,18},{3,11},{4,20},{5,13},{6,22},{7,15},{8,24},{9,1... | collective-permute-start | bytes 368648 | tf_op jit(solution)/shard_map/ppermute | solution.py:829
  (15 other events, 101.4 us)
where the time goes:
time: 293 us; the launch traced here: 292 us
  Pallas kernels  177 us (60%)
  waiting for transfers between devices  64.7 us (22%)
  starting transfers between devices  36.3 us (12%)
  local copies, waits for them, and re-layouts  12.3 us (4%)
    pallas_call x20, Pallas kernels, call(): return pl.pallas_call(body, in_specs=in_specs, **options)(*operands, *deps)  99.2 us
    ppermute x37, waiting for transfers between devices, move(): return lax.ppermute(v, AXES, [(i, i ^ masks[i & 1]) for i in range(SLABS)])  64.7 us
    pallas_call x1, Pallas kernels, feed_forward(): pl.pallas_call(functools.partial(ffn_kernel, meta, len(pieces), blocks),...  49 us
    ppermute x37, starting transfers between devices, move(): return lax.ppermute(v, AXES, [(i, i ^ masks[i & 1]) for i in range(SLABS)])  36.3 us
    pallas_call x1, Pallas kernels, attend(): pl.pallas_call(functools.partial(attend_kernel, meta, len(pieces)), grid=...  17.4 us
    pallas_call x1, Pallas kernels, inner_grads(): pl.pallas_call(inner_grads_kernel, grid=(steps + 1,), in_specs=[whole(D,...  11 us
    unnamed x26, local copies, waits for them, and re-layouts  7.86 us
  transfers between devices with their start and end apart: 37, of which 21 were waited for; matrix products, arithmetic and copies ran while one was open for 1% of the time, Pallas kernels for 36%

commit v1 on v0

--- a/solution.py
+++ b/solution.py
@@ -733,19 +733,16 @@
 
 def add_up(place, *groups, passed=(), deps=(), vmem=ALL_VMEM):
     operands, specs, out_specs, shapes, jobs = [], [], [], [], []
-    steps = 3 if any(size == CHIPS for size, _ in groups) else 1
-    one_step = all(size > 1 for size, _ in groups)
-    steps = steps if one_step else 1
-    for size, terms in groups:
+    for size, terms, lazy in groups:
         _, rows, lanes = terms[0].shape
-        half, block = size // 2, rows // steps
-        kind = "upper" if size == CHIPS else "both" if size > 1 else "down" if lanes == DOWN_BLOCK else "halves"
+        half = size // 2
+        kind = "upper" if lazy else "both" if size > 1 else "down" if lanes == DOWN_BLOCK else "halves"
         operands += terms
         take = (half, 1) if kind == "upper" else (size, 0)
-        specs += [pl.BlockSpec((take[0], block, lanes), lambda s, at=take[1]: (at, s, 0))] * len(terms)
+        specs += [pl.BlockSpec((take[0], rows, lanes), lambda s, at=take[1]: (at, 0, 0))] * len(terms)
         if size > 1:
             kinds = [bf16] if kind == "upper" else [bf16, f32]
-            out_specs += [pl.BlockSpec((half, block, lanes), lambda s: (0, s, 0))] * len(kinds)
+            out_specs += [whole(half, rows, lanes)] * len(kinds)
             shapes += [jax.ShapeDtypeStruct((half, rows, lanes), dtype) for dtype in kinds]
         else:
             ends = [(2 * PAIR_ROWS, D)] if kind == "down" else [(SLAB, lanes)] * 2
@@ -756,7 +753,7 @@
         lambda *refs: add_up_kernel(jobs, len(passed), refs[0], *refs[1:]),
         [place] + operands + list(passed),
         deps,
-        grid=(steps,),
+        grid=(1,),
         in_specs=[SMEM] + specs + [ANY] * len(passed),
         out_specs=out_specs + [ANY] * len(passed) + [whole(8, 128)],
         out_shape=shapes
@@ -840,23 +837,20 @@
     def __init__(self, keep, got):
         self.size, self.terms, self.step = CHIPS, [keep, got], 0
 
-    def job(self):
-        return self.size, self.terms
-
-    def send(self, outs):
+    def send(self, outs, lazy):
         ready = outs.pop(0)
-        if self.size < CHIPS:
+        if not lazy:
             self.terms = [outs.pop(0)]
         self.size //= 2
         self.terms = self.terms + [move(ready, SUM_STEPS[self.step])]
         self.step += 1
 
 
-def add_and_send(place, *groups, **options):
-    outs = list(add_up(place, *[g.job() for g in groups], **options))
+def add_and_send(place, *groups, lazy=False, **options):
+    outs = list(add_up(place, *[(g.size, g.terms, lazy) for g in groups], **options))
     for g in groups:
         if g.size > 1:
-            g.send(outs)
+            g.send(outs, lazy)
     return outs
 
 
@@ -945,31 +939,29 @@
     deps = []
     if fast:
         down = Sums(down_keep, move(down_send, CORE))
-        inner_send, *deps = add_and_send(place, down, passed=[inner_send], deps=[inner_keep])
+        inner_send, *deps = add_and_send(place, down, lazy=True, passed=[inner_send], deps=[inner_keep])
         inner = Sums(inner_keep, move(inner_send, CORE))
     grads = attend_back(0, third, qkv, back, prob, deps=deps)
     if fast:
-        deps = add_and_send(place, inner, deps=grads[:1])
+        deps = add_and_send(place, inner, lazy=True, deps=grads[:1])
     grads = attend_back(third, third, qkv, back, prob, grads, deps=deps)
     if fast:
-        deps = add_and_send(place, down, deps=grads[:1])
+        deps = add_and_send(place, down, lazy=True, deps=grads[:1])
     grads = attend_back(2 * third, pairs - 2 * third, qkv, back, prob, grads, deps=deps)
     if fast:
-        deps = add_and_send(place, inner, down, deps=grads[:1])
+        deps = add_and_send(place, inner, down, lazy=True, deps=grads[:1])
     proj_keep, proj_send = proj_grads(place, inputs_t, small, db1, grads, deps=deps)
     blocks = inputs.shape[0] // BLOCK
-    early = 1
     if fast:
         proj_send, *deps = add_and_send(place, inner, down, passed=[proj_send], deps=[proj_keep])
         proj = Sums(proj_keep, move(proj_send, CORE))
-        grad_input, *deps = input_back(0, early, first_back, grads, weights, deps=deps)
-        down_grad, *deps = add_and_send(place, proj, down, deps=deps)
-        grad_input, *deps = input_back(early, blocks - early, first_back, grads, weights, [grad_input], deps=deps)
-        deps = add_and_send(place, proj, inner, deps=deps, vmem=LITTLE)
+        deps = add_and_send(place, proj, lazy=True, deps=deps)
+        grad_input, *deps = input_back(0, blocks, first_back, grads, weights, deps=deps)
+        down_grad, *deps = add_and_send(place, proj, inner, down, deps=deps, vmem=LITTLE)
         mine, other, *deps = add_and_send(place, proj, inner, deps=deps, vmem=LITTLE)
         out_grad, inner_grad, *deps = finish_inner(place, mine, move(other, CORE))
-        add_and_send(place, proj, deps=deps, vmem=LITTLE)
-        mine, other, _ = add_and_send(place, proj, vmem=LITTLE)
+        deps = add_and_send(place, proj, deps=deps, vmem=LITTLE)
+        mine, other, _ = add_and_send(place, proj, deps=deps, vmem=LITTLE)
         *square, bias, v0, v1, v2, v3, v4, v5, v6, v7 = finish_proj(place, mine, move(other, CORE))
         vectors = [v0, v1, v2, v3, v4, v5, v6, v7]
     else:

time: 293 us -> 289 us (0.986)
  Pallas kernels: 177 us -> 169 us
    pallas_call x20 -> x19, Pallas kernels: 99.2 us -> 92 us  [call(): return pl.pallas_call(body, in_specs=in_specs, **options)(*operands, *deps)]
  transfers between devices with their start and end apart: 37 -> 37, of which waited for: 21 -> 21; matrix products, arithmetic and copies ran while one was open for 1% -> 1% of each run, Pallas kernels for 36% -> 35%
where the time goes in v1:
time: 289 us; the launch traced here: 287 us
  Pallas kernels  169 us (58%)
  waiting for transfers between devices  66 us (23%)
  starting transfers between devices  37.3 us (13%)
  local copies, waits for them, and re-layouts  12.9 us (4%)
    pallas_call x19, Pallas kernels, call(): return pl.pallas_call(body, in_specs=in_specs, **options)(*operands, *deps)  92 us
    ppermute x37, waiting for transfers between devices, move(): return lax.ppermute(v, AXES, [(i, i ^ masks[i & 1]) for i in range(SLABS)])  66 us
    pallas_call x1, Pallas kernels, feed_forward(): pl.pallas_call(functools.partial(ffn_kernel, meta, len(pieces), blocks),...  49 us
    ppermute x37, starting transfers between devices, move(): return lax.ppermute(v, AXES, [(i, i ^ masks[i & 1]) for i in range(SLABS)])  37.3 us
    pallas_call x1, Pallas kernels, attend(): pl.pallas_call(functools.partial(attend_kernel, meta, len(pieces)), grid=...  17.4 us
    pallas_call x1, Pallas kernels, inner_grads(): pl.pallas_call(inner_grads_kernel, grid=(steps + 1,), in_specs=[whole(D,...  11 us
    unnamed x26, local copies, waits for them, and re-layouts  8.45 us
  transfers between devices with their start and end apart: 37, of which 21 were waited for; matrix products, arithmetic and copies ran while one was open for 1% of the time, Pallas kernels for 35%

profile of v1, /device:TPU:0, one launch (start us, length us, event | category | flops | bytes accessed | tf_op | source)
XLA Modules:
  0.0 287.4 jit_solution(15696228319643259269)
XLA Ops:
  7.8 4.0 %collective-permute-start.1 = (bf16[1,48,1664]{2,1,0:T(8,128)(2,1)S(1)}, bf16[1,48,1664]{2,1,0:T(8,128)(2,1)S(1)}, u32[]{:S(2)}, u32[]{:S(2)}) collective-permute-start(bf16[1,48,1664]{2,1,0:T(8,128)(2,1)S(1)} %fusion.4), channel_id=1, source_target_pairs={{0,16},{1,9},{2,18},{3,11},{4,20},{5,13},{6,22},{7,15},{8,24},{9,1... | collective-permute-start | bytes 479240 | tf_op jit(solution)/shard_map/ppermute | solution.py:826
  11.9 3.7 %collective-permute-done.1 = bf16[1,48,1664]{2,1,0:T(8,128)(2,1)S(1)} collective-permute-done((bf16[1,48,1664]{2,1,0:T(8,128)(2,1)S(1)}, bf16[1,48,1664]{2,1,0:T(8,128)(2,1)S(1)}, u32[]{:S(2)}, u32[]{:S(2)}) %collective-permute-start.1) | collective-permute-done | bytes 159776 | tf_op jit(solution)/shard_map/ppermute | solution.py:826
  15.6 2.5 collective-permute-start.2
  18.1 8.3 %collective-permute-done.2 = bf16[2,48,1664]{2,1,0:T(8,128)(2,1)S(1)} collective-permute-done((bf16[2,48,1664]{2,1,0:T(8,128)(2,1)S(1)}, bf16[2,48,1664]{2,1,0:T(8,128)(2,1)S(1)}, u32[]{:S(2)}, u32[]{:S(2)}) %collective-permute-start.2) | collective-permute-done | bytes 319520 | tf_op jit(solution)/shard_map/ppermute | solution.py:826
  28.2 2.9 %collective-permute-start.8 = (bf16[1,48,3072]{2,1,0:T(8,128)(2,1)S(1)}, bf16[1,48,3072]{2,1,0:T(8,128)(2,1)S(1)}, u32[]{:S(2)}, u32[]{:S(2)}) collective-permute-start(bf16[1,48,3072]{2,1,0:T(8,128)(2,1)S(1)} %fusion.2), channel_id=1, source_target_pairs={{0,24},{1,25},{2,26},{3,27},{4,28},{5,29},{6,30},{7,31},{8,16},{9,... | collective-permute-start | bytes 884744 | tf_op jit(solution)/shard_map/ppermute | solution.py:826
  34.1 7.3 %collective-permute-done.4.refs_1_ = bf16[4,48,1664]{2,1,0:T(8,128)(2,1)S(1)} collective-permute-done((bf16[4,48,1664]{2,1,0:T(8,128)(2,1)S(1)}, bf16[4,48,1664]{2,1,0:T(8,128)(2,1)S(1)}, u32[]{:S(2)}, u32[]{:S(2)}) %collective-permute-start.4) | collective-permute-done | bytes 639008 | tf_op jit(solution)/shard_map/ppermute | solution.py:826
  41.4 2.9 %collective-permute-start.5 = (bf16[4,48,1664]{2,1,0:T(8,128)(2,1)S(1)}, bf16[4,48,1664]{2,1,0:T(8,128)(2,1)}, u32[]{:S(2)}, u32[]{:S(2)}) collective-permute-start(bf16[4,48,1664]{2,1,0:T(8,128)(2,1)S(1)} %collective-permute-done.4.refs_1_), channel_id=1, source_target_pairs={{0,4},{1,3},{2,6},{3,1},{4,0},{5,7},{6,2},{7,5},{8,12},{9,11},{10,... | collective-permute-start | bytes 1916936 | tf_op jit(solution)/shard_map/ppermute | solution.py:826
  45.0 8.7 %collective-permute-done.6 = bf16[1,48,3072]{2,1,0:T(8,128)(2,1)S(1)} collective-permute-done((bf16[1,48,3072]{2,1,0:T(8,128)(2,1)S(1)}, bf16[1,48,3072]{2,1,0:T(8,128)(2,1)S(1)}, u32[]{:S(2)}, u32[]{:S(2)}) %collective-permute-start.6) | collective-permute-done | bytes 294944 | tf_op jit(solution)/shard_map/ppermute | solution.py:826
  58.9 17.4 %attend.1 = (bf16[1024,2304]{1,0:T(8,128)(2,1)}, bf16[1024,768]{1,0:T(8,128)(2,1)}, f32[2,16,512]{2,1,0:T(8,128)}, bf16[768,3328]{1,0:T(8,128)(2,1)}, f32[16,768]{1,0:T(8,128)}) custom-call(s32[2]{0:T(128)} %pad_add_fusion.place.refs_0_, s32[2]{0:T(128)} %refs_0_.3, f32[1024,768]{1,0:T(8,128)} %refs_5_.1, bf16[4,48,1664]{2,1,0:T(8,128)(2,1)} %copy-done.7, ...), custom_call_target="tpu_custom_call" | custom-call | flops 17999998976 | bytes 20971520 | tf_op jit(solution)/shard_map/attend/pallas_call | solution.py:202
  77.9 7.0 %probs.1.refs_4_ = bf16[24,512,512]{2,1,0:T(8,128)(2,1)} custom-call(s32[2]{0:T(128)} %refs_0_.3, bf16[1024,2304]{1,0:T(8,128)(2,1)} %get-tuple-element.117.refs_1_.refs_2_.refs_0_, bf16[1024,2304]{1,0:T(8,128)(2,1)} %get-tuple-element.117.refs_1_.refs_2_.refs_0_, f32[2,16,512]{2,1,0:T(8,128)} %get-tuple-element.118.refs_3_), custom_call_target="tpu_custom_call" | custom-call | flops 8000000000 | bytes 1048576 | tf_op jit(solution)/shard_map/probs/pallas_call | solution.py:67
  86.1 13.2 %window.1 = (bf16[24,512,512]{2,1,0:T(8,128)(2,1)}, f32[1024,768]{1,0:T(8,128)}, f32[1024,128]{1,0:T(8,128)}, bf16[1024,768]{1,0:T(8,128)(2,1)}, bf16[768,1024]{...) custom-call(s32[2]{0:T(128)} %refs_0_.3, ...), custom_call_target="tpu_custom_call", output_to_operand_aliasing={{0}: (4, {})} | custom-call | flops 14000000000 | bytes 1048576 | tf_op jit(solution)/shard_map/window/pallas_call | solution.py:67
  99.2 2.6 collective-permute-done.15.refs_3_
  102.4 2.7 collective-permute-done.18.refs_6_
  106.7 49.0 %feed_forward.1 = (f32[1024,768]{1,0:T(8,128)}, f32[1024,768]{1,0:T(8,128)}, bf16[1024,768]{1,0:T(8,128)(2,1)}, bf16[1024,3072]{1,0:T(8,128)(2,1)}, bf16[1024,76...) custom-call(s32[2]{0:T(128)} %pad_add_fusion.place.refs_0_, ...), custom_call_target="tpu_custom_call" | custom-call | flops 51999997952 | bytes 41943040 | tf_op jit(solution)/shard_map/feed_forward/pallas_call | solution.py:448
  155.9 11.0 %inner_grads.1 = (bf16[16,48,1920]{2,1,0:T(8,128)(2,1)}, bf16[16,48,1920]{2,1,0:T(8,128)(2,1)}) custom-call(bf16[768,1024]{1,0:T(8,128)(2,1)} %get-tuple-element.137.hid_t, bf16[1024,3072]{1,0:T(8,128)(2,1)} %get-tuple-element.138.ib_ref, s32[2]{0:T(128)} %pad_add_fusion.place.refs_0_, bf16[768,1024]{1,0:T(8,128)(2,1)} %get-tuple-element.139.att_in, ...), custom_call_target="tpu_custom_call" | custom-call | flops 4000000000 | bytes 1048576 | tf_op jit(solution)/shard_map/inner_grads/pallas_call | solution.py:518
  166.9 3.0 %add_up.10 = (bf16[8,48,1536]{2,1,0:T(8,128)(2,1)}, bf16[16,48,1920]{2,1,0:T(8,128)(2,1)}, f32[8,128]{1,0:T(8,128)}) custom-call(s32[2]{0:T(128)} %pad_add_fusion.place.refs_0_, bf16[16,48,1536]{2,1,0:T(8,128)(2,1)} %get-tuple-element.135.refs_1_.refs_4_.refs_5_, ...), custom_call_target="tpu_custom_call", output_to_operand_aliasing={{1}: (3, {})} | custom-call | flops 1000 | bytes 1000 | tf_op jit(solution)/shard_map/add_up/pallas_call | solution.py:67
  171.0 8.5 %attend_back_0.1 = (bf16[1024,768]{1,0:T(8,128)(2,1)}, bf16[1024,768]{1,0:T(8,128)(2,1)}, bf16[1024,768]{1,0:T(8,128)(2,1)}) custom-call(bf16[1024,2304]{1,0:T(8,128)(2,1)} %get-tuple-element.117.refs_1_.refs_2_.refs_0_, bf16[1024,2304]{1,0:T(8,128)(2,1)} %get-tuple-element.117.refs_1_.refs_2_.refs_0_, ...), custom_call_target="tpu_custom_call" | custom-call | flops 3000000000 | bytes 1048576 | tf_op jit(solution)/shard_map/attend_back_0/pallas_call | solution.py:67
  179.5 3.3 %add_up.11 = (bf16[8,48,1920]{2,1,0:T(8,128)(2,1)}, f32[8,128]{1,0:T(8,128)}) custom-call(s32[2]{0:T(128)} %pad_add_fusion.place.refs_0_, bf16[16,48,1920]{2,1,0:T(8,128)(2,1)} %get-tuple-element.142.refs_4_.refs_1_, bf16[16,48,1920]{2,1,0:T(8,128)(2,1)} %collective-permute-done.21.refs_2_, bf16[1024,768]{1,0:T(8,128)(2,1)} %get-tuple-element.144.refs_3_.refs_5_), custom_call_target="tpu_custom_call" | custom-call | flops 1000 | bytes 1000 | tf_op jit(solution)/shard_map/add_up/pallas_call | solution.py:67
  184.1 8.5 %attend_back_4.1 = (bf16[1024,768]{1,0:T(8,128)(2,1)}, bf16[1024,768]{1,0:T(8,128)(2,1)}, bf16[1024,768]{1,0:T(8,128)(2,1)}) custom-call(bf16[1024,2304]{1,0:T(8,128)(2,1)} %get-tuple-element.117.refs_1_.refs_2_.refs_0_, bf16[1024,2304]{1,0:T(8,128)(2,1)} %get-tuple-element.117.refs_1_.refs_2_.refs_0_, ...), custom_call_target="tpu_custom_call", output_to_operand_aliasing={{0}: (5, {}), {1}: (6, {}), {2}: (7, {})} | custom-call | flops 3000000000 | bytes 1048576 | tf_op jit(solution)/shard_map/attend_back_4/pallas_call | solution.py:67
  196.3 8.4 %attend_back_8.1 = (bf16[1024,768]{1,0:T(8,128)(2,1)}, bf16[1024,768]{1,0:T(8,128)(2,1)}, bf16[1024,768]{1,0:T(8,128)(2,1)}) custom-call(bf16[1024,2304]{1,0:T(8,128)(2,1)} %get-tuple-element.117.refs_1_.refs_2_.refs_0_, bf16[1024,2304]{1,0:T(8,128)(2,1)} %get-tuple-element.117.refs_1_.refs_2_.refs_0_, ...), custom_call_target="tpu_custom_call", output_to_operand_aliasing={{0}: (5, {}), {1}: (6, {}), {2}: (7, {})} | custom-call | flops 3000000000 | bytes 1048576 | tf_op jit(solution)/shard_map/attend_back_8/pallas_call | solution.py:67
  204.7 3.5 %collective-permute-done.24.refs_7_.refs_8_ = bf16[4,48,1536]{2,1,0:T(8,128)(2,1)} collective-permute-done((bf16[4,48,1536]{2,1,0:T(8,128)(2,1)}, bf16[4,48,1536]{2,1,0:T(8,128)(2,1)}, u32[]{:S(2)}, u32[]{:S(2)}) %collective-permute-start.24) | collective-permute-done | bytes 589856 | tf_op jit(solution)/shard_map/ppermute | solution.py:826
  208.2 3.2 %add_up.13 = (bf16[4,48,1920]{2,1,0:T(8,128)(2,1)}, bf16[2,48,1536]{2,1,0:T(8,128)(2,1)}, f32[8,128]{1,0:T(8,128)}) custom-call(s32[2]{0:T(128)} %pad_add_fusion.place.refs_0_, bf16[16,48,1920]{2,1,0:T(8,128)(2,1)} %get-tuple-element.142.refs_4_.refs_1_, bf16[16,48,1920]{2,1,0:T(8,128)(2,1)} %collective-permute-done.21.refs_2_, ...), custom_call_target="tpu_custom_call" | custom-call | flops 1000 | bytes 1000 | tf_op jit(solution)/shard_map/add_up/pallas_call | solution.py:67
  212.5 10.3 %proj_grads.1 = (bf16[16,48,1280]{2,1,0:T(8,128)(2,1)}, bf16[16,48,1280]{2,1,0:T(8,128)(2,1)}) custom-call(s32[2]{0:T(128)} %pad_add_fusion.place.refs_0_, bf16[768,1024]{1,0:T(8,128)(2,1)} %get-tuple-element.157.refs_1_, f32[6,8,768]{2,1,0:T(8,128)} %get-tuple-element.158.refs_2_, f32[8,3072]{1,0:T(8,128)} %get-tuple-element.159.refs_3_, ...), custom_call_target="tpu_custom_call" | custom-call | flops 4000000000 | bytes 1048576 | tf_op jit(solution)/shard_map/proj_grads/pallas_call | solution.py:67
  223.6 3.6 %add_up.14 = (bf16[2,48,1920]{2,1,0:T(8,128)(2,1)}, f32[2,48,1920]{2,1,0:T(8,128)}, bf16[1,48,1536]{2,1,0:T(8,128)(2,1)}, f32[1,48,1536]{2,1,0:T(8,128)}, bf16[1...) custom-call(s32[2]{0:T(128)} %pad_add_fusion.place.refs_0_, ...), custom_call_target="tpu_custom_call", output_to_operand_aliasing={{4}: (10, {})} | custom-call | flops 1000 | bytes 1000 | tf_op jit(solution)/shard_map/add_up/pallas_call | solution.py:67
  227.6 3.9 %collective-permute-done.27.refs_2_ = bf16[16,48,1280]{2,1,0:T(8,128)(2,1)} collective-permute-done((bf16[16,48,1280]{2,1,0:T(8,128)(2,1)}, bf16[16,48,1280]{2,1,0:T(8,128)(2,1)}, u32[]{:S(2)}, u32[]{:S(2)}) %collective-permute-start.27) | collective-permute-done | bytes 1966112 | tf_op jit(solution)/shard_map/ppermute | solution.py:826
  231.5 2.7 add_up.15
  235.2 3.2 %collective-permute-start.30 = (bf16[1,48,1536]{2,1,0:T(8,128)(2,1)}, bf16[1,48,1536]{2,1,0:T(8,128)(2,1)}, u32[]{:S(2)}, u32[]{:S(2)}) collective-permute-start(bf16[1,48,1536]{2,1,0:T(8,128)(2,1)} %get-tuple-element.175), channel_id=1, source_target_pairs={{0,16},{1,9},{2,18},{3,11},{4,20},{5,13},{6,22},{7,15},{8,24},{9,1... | collective-permute-start | bytes 442376 | tf_op jit(solution)/shard_map/ppermute | solution.py:826
  238.4 9.7 %input_back_0.1 = (f32[1024,768]{1,0:T(8,128)}, f32[8,128]{1,0:T(8,128)}) custom-call(f32[1024,768]{1,0:T(8,128)} %get-tuple-element.132.refs_0_, bf16[1024,768]{1,0:T(8,128)(2,1)} %get-tuple-element.154.refs_8_.refs_4_.refs_1_, bf16[1024,768]{1,0:T(8,128)(2,1)} %get-tuple-element.155.refs_5_.refs_2_, bf16[1024,768]{1,0:T(8,128)(2,1)} %get-tuple-element.156.refs_6_.refs_3_, ...), custom_call_target="tpu_custom_call" | custom-call | flops 10000000000 | bytes 1048576 | tf_op jit(solution)/shard_map/input_back_0/pallas_call | solution.py:67
  254.3 2.7 add_up.16
  260.3 6.0 %collective-permute-done.32.refs_4_ = bf16[1,48,1920]{2,1,0:T(8,128)(2,1)S(1)} collective-permute-done((bf16[1,48,1920]{2,1,0:T(8,128)(2,1)S(1)}, bf16[1,48,1920]{2,1,0:T(8,128)(2,1)S(1)}, u32[]{:S(2)}, u32[]{:S(2)}) %collective-permute-start.32) | collective-permute-done | bytes 184352 | tf_op jit(solution)/shard_map/ppermute | solution.py:826
  272.1 4.2 %collective-permute-done.33.refs_2_ = bf16[2,48,1280]{2,1,0:T(8,128)(2,1)S(1)} collective-permute-done((bf16[2,48,1280]{2,1,0:T(8,128)(2,1)S(1)}, bf16[2,48,1280]{2,1,0:T(8,128)(2,1)S(1)}, u32[]{:S(2)}, u32[]{:S(2)}) %collective-permute-start.33) | collective-permute-done | bytes 245792 | tf_op jit(solution)/shard_map/ppermute | solution.py:826
  276.9 6.5 %collective-permute-done.35.refs_2_ = bf16[1,48,1280]{2,1,0:T(8,128)(2,1)S(1)} collective-permute-done((bf16[1,48,1280]{2,1,0:T(8,128)(2,1)S(1)}, bf16[1,48,1280]{2,1,0:T(8,128)(2,1)S(1)}, u32[]{:S(2)}, u32[]{:S(2)}) %collective-permute-start.35) | collective-permute-done | bytes 122912 | tf_op jit(solution)/shard_map/ppermute | solution.py:826
  (104 shorter events, 52.0 us)
Async XLA Ops:
  7.8 7.8 %collective-permute-start.1 = (bf16[1,48,1664]{2,1,0:T(8,128)(2,1)S(1)}, bf16[1,48,1664]{2,1,0:T(8,128)(2,1)S(1)}, u32[]{:S(2)}, u32[]{:S(2)}) collective-permute-start(bf16[1,48,1664]{2,1,0:T(8,128)(2,1)S(1)} %fusion.4), channel_id=1, source_target_pairs={{0,16},{1,9},{2,18},{3,11},{4,20},{5,13},{6,22},{7,15},{8,24},{9,1... | collective-permute-start | bytes 479240 | tf_op jit(solution)/shard_map/ppermute | solution.py:826
  15.6 10.8 %collective-permute-start.2 = (bf16[2,48,1664]{2,1,0:T(8,128)(2,1)S(1)}, bf16[2,48,1664]{2,1,0:T(8,128)(2,1)S(1)}, u32[]{:S(2)}, u32[]{:S(2)}) collective-permute-start(bf16[2,48,1664]{2,1,0:T(8,128)(2,1)S(1)} %pad_maximum_fusion.1), channel_id=1, source_target_pairs={{0,8},{1,17},{2,10},{3,19},{4,12},{5,21},{6,14},{7,23},{8,0},{9,25... | collective-permute-start | bytes 958472 | tf_op jit(solution)/shard_map/ppermute | solution.py:826
  26.4 14.9 %collective-permute-start.4 = (bf16[4,48,1664]{2,1,0:T(8,128)(2,1)S(1)}, bf16[4,48,1664]{2,1,0:T(8,128)(2,1)S(1)}, u32[]{:S(2)}, u32[]{:S(2)}) collective-permute-start(bf16[4,48,1664]{2,1,0:T(8,128)(2,1)S(1)} %constant_dynamic-update-slice_fusion.8.refs_0_), channel_id=1, source_target_pairs={{0,2},{1,5},{2,0},{3,7},{4,6},{5,1},{6,4},{7,3},{8,10},{9,13},{10,... | collective-permute-start | bytes 1916936 | tf_op jit(solution)/shard_map/ppermute | solution.py:826
  28.2 16.1 %collective-permute-start.8 = (bf16[1,48,3072]{2,1,0:T(8,128)(2,1)S(1)}, bf16[1,48,3072]{2,1,0:T(8,128)(2,1)S(1)}, u32[]{:S(2)}, u32[]{:S(2)}) collective-permute-start(bf16[1,48,3072]{2,1,0:T(8,128)(2,1)S(1)} %fusion.2), channel_id=1, source_target_pairs={{0,24},{1,25},{2,26},{3,27},{4,28},{5,29},{6,30},{7,31},{8,16},{9,... | collective-permute-start | bytes 884744 | tf_op jit(solution)/shard_map/ppermute | solution.py:826
  31.1 13.9 %collective-permute-start.7 = (bf16[1,48,3072]{2,1,0:T(8,128)(2,1)S(1)}, bf16[1,48,3072]{2,1,0:T(8,128)(2,1)S(1)}, u32[]{:S(2)}, u32[]{:S(2)}) collective-permute-start(bf16[1,48,3072]{2,1,0:T(8,128)(2,1)S(1)} %fusion.2), channel_id=1, source_target_pairs={{0,8},{1,17},{2,10},{3,19},{4,12},{5,21},{6,14},{7,23},{8,0},{9,25... | collective-permute-start | bytes 884744 | tf_op jit(solution)/shard_map/ppermute | solution.py:826
  31.1 22.6 %collective-permute-start.6 = (bf16[1,48,3072]{2,1,0:T(8,128)(2,1)S(1)}, bf16[1,48,3072]{2,1,0:T(8,128)(2,1)S(1)}, u32[]{:S(2)}, u32[]{:S(2)}) collective-permute-start(bf16[1,48,3072]{2,1,0:T(8,128)(2,1)S(1)} %fusion.2), channel_id=1, source_target_pairs={{0,16},{1,9},{2,18},{3,11},{4,20},{5,13},{6,22},{7,15},{8,24},{9,1... | collective-permute-start | bytes 884744 | tf_op jit(solution)/shard_map/ppermute | solution.py:826
  32.6 21.9 %collective-permute-start.3 = (bf16[4,48,1664]{2,1,0:T(8,128)(2,1)S(1)}, bf16[4,48,1664]{2,1,0:T(8,128)(2,1)S(1)}, u32[]{:S(2)}, u32[]{:S(2)}) collective-permute-start(bf16[4,48,1664]{2,1,0:T(8,128)(2,1)S(1)} %constant_dynamic-update-slice_fusion.8.refs_0_), channel_id=1, source_target_pairs={{0,4},{1,3},{2,6},{3,1},{4,0},{5,7},{6,2},{7,5},{8,12},{9,11},{10,... | collective-permute-start | bytes 1916936 | tf_op jit(solution)/shard_map/ppermute | solution.py:826
  41.4 13.1 %collective-permute-start.5 = (bf16[4,48,1664]{2,1,0:T(8,128)(2,1)S(1)}, bf16[4,48,1664]{2,1,0:T(8,128)(2,1)}, u32[]{:S(2)}, u32[]{:S(2)}) collective-permute-start(bf16[4,48,1664]{2,1,0:T(8,128)(2,1)S(1)} %collective-permute-done.4.refs_1_), channel_id=1, source_target_pairs={{0,4},{1,3},{2,6},{3,1},{4,0},{5,7},{6,2},{7,5},{8,12},{9,11},{10,... | collective-permute-start | bytes 1916936 | tf_op jit(solution)/shard_map/ppermute | solution.py:826
  53.9 4.0 %collective-permute-start.12 = (bf16[4,48,1664]{2,1,0:T(8,128)(2,1)S(1)}, bf16[4,48,1664]{2,1,0:T(8,128)(2,1)}, u32[]{:S(2)}, u32[]{:S(2)}) collective-permute-start(bf16[4,48,1664]{2,1,0:T(8,128)(2,1)S(1)} %collective-permute-done.4.refs_1_), channel_id=1, source_target_pairs={{0,1},{1,0},{2,3},{3,2},{4,5},{5,4},{6,7},{7,6},{8,9},{9,8},{10,11... | collective-permute-start | bytes 1916936 | tf_op jit(solution)/shard_map/ppermute | solution.py:826
  54.4 4.4 %collective-permute-start.13 = (bf16[4,48,1664]{2,1,0:T(8,128)(2,1)S(1)}, bf16[4,48,1664]{2,1,0:T(8,128)(2,1)}, u32[]{:S(2)}, u32[]{:S(2)}) collective-permute-start(bf16[4,48,1664]{2,1,0:T(8,128)(2,1)S(1)} %collective-permute-done.3.refs_2_), channel_id=1, source_target_pairs={{0,1},{1,0},{2,3},{3,2},{4,5},{5,4},{6,7},{7,6},{8,9},{9,8},{10,11... | collective-permute-start | bytes 1916936 | tf_op jit(solution)/shard_map/ppermute | solution.py:826
  54.6 4.3 %collective-permute-start.14 = (bf16[4,48,1664]{2,1,0:T(8,128)(2,1)}, bf16[4,48,1664]{2,1,0:T(8,128)(2,1)}, u32[]{:S(2)}, u32[]{:S(2)}) collective-permute-start(bf16[4,48,1664]{2,1,0:T(8,128)(2,1)} %collective-permute-done.5.refs_3_), channel_id=1, source_target_pairs={{0,1},{1,0},{2,3},{3,2},{4,5},{5,4},{6,7},{7,6},{8,9},{9,8},{10,11... | collective-permute-start | bytes 1916936 | tf_op jit(solution)/shard_map/ppermute | solution.py:826
  55.6 46.8 %collective-permute-start.16 = (bf16[4,48,3072]{2,1,0:T(8,128)(2,1)S(1)}, bf16[4,48,3072]{2,1,0:T(8,128)(2,1)}, u32[]{:S(2)}, u32[]{:S(2)}) collective-permute-start(bf16[4,48,3072]{2,1,0:T(8,128)(2,1)S(1)} %pad_maximum_fusion.refs_0_), channel_id=1, source_target_pairs={{0,1},{1,0},{2,3},{3,2},{4,5},{5,4},{6,7},{7,6},{8,9},{9,8},{10,11... | collective-permute-start | bytes 3538952 | tf_op jit(solution)/shard_map/ppermute | solution.py:826
  56.1 28.8 %collective-permute-start.10 = (bf16[4,48,3072]{2,1,0:T(8,128)(2,1)S(1)}, bf16[4,48,3072]{2,1,0:T(8,128)(2,1)}, u32[]{:S(2)}, u32[]{:S(2)}) collective-permute-start(bf16[4,48,3072]{2,1,0:T(8,128)(2,1)S(1)} %pad_maximum_fusion.refs_0_), channel_id=1, source_target_pairs={{0,2},{1,5},{2,0},{3,7},{4,6},{5,1},{6,4},{7,3},{8,10},{9,13},{10,... | collective-permute-start | bytes 3538952 | tf_op jit(solution)/shard_map/ppermute | solution.py:826
  57.9 41.3 %collective-permute-start.9 = (bf16[4,48,3072]{2,1,0:T(8,128)(2,1)S(1)}, bf16[4,48,3072]{2,1,0:T(8,128)(2,1)}, u32[]{:S(2)}, u32[]{:S(2)}) collective-permute-start(bf16[4,48,3072]{2,1,0:T(8,128)(2,1)S(1)} %pad_maximum_fusion.refs_0_), channel_id=1, source_target_pairs={{0,4},{1,3},{2,6},{3,1},{4,0},{5,7},{6,2},{7,5},{8,12},{9,11},{10,... | collective-permute-start | bytes 3538952 | tf_op jit(solution)/shard_map/ppermute | solution.py:826
  84.9 17.5 %collective-permute-start.17 = (bf16[4,48,3072]{2,1,0:T(8,128)(2,1)}, bf16[4,48,3072]{2,1,0:T(8,128)(2,1)}, u32[]{:S(2)}, u32[]{:S(2)}) collective-permute-start(bf16[4,48,3072]{2,1,0:T(8,128)(2,1)} %collective-permute-done.10.refs_1_), channel_id=1, source_target_pairs={{0,1},{1,0},{2,3},{3,2},{4,5},{5,4},{6,7},{7,6},{8,9},{9,8},{10,11... | collective-permute-start | bytes 3538952 | tf_op jit(solution)/shard_map/ppermute | solution.py:826
  85.3 16.5 %collective-permute-start.15 = (bf16[4,48,3072]{2,1,0:T(8,128)(2,1)}, bf16[4,48,3072]{2,1,0:T(8,128)(2,1)}, u32[]{:S(2)}, u32[]{:S(2)}) collective-permute-start(bf16[4,48,3072]{2,1,0:T(8,128)(2,1)} %collective-permute-done.10.refs_1_), channel_id=1, source_target_pairs={{0,4},{1,3},{2,6},{3,1},{4,0},{5,7},{6,2},{7,5},{8,12},{9,11},{10,... | collective-permute-start | bytes 3538952 | tf_op jit(solution)/shard_map/ppermute | solution.py:826
  101.9 4.9 %collective-permute-start.19 = (bf16[4,48,3072]{2,1,0:T(8,128)(2,1)}, bf16[4,48,3072]{2,1,0:T(8,128)(2,1)}, u32[]{:S(2)}, u32[]{:S(2)}) collective-permute-start(bf16[4,48,3072]{2,1,0:T(8,128)(2,1)} %collective-permute-done.15.refs_3_), channel_id=1, source_target_pairs={{0,1},{1,0},{2,3},{3,2},{4,5},{5,4},{6,7},{7,6},{8,9},{9,8},{10,11... | collective-permute-start | bytes 3538952 | tf_op jit(solution)/shard_map/ppermute | solution.py:826
  155.7 11.2 %collective-permute-start.20 = (bf16[16,48,1536]{2,1,0:T(8,128)(2,1)}, bf16[16,48,1536]{2,1,0:T(8,128)(2,1)}, u32[]{:S(2)}, u32[]{:S(2)}) collective-permute-start(bf16[16,48,1536]{2,1,0:T(8,128)(2,1)} %get-tuple-element.136), channel_id=1, source_target_pairs={{0,1},{1,0},{2,3},{3,2},{4,5},{5,4},{6,7},{7,6},{8,9},{9,8},{10,11... | collective-permute-start | bytes 7077896 | tf_op jit(solution)/shard_map/ppermute | solution.py:826
  169.9 9.6 %collective-permute-start.21 = (bf16[16,48,1920]{2,1,0:T(8,128)(2,1)}, bf16[16,48,1920]{2,1,0:T(8,128)(2,1)}, u32[]{:S(2)}, u32[]{:S(2)}) collective-permute-start(bf16[16,48,1920]{2,1,0:T(8,128)(2,1)} %get-tuple-element.147), channel_id=1, source_target_pairs={{0,1},{1,0},{2,3},{3,2},{4,5},{5,4},{6,7},{7,6},{8,9},{9,8},{10,11... | collective-permute-start | bytes 8847368 | tf_op jit(solution)/shard_map/ppermute | solution.py:826
  170.2 22.3 %collective-permute-start.22 = (bf16[8,48,1536]{2,1,0:T(8,128)(2,1)}, bf16[8,48,1536]{2,1,0:T(8,128)(2,1)}, u32[]{:S(2)}, u32[]{:S(2)}) collective-permute-start(bf16[8,48,1536]{2,1,0:T(8,128)(2,1)} %get-tuple-element.152), channel_id=1, source_target_pairs={{0,4},{1,3},{2,6},{3,1},{4,0},{5,7},{6,2},{7,5},{8,12},{9,11},{10,... | collective-permute-start | bytes 3538952 | tf_op jit(solution)/shard_map/ppermute | solution.py:826
  182.8 25.4 %collective-permute-start.23 = (bf16[8,48,1920]{2,1,0:T(8,128)(2,1)}, bf16[8,48,1920]{2,1,0:T(8,128)(2,1)}, u32[]{:S(2)}, u32[]{:S(2)}) collective-permute-start(bf16[8,48,1920]{2,1,0:T(8,128)(2,1)} %get-tuple-element.160), channel_id=1, source_target_pairs={{0,4},{1,3},{2,6},{3,1},{4,0},{5,7},{6,2},{7,5},{8,12},{9,11},{10,... | collective-permute-start | bytes 4423688 | tf_op jit(solution)/shard_map/ppermute | solution.py:826
  195.0 13.1 %collective-permute-start.24 = (bf16[4,48,1536]{2,1,0:T(8,128)(2,1)}, bf16[4,48,1536]{2,1,0:T(8,128)(2,1)}, u32[]{:S(2)}, u32[]{:S(2)}) collective-permute-start(bf16[4,48,1536]{2,1,0:T(8,128)(2,1)} %get-tuple-element.161), channel_id=1, source_target_pairs={{0,2},{1,5},{2,0},{3,7},{4,6},{5,1},{6,4},{7,3},{8,10},{9,13},{10,... | collective-permute-start | bytes 1769480 | tf_op jit(solution)/shard_map/ppermute | solution.py:826
  211.4 11.8 %collective-permute-start.25 = (bf16[4,48,1920]{2,1,0:T(8,128)(2,1)}, bf16[4,48,1920]{2,1,0:T(8,128)(2,1)}, u32[]{:S(2)}, u32[]{:S(2)}) collective-permute-start(bf16[4,48,1920]{2,1,0:T(8,128)(2,1)} %get-tuple-element.164), channel_id=1, source_target_pairs={{0,2},{1,5},{2,0},{3,7},{4,6},{5,1},{6,4},{7,3},{8,10},{9,13},{10,... | collective-permute-start | bytes 2211848 | tf_op jit(solution)/shard_map/ppermute | solution.py:826
  212.5 10.3 %collective-permute-start.26 = (bf16[2,48,1536]{2,1,0:T(8,128)(2,1)}, bf16[2,48,1536]{2,1,0:T(8,128)(2,1)S(1)}, u32[]{:S(2)}, u32[]{:S(2)}) collective-permute-start(bf16[2,48,1536]{2,1,0:T(8,128)(2,1)} %get-tuple-element.165), channel_id=1, source_target_pairs={{0,8},{1,17},{2,10},{3,19},{4,12},{5,21},{6,14},{7,23},{8,0},{9,25... | collective-permute-start | bytes 884744 | tf_op jit(solution)/shard_map/ppermute | solution.py:826
  227.2 4.3 %collective-permute-start.27 = (bf16[16,48,1280]{2,1,0:T(8,128)(2,1)}, bf16[16,48,1280]{2,1,0:T(8,128)(2,1)}, u32[]{:S(2)}, u32[]{:S(2)}) collective-permute-start(bf16[16,48,1280]{2,1,0:T(8,128)(2,1)} %get-tuple-element.167), channel_id=1, source_target_pairs={{0,1},{1,0},{2,3},{3,2},{4,5},{5,4},{6,7},{7,6},{8,9},{9,8},{10,11... | collective-permute-start | bytes 5898248 | tf_op jit(solution)/shard_map/ppermute | solution.py:826
  234.2 15.8 %collective-permute-start.28 = (bf16[8,48,1280]{2,1,0:T(8,128)(2,1)}, bf16[8,48,1280]{2,1,0:T(8,128)(2,1)}, u32[]{:S(2)}, u32[]{:S(2)}) collective-permute-start(bf16[8,48,1280]{2,1,0:T(8,128)(2,1)} %get-tuple-element.171), channel_id=1, source_target_pairs={{0,4},{1,3},{2,6},{3,1},{4,0},{5,7},{6,2},{7,5},{8,12},{9,11},{10,... | collective-permute-start | bytes 2949128 | tf_op jit(solution)/shard_map/ppermute | solution.py:826
  235.2 12.9 %collective-permute-start.30 = (bf16[1,48,1536]{2,1,0:T(8,128)(2,1)}, bf16[1,48,1536]{2,1,0:T(8,128)(2,1)}, u32[]{:S(2)}, u32[]{:S(2)}) collective-permute-start(bf16[1,48,1536]{2,1,0:T(8,128)(2,1)} %get-tuple-element.175), channel_id=1, source_target_pairs={{0,16},{1,9},{2,18},{3,11},{4,20},{5,13},{6,22},{7,15},{8,24},{9,1... | collective-permute-start | bytes 442376 | tf_op jit(solution)/shard_map/ppermute | solution.py:826
  238.4 11.6 %collective-permute-start.29 = (bf16[2,48,1920]{2,1,0:T(8,128)(2,1)}, bf16[2,48,1920]{2,1,0:T(8,128)(2,1)S(1)}, u32[]{:S(2)}, u32[]{:S(2)}) collective-permute-start(bf16[2,48,1920]{2,1,0:T(8,128)(2,1)} %get-tuple-element.173), channel_id=1, source_target_pairs={{0,8},{1,17},{2,10},{3,19},{4,12},{5,21},{6,14},{7,23},{8,0},{9,25... | collective-permute-start | bytes 1105928 | tf_op jit(solution)/shard_map/ppermute | solution.py:826
  257.0 9.3 %collective-permute-start.31 = (bf16[4,48,1280]{2,1,0:T(8,128)(2,1)S(1)}, bf16[4,48,1280]{2,1,0:T(8,128)(2,1)S(1)}, u32[]{:S(2)}, u32[]{:S(2)}) collective-permute-start(bf16[4,48,1280]{2,1,0:T(8,128)(2,1)S(1)} %get-tuple-element.178), channel_id=1, source_target_pairs={{0,2},{1,5},{2,0},{3,7},{4,6},{5,1},{6,4},{7,3},{8,10},{9,13},{10,... | collective-permute-start | bytes 1474568 | tf_op jit(solution)/shard_map/ppermute | solution.py:826
  257.8 8.5 %collective-permute-start.32 = (bf16[1,48,1920]{2,1,0:T(8,128)(2,1)S(1)}, bf16[1,48,1920]{2,1,0:T(8,128)(2,1)S(1)}, u32[]{:S(2)}, u32[]{:S(2)}) collective-permute-start(bf16[1,48,1920]{2,1,0:T(8,128)(2,1)S(1)} %get-tuple-element.180), channel_id=1, source_target_pairs={{0,16},{1,9},{2,18},{3,11},{4,20},{5,13},{6,22},{7,15},{8,24},{9,1... | collective-permute-start | bytes 552968 | tf_op jit(solution)/shard_map/ppermute | solution.py:826
  267.5 8.8 %collective-permute-start.33 = (bf16[2,48,1280]{2,1,0:T(8,128)(2,1)S(1)}, bf16[2,48,1280]{2,1,0:T(8,128)(2,1)S(1)}, u32[]{:S(2)}, u32[]{:S(2)}) collective-permute-start(bf16[2,48,1280]{2,1,0:T(8,128)(2,1)S(1)} %get-tuple-element.183), channel_id=1, source_target_pairs={{0,8},{1,17},{2,10},{3,19},{4,12},{5,21},{6,14},{7,23},{8,0},{9,25... | collective-permute-start | bytes 737288 | tf_op jit(solution)/shard_map/ppermute | solution.py:826
  276.9 6.6 %collective-permute-start.35 = (bf16[1,48,1280]{2,1,0:T(8,128)(2,1)S(1)}, bf16[1,48,1280]{2,1,0:T(8,128)(2,1)S(1)}, u32[]{:S(2)}, u32[]{:S(2)}) collective-permute-start(bf16[1,48,1280]{2,1,0:T(8,128)(2,1)S(1)} %get-tuple-element.188), channel_id=1, source_target_pairs={{0,16},{1,9},{2,18},{3,11},{4,20},{5,13},{6,22},{7,15},{8,24},{9,1... | collective-permute-start | bytes 368648 | tf_op jit(solution)/shard_map/ppermute | solution.py:826
  (15 other events, 101.0 us)

commit v2 on v1

--- a/solution.py
+++ b/solution.py
@@ -613,10 +613,8 @@
         one = lax.broadcasted_iota(jnp.int32, (SLABS, FF), 0)
         mine = jnp.where(owner == one, jnp.sum(db1_ref[...], axis=0, keepdims=True), 0.0)
         place_of = lax.broadcasted_iota(jnp.int32, (FF, 128), 0) % (4 * SLAB)
-        pick = (place_of == lax.broadcasted_iota(jnp.int32, (FF, 128), 1)).astype(f32)
-        table = lax.dot_general(
-            mine, pick, (((1,), (0,)), ((), ())), precision=lax.Precision.HIGHEST, preferred_element_type=f32
-        )
+        pick = place_of == lax.broadcasted_iota(jnp.int32, (FF, 128), 1)
+        table = dot(mine.astype(bf16), pick.astype(bf16))
         spread = jnp.broadcast_to(table[:, None, :], (SLABS, SLAB, 128)).reshape(D, 128)
         packed[:, QKV_BLOCK + QKV_HALF :] = spread.astype(bf16)
 
@@ -667,7 +665,7 @@
     total = total + dot_t(dk_ref[:, :half], w_ref[:, D:QKV_HALF])
     total = total + dot_t(dk_ref[:, half:], w_ref[:, PROJ_BLOCK : PROJ_BLOCK + half])
     out_ref, small_ref = refs[-2:]
-    small_ref[...] = total[0:8, 0:128]
+    small_ref[...] = total[0:16, 0:128]
     out_ref[...] = total + dot_t(dv_ref[...], w_ref[:, PROJ_BLOCK + half : PROJ_BLOCK + QKV_HALF])
 
 
@@ -679,8 +677,8 @@
         deps,
         grid=(blocks,),
         in_specs=[token] * 4 + [whole(D, 2 * PROJ_BLOCK)] + [ANY] * len(given),
-        out_specs=[token, whole(8, 128)],
-        out_shape=[jax.ShapeDtypeStruct(first_back.shape, f32), jax.ShapeDtypeStruct((8, 128), f32)],
+        out_specs=[token, whole(16, 128)],
+        out_shape=[jax.ShapeDtypeStruct(first_back.shape, f32), jax.ShapeDtypeStruct((16, 128), f32)],
         input_output_aliases={5: 0} if given else {},
         compiler_params=pltpu.CompilerParams(vmem_limit_bytes=ALL_VMEM),
         cost_estimate=pl.CostEstimate(flops=10_000_000_000, bytes_accessed=MIB, transcendentals=0),
@@ -766,6 +764,22 @@
     )
 
 
+def gate(value, deps, vmem=ALL_VMEM):
+    return call(
+        lambda value_ref, out_ref: None,
+        [value],
+        deps,
+        grid=(1,),
+        in_specs=[ANY],
+        out_specs=ANY,
+        out_shape=jax.ShapeDtypeStruct(value.shape, value.dtype),
+        input_output_aliases={0: 0},
+        compiler_params=pltpu.CompilerParams(vmem_limit_bytes=vmem),
+        cost_estimate=pl.CostEstimate(flops=1000, bytes_accessed=1000, transcendentals=0),
+        name="gate",
+    )
+
+
 def finish_inner_kernel(place, mine, other, out_g, inner_g, small):
     low_core = place[1] == 0
     low = jnp.where(low_core, mine[...], other[...])
@@ -919,17 +933,17 @@
     qkv, attended, stats, weights, vectors = attend(place, lengths, inputs, first, meta)
     prob = probs(0, lengths, qkv, stats)
     if fast:
-        second_came, prob = after(second_came, prob)
-        second_last, came_core = move(second_came, ALONG_XY_THEN), move(second_came, CORE)
+        second_came, second_then, prob = after(second_came, second_then, prob)
+        second_last, came_core, then_core = move(second_came, ALONG_XY_THEN), move(second_came, CORE), move(second_then, CORE)
     prob, normed, rstd, hid, inputs_t, attended_t, hid_t = window(
         1, lengths, inputs, qkv, attended, stats, weights, vectors, prob
     )
     bias_at = PROJ_BLOCK + QKV_HALF
     inner_bias = weights[::SLAB, bias_at : bias_at + 4 * SLAB].reshape(1, FF).astype(f32)
     if fast:
-        second_then, second_last, normed, inner_bias = after(second_then, second_last, normed, inner_bias)
+        second_last, normed, inner_bias = after(second_last, normed, inner_bias)
         second = [second, second_came, second_then, second_last]
-        second += [second_core, came_core, move(second_then, CORE), move(second_last, CORE)]
+        second += [second_core, came_core, then_core, move(second_last, CORE)]
     output, first_back, back, inner_back, branch, small, db1, down_keep, down_send = feed_forward(
         place, normed, rstd, hid, cotangent, vectors, inner_bias, weights, second, meta
     )
@@ -953,14 +967,18 @@
     proj_keep, proj_send = proj_grads(place, inputs_t, small, db1, grads, deps=deps)
     blocks = inputs.shape[0] // BLOCK
     if fast:
-        proj_send, *deps = add_and_send(place, inner, down, passed=[proj_send], deps=[proj_keep])
+        proj_send = gate(proj_send, [inner.terms[-1], down.terms[-1]])
         proj = Sums(proj_keep, move(proj_send, CORE))
+        deps = add_and_send(place, inner, down, deps=[proj_keep])
         deps = add_and_send(place, proj, lazy=True, deps=deps)
-        grad_input, *deps = input_back(0, blocks, first_back, grads, weights, deps=deps)
-        down_grad, *deps = add_and_send(place, proj, inner, down, deps=deps, vmem=LITTLE)
+        grad_input, came = input_back(0, blocks, first_back, grads, weights, deps=deps)
+        proj.terms[-1] = gate(proj.terms[-1], [inner.terms[-1], down.terms[-1], came], MIB)
+        deps = add_and_send(place, proj, vmem=LITTLE)
+        down_grad, *deps = add_and_send(place, inner, down, deps=deps, vmem=LITTLE)
+        proj.terms[-1] = gate(proj.terms[-1], [inner.terms[-1]], MIB)
+        deps = add_and_send(place, proj, deps=deps, vmem=LITTLE)
         mine, other, *deps = add_and_send(place, proj, inner, deps=deps, vmem=LITTLE)
         out_grad, inner_grad, *deps = finish_inner(place, mine, move(other, CORE))
-        deps = add_and_send(place, proj, deps=deps, vmem=LITTLE)
         mine, other, _ = add_and_send(place, proj, deps=deps, vmem=LITTLE)
         *square, bias, v0, v1, v2, v3, v4, v5, v6, v7 = finish_proj(place, mine, move(other, CORE))
         vectors = [v0, v1, v2, v3, v4, v5, v6, v7]

time: 289 us -> 279 us (0.965)
  waiting for transfers between devices: 66 us -> 57 us
  local copies, waits for them, and re-layouts: 12.9 us -> 8.91 us
    ppermute x37, waiting for transfers between devices: 66 us -> 57 us  [move(): return lax.ppermute(v, AXES, [(i, i ^ masks[i & 1]) for i in range(SLABS)])]
    unnamed x26, local copies, waits for them, and re-layouts: 8.45 us -> 4.48 us
    pallas_call x19 -> x23, Pallas kernels: 92 us -> 92.2 us  [call(): return pl.pallas_call(body, in_specs=in_specs, **options)(*operands, *deps)]
  transfers between devices with their start and end apart: 37 -> 37, of which waited for: 21 -> 18; matrix products, arithmetic and copies ran while one was open for 1% -> 1% of each run, Pallas kernels for 35% -> 38%
where the time goes in v2:
time: 279 us; the launch traced here: 278 us
  Pallas kernels  170 us (61%)
  waiting for transfers between devices  57 us (20%)
  starting transfers between devices  40.1 us (14%)
  local copies, waits for them, and re-layouts  8.91 us (3%)
    pallas_call x23, Pallas kernels, call(): return pl.pallas_call(body, in_specs=in_specs, **options)(*operands, *deps)  92.2 us
    ppermute x37, waiting for transfers between devices, move(): return lax.ppermute(v, AXES, [(i, i ^ masks[i & 1]) for i in range(SLABS)])  57 us
    pallas_call x1, Pallas kernels, feed_forward(): pl.pallas_call(functools.partial(ffn_kernel, meta, len(pieces), blocks),...  49 us
    ppermute x37, starting transfers between devices, move(): return lax.ppermute(v, AXES, [(i, i ^ masks[i & 1]) for i in range(SLABS)])  40.1 us
    pallas_call x1, Pallas kernels, attend(): pl.pallas_call(functools.partial(attend_kernel, meta, len(pieces)), grid=...  17.4 us
    pallas_call x1, Pallas kernels, inner_grads(): pl.pallas_call(inner_grads_kernel, grid=(steps + 1,), in_specs=[whole(D,...  11 us
  transfers between devices with their start and end apart: 37, of which 18 were waited for; matrix products, arithmetic and copies ran while one was open for 1% of the time, Pallas kernels for 38%

profile of v2, /device:TPU:0, one launch (start us, length us, event | category | flops | bytes accessed | tf_op | source)
XLA Modules:
  0.0 277.5 jit_solution(9562971315832343740)
XLA Ops:
  7.8 4.0 %collective-permute-start.1 = (bf16[1,48,1664]{2,1,0:T(8,128)(2,1)S(1)}, bf16[1,48,1664]{2,1,0:T(8,128)(2,1)S(1)}, u32[]{:S(2)}, u32[]{:S(2)}) collective-permute-start(bf16[1,48,1664]{2,1,0:T(8,128)(2,1)S(1)} %fusion.4), channel_id=1, source_target_pairs={{0,16},{1,9},{2,18},{3,11},{4,20},{5,13},{6,22},{7,15},{8,24},{9,1... | collective-permute-start | bytes 479240 | tf_op jit(solution)/shard_map/ppermute | solution.py:840
  11.9 3.7 %collective-permute-done.1 = bf16[1,48,1664]{2,1,0:T(8,128)(2,1)S(1)} collective-permute-done((bf16[1,48,1664]{2,1,0:T(8,128)(2,1)S(1)}, bf16[1,48,1664]{2,1,0:T(8,128)(2,1)S(1)}, u32[]{:S(2)}, u32[]{:S(2)}) %collective-permute-start.1) | collective-permute-done | bytes 159776 | tf_op jit(solution)/shard_map/ppermute | solution.py:840
  15.6 2.5 collective-permute-start.2
  18.1 8.3 %collective-permute-done.2 = bf16[2,48,1664]{2,1,0:T(8,128)(2,1)S(1)} collective-permute-done((bf16[2,48,1664]{2,1,0:T(8,128)(2,1)S(1)}, bf16[2,48,1664]{2,1,0:T(8,128)(2,1)S(1)}, u32[]{:S(2)}, u32[]{:S(2)}) %collective-permute-start.2) | collective-permute-done | bytes 319520 | tf_op jit(solution)/shard_map/ppermute | solution.py:840
  28.2 2.9 %collective-permute-start.8 = (bf16[1,48,3072]{2,1,0:T(8,128)(2,1)S(1)}, bf16[1,48,3072]{2,1,0:T(8,128)(2,1)S(1)}, u32[]{:S(2)}, u32[]{:S(2)}) collective-permute-start(bf16[1,48,3072]{2,1,0:T(8,128)(2,1)S(1)} %fusion.2), channel_id=1, source_target_pairs={{0,24},{1,25},{2,26},{3,27},{4,28},{5,29},{6,30},{7,31},{8,16},{9,... | collective-permute-start | bytes 884744 | tf_op jit(solution)/shard_map/ppermute | solution.py:840
  34.1 7.3 %collective-permute-done.4.refs_1_ = bf16[4,48,1664]{2,1,0:T(8,128)(2,1)S(1)} collective-permute-done((bf16[4,48,1664]{2,1,0:T(8,128)(2,1)S(1)}, bf16[4,48,1664]{2,1,0:T(8,128)(2,1)S(1)}, u32[]{:S(2)}, u32[]{:S(2)}) %collective-permute-start.4) | collective-permute-done | bytes 639008 | tf_op jit(solution)/shard_map/ppermute | solution.py:840
  41.4 2.9 %collective-permute-start.5 = (bf16[4,48,1664]{2,1,0:T(8,128)(2,1)S(1)}, bf16[4,48,1664]{2,1,0:T(8,128)(2,1)}, u32[]{:S(2)}, u32[]{:S(2)}) collective-permute-start(bf16[4,48,1664]{2,1,0:T(8,128)(2,1)S(1)} %collective-permute-done.4.refs_1_), channel_id=1, source_target_pairs={{0,4},{1,3},{2,6},{3,1},{4,0},{5,7},{6,2},{7,5},{8,12},{9,11},{10,... | collective-permute-start | bytes 1916936 | tf_op jit(solution)/shard_map/ppermute | solution.py:840
  45.0 8.7 %collective-permute-done.6 = bf16[1,48,3072]{2,1,0:T(8,128)(2,1)S(1)} collective-permute-done((bf16[1,48,3072]{2,1,0:T(8,128)(2,1)S(1)}, bf16[1,48,3072]{2,1,0:T(8,128)(2,1)S(1)}, u32[]{:S(2)}, u32[]{:S(2)}) %collective-permute-start.6) | collective-permute-done | bytes 294944 | tf_op jit(solution)/shard_map/ppermute | solution.py:840
  59.4 17.4 %attend.1 = (bf16[1024,2304]{1,0:T(8,128)(2,1)}, bf16[1024,768]{1,0:T(8,128)(2,1)}, f32[2,16,512]{2,1,0:T(8,128)}, bf16[768,3328]{1,0:T(8,128)(2,1)}, f32[16,768]{1,0:T(8,128)}) custom-call(s32[2]{0:T(128)} %pad_add_fusion.place.refs_0_, s32[2]{0:T(128)} %refs_0_.3, f32[1024,768]{1,0:T(8,128)} %refs_5_.1, bf16[4,48,1664]{2,1,0:T(8,128)(2,1)} %copy-done.7, ...), custom_call_target="tpu_custom_call" | custom-call | flops 17999998976 | bytes 20971520 | tf_op jit(solution)/shard_map/attend/pallas_call | solution.py:202
  78.5 7.0 %probs.1.refs_4_ = bf16[24,512,512]{2,1,0:T(8,128)(2,1)} custom-call(s32[2]{0:T(128)} %refs_0_.3, bf16[1024,2304]{1,0:T(8,128)(2,1)} %get-tuple-element.117.refs_1_.refs_2_.refs_0_, bf16[1024,2304]{1,0:T(8,128)(2,1)} %get-tuple-element.117.refs_1_.refs_2_.refs_0_, f32[2,16,512]{2,1,0:T(8,128)} %get-tuple-element.118.refs_3_), custom_call_target="tpu_custom_call" | custom-call | flops 8000000000 | bytes 1048576 | tf_op jit(solution)/shard_map/probs/pallas_call | solution.py:67
  86.7 13.2 %window.1 = (bf16[24,512,512]{2,1,0:T(8,128)(2,1)}, f32[1024,768]{1,0:T(8,128)}, f32[1024,128]{1,0:T(8,128)}, bf16[1024,768]{1,0:T(8,128)(2,1)}, bf16[768,1024]{...) custom-call(s32[2]{0:T(128)} %refs_0_.3, ...), custom_call_target="tpu_custom_call", output_to_operand_aliasing={{0}: (4, {})} | custom-call | flops 14000000000 | bytes 1048576 | tf_op jit(solution)/shard_map/window/pallas_call | solution.py:67
  99.9 2.3 collective-permute-done.15.refs_3_
  102.2 3.2 %collective-permute-done.19.refs_7_ = bf16[4,48,3072]{2,1,0:T(8,128)(2,1)} collective-permute-done((bf16[4,48,3072]{2,1,0:T(8,128)(2,1)}, bf16[4,48,3072]{2,1,0:T(8,128)(2,1)}, u32[]{:S(2)}, u32[]{:S(2)}) %collective-permute-start.19) | collective-permute-done | bytes 1179680 | tf_op jit(solution)/shard_map/ppermute | solution.py:840
  105.4 49.0 %feed_forward.1 = (f32[1024,768]{1,0:T(8,128)}, f32[1024,768]{1,0:T(8,128)}, bf16[1024,768]{1,0:T(8,128)(2,1)}, bf16[1024,3072]{1,0:T(8,128)(2,1)}, bf16[1024,76...) custom-call(s32[2]{0:T(128)} %pad_add_fusion.place.refs_0_, ...), custom_call_target="tpu_custom_call" | custom-call | flops 51999997952 | bytes 41943040 | tf_op jit(solution)/shard_map/feed_forward/pallas_call | solution.py:448
  154.6 11.0 %inner_grads.1 = (bf16[16,48,1920]{2,1,0:T(8,128)(2,1)}, bf16[16,48,1920]{2,1,0:T(8,128)(2,1)}) custom-call(bf16[768,1024]{1,0:T(8,128)(2,1)} %get-tuple-element.137.hid_t, bf16[1024,3072]{1,0:T(8,128)(2,1)} %get-tuple-element.138.ib_ref, s32[2]{0:T(128)} %pad_add_fusion.place.refs_0_, bf16[768,1024]{1,0:T(8,128)(2,1)} %get-tuple-element.139.att_in, ...), custom_call_target="tpu_custom_call" | custom-call | flops 4000000000 | bytes 1048576 | tf_op jit(solution)/shard_map/inner_grads/pallas_call | solution.py:518
  165.6 3.0 %add_up.11 = (bf16[8,48,1536]{2,1,0:T(8,128)(2,1)}, bf16[16,48,1920]{2,1,0:T(8,128)(2,1)}, f32[8,128]{1,0:T(8,128)}) custom-call(s32[2]{0:T(128)} %pad_add_fusion.place.refs_0_, bf16[16,48,1536]{2,1,0:T(8,128)(2,1)} %get-tuple-element.135.refs_1_.refs_4_.refs_5_, ...), custom_call_target="tpu_custom_call", output_to_operand_aliasing={{1}: (3, {})} | custom-call | flops 1000 | bytes 1000 | tf_op jit(solution)/shard_map/add_up/pallas_call | solution.py:67
  169.4 8.4 %attend_back_0.1 = (bf16[1024,768]{1,0:T(8,128)(2,1)}, bf16[1024,768]{1,0:T(8,128)(2,1)}, bf16[1024,768]{1,0:T(8,128)(2,1)}) custom-call(bf16[1024,2304]{1,0:T(8,128)(2,1)} %get-tuple-element.117.refs_1_.refs_2_.refs_0_, bf16[1024,2304]{1,0:T(8,128)(2,1)} %get-tuple-element.117.refs_1_.refs_2_.refs_0_, ...), custom_call_target="tpu_custom_call" | custom-call | flops 3000000000 | bytes 1048576 | tf_op jit(solution)/shard_map/attend_back_0/pallas_call | solution.py:67
  177.8 3.3 %add_up.12 = (bf16[8,48,1920]{2,1,0:T(8,128)(2,1)}, f32[8,128]{1,0:T(8,128)}) custom-call(s32[2]{0:T(128)} %pad_add_fusion.place.refs_0_, bf16[16,48,1920]{2,1,0:T(8,128)(2,1)} %get-tuple-element.142.refs_4_.refs_1_, bf16[16,48,1920]{2,1,0:T(8,128)(2,1)} %collective-permute-done.21.refs_2_, bf16[1024,768]{1,0:T(8,128)(2,1)} %get-tuple-element.144.refs_3_.refs_5_), custom_call_target="tpu_custom_call" | custom-call | flops 1000 | bytes 1000 | tf_op jit(solution)/shard_map/add_up/pallas_call | solution.py:67
  182.7 8.4 %attend_back_4.1 = (bf16[1024,768]{1,0:T(8,128)(2,1)}, bf16[1024,768]{1,0:T(8,128)(2,1)}, bf16[1024,768]{1,0:T(8,128)(2,1)}) custom-call(bf16[1024,2304]{1,0:T(8,128)(2,1)} %get-tuple-element.117.refs_1_.refs_2_.refs_0_, bf16[1024,2304]{1,0:T(8,128)(2,1)} %get-tuple-element.117.refs_1_.refs_2_.refs_0_, ...), custom_call_target="tpu_custom_call", output_to_operand_aliasing={{0}: (5, {}), {1}: (6, {}), {2}: (7, {})} | custom-call | flops 3000000000 | bytes 1048576 | tf_op jit(solution)/shard_map/attend_back_4/pallas_call | solution.py:67
  191.1 2.5 add_up.13
  194.6 8.5 %attend_back_8.1 = (bf16[1024,768]{1,0:T(8,128)(2,1)}, bf16[1024,768]{1,0:T(8,128)(2,1)}, bf16[1024,768]{1,0:T(8,128)(2,1)}) custom-call(bf16[1024,2304]{1,0:T(8,128)(2,1)} %get-tuple-element.117.refs_1_.refs_2_.refs_0_, bf16[1024,2304]{1,0:T(8,128)(2,1)} %get-tuple-element.117.refs_1_.refs_2_.refs_0_, ...), custom_call_target="tpu_custom_call", output_to_operand_aliasing={{0}: (5, {}), {1}: (6, {}), {2}: (7, {})} | custom-call | flops 3000000000 | bytes 1048576 | tf_op jit(solution)/shard_map/attend_back_8/pallas_call | solution.py:67
  203.0 3.7 %collective-permute-done.24.refs_7_.refs_8_ = bf16[4,48,1536]{2,1,0:T(8,128)(2,1)} collective-permute-done((bf16[4,48,1536]{2,1,0:T(8,128)(2,1)}, bf16[4,48,1536]{2,1,0:T(8,128)(2,1)}, u32[]{:S(2)}, u32[]{:S(2)}) %collective-permute-start.24) | collective-permute-done | bytes 589856 | tf_op jit(solution)/shard_map/ppermute | solution.py:840
  206.7 3.2 %add_up.14 = (bf16[4,48,1920]{2,1,0:T(8,128)(2,1)}, bf16[2,48,1536]{2,1,0:T(8,128)(2,1)}, f32[8,128]{1,0:T(8,128)}) custom-call(s32[2]{0:T(128)} %pad_add_fusion.place.refs_0_, bf16[16,48,1920]{2,1,0:T(8,128)(2,1)} %get-tuple-element.142.refs_4_.refs_1_, bf16[16,48,1920]{2,1,0:T(8,128)(2,1)} %collective-permute-done.21.refs_2_, ...), custom_call_target="tpu_custom_call" | custom-call | flops 1000 | bytes 1000 | tf_op jit(solution)/shard_map/add_up/pallas_call | solution.py:67
  210.9 9.6 %proj_grads.1 = (bf16[16,48,1280]{2,1,0:T(8,128)(2,1)}, bf16[16,48,1280]{2,1,0:T(8,128)(2,1)}) custom-call(s32[2]{0:T(128)} %pad_add_fusion.place.refs_0_, bf16[768,1024]{1,0:T(8,128)(2,1)} %get-tuple-element.157.refs_1_, f32[6,8,768]{2,1,0:T(8,128)} %get-tuple-element.158.refs_2_, f32[8,3072]{1,0:T(8,128)} %get-tuple-element.159.refs_3_, ...), custom_call_target="tpu_custom_call" | custom-call | flops 4000000000 | bytes 1048576 | tf_op jit(solution)/shard_map/proj_grads/pallas_call | solution.py:67
  222.0 3.6 %add_up.15 = (bf16[2,48,1920]{2,1,0:T(8,128)(2,1)}, f32[2,48,1920]{2,1,0:T(8,128)}, bf16[1,48,1536]{2,1,0:T(8,128)(2,1)}, f32[1,48,1536]{2,1,0:T(8,128)}, f32[8,128]{1,0:T(8,128)}) custom-call(s32[2]{0:T(128)} %pad_add_fusion.place.refs_0_, bf16[16,48,1920]{2,1,0:T(8,128)(2,1)} %get-tuple-element.142.refs_4_.refs_1_, ...), custom_call_target="tpu_custom_call" | custom-call | flops 1000 | bytes 1000 | tf_op jit(solution)/shard_map/add_up/pallas_call | solution.py:67
  226.0 2.7 add_up.16
  230.1 2.5 collective-permute-start.30
  233.5 9.7 %input_back_0.1 = (f32[1024,768]{1,0:T(8,128)}, f32[16,128]{1,0:T(8,128)}) custom-call(f32[1024,768]{1,0:T(8,128)} %get-tuple-element.132.refs_0_, bf16[1024,768]{1,0:T(8,128)(2,1)} %get-tuple-element.154.refs_8_.refs_4_.refs_1_, bf16[1024,768]{1,0:T(8,128)(2,1)} %get-tuple-element.155.refs_5_.refs_2_, bf16[1024,768]{1,0:T(8,128)(2,1)} %get-tuple-element.156.refs_6_.refs_3_, ...), custom_call_target="tpu_custom_call" | custom-call | flops 10000000000 | bytes 1048576 | tf_op jit(solution)/shard_map/input_back_0/pallas_call | solution.py:67
  251.8 4.4 %collective-permute-done.32.refs_1_.refs_4_ = bf16[1,48,1920]{2,1,0:T(8,128)(2,1)S(1)} collective-permute-done((bf16[1,48,1920]{2,1,0:T(8,128)(2,1)S(1)}, bf16[1,48,1920]{2,1,0:T(8,128)(2,1)S(1)}, u32[]{:S(2)}, u32[]{:S(2)}) %collective-permute-start.32) | collective-permute-done | bytes 184352 | tf_op jit(solution)/shard_map/ppermute | solution.py:840
  256.8 2.5 collective-permute-start.33
  259.3 5.5 %collective-permute-done.33.refs_2_ = bf16[2,48,1280]{2,1,0:T(8,128)(2,1)S(1)} collective-permute-done((bf16[2,48,1280]{2,1,0:T(8,128)(2,1)S(1)}, bf16[2,48,1280]{2,1,0:T(8,128)(2,1)S(1)}, u32[]{:S(2)}, u32[]{:S(2)}) %collective-permute-start.33) | collective-permute-done | bytes 245792 | tf_op jit(solution)/shard_map/ppermute | solution.py:840
  269.9 3.7 %collective-permute-done.34.refs_2_ = bf16[1,48,1280]{2,1,0:T(8,128)(2,1)S(1)} collective-permute-done((bf16[1,48,1280]{2,1,0:T(8,128)(2,1)S(1)}, bf16[1,48,1280]{2,1,0:T(8,128)(2,1)S(1)}, u32[]{:S(2)}, u32[]{:S(2)}) %collective-permute-start.34) | collective-permute-done | bytes 122912 | tf_op jit(solution)/shard_map/ppermute | solution.py:840
  (108 shorter events, 48.0 us)
Async XLA Ops:
  7.8 7.8 %collective-permute-start.1 = (bf16[1,48,1664]{2,1,0:T(8,128)(2,1)S(1)}, bf16[1,48,1664]{2,1,0:T(8,128)(2,1)S(1)}, u32[]{:S(2)}, u32[]{:S(2)}) collective-permute-start(bf16[1,48,1664]{2,1,0:T(8,128)(2,1)S(1)} %fusion.4), channel_id=1, source_target_pairs={{0,16},{1,9},{2,18},{3,11},{4,20},{5,13},{6,22},{7,15},{8,24},{9,1... | collective-permute-start | bytes 479240 | tf_op jit(solution)/shard_map/ppermute | solution.py:840
  15.6 10.8 %collective-permute-start.2 = (bf16[2,48,1664]{2,1,0:T(8,128)(2,1)S(1)}, bf16[2,48,1664]{2,1,0:T(8,128)(2,1)S(1)}, u32[]{:S(2)}, u32[]{:S(2)}) collective-permute-start(bf16[2,48,1664]{2,1,0:T(8,128)(2,1)S(1)} %pad_maximum_fusion.1), channel_id=1, source_target_pairs={{0,8},{1,17},{2,10},{3,19},{4,12},{5,21},{6,14},{7,23},{8,0},{9,25... | collective-permute-start | bytes 958472 | tf_op jit(solution)/shard_map/ppermute | solution.py:840
  26.4 14.9 %collective-permute-start.4 = (bf16[4,48,1664]{2,1,0:T(8,128)(2,1)S(1)}, bf16[4,48,1664]{2,1,0:T(8,128)(2,1)S(1)}, u32[]{:S(2)}, u32[]{:S(2)}) collective-permute-start(bf16[4,48,1664]{2,1,0:T(8,128)(2,1)S(1)} %constant_dynamic-update-slice_fusion.8.refs_0_), channel_id=1, source_target_pairs={{0,2},{1,5},{2,0},{3,7},{4,6},{5,1},{6,4},{7,3},{8,10},{9,13},{10,... | collective-permute-start | bytes 1916936 | tf_op jit(solution)/shard_map/ppermute | solution.py:840
  28.2 16.1 %collective-permute-start.8 = (bf16[1,48,3072]{2,1,0:T(8,128)(2,1)S(1)}, bf16[1,48,3072]{2,1,0:T(8,128)(2,1)S(1)}, u32[]{:S(2)}, u32[]{:S(2)}) collective-permute-start(bf16[1,48,3072]{2,1,0:T(8,128)(2,1)S(1)} %fusion.2), channel_id=1, source_target_pairs={{0,24},{1,25},{2,26},{3,27},{4,28},{5,29},{6,30},{7,31},{8,16},{9,... | collective-permute-start | bytes 884744 | tf_op jit(solution)/shard_map/ppermute | solution.py:840
  31.1 13.9 %collective-permute-start.7 = (bf16[1,48,3072]{2,1,0:T(8,128)(2,1)S(1)}, bf16[1,48,3072]{2,1,0:T(8,128)(2,1)S(1)}, u32[]{:S(2)}, u32[]{:S(2)}) collective-permute-start(bf16[1,48,3072]{2,1,0:T(8,128)(2,1)S(1)} %fusion.2), channel_id=1, source_target_pairs={{0,8},{1,17},{2,10},{3,19},{4,12},{5,21},{6,14},{7,23},{8,0},{9,25... | collective-permute-start | bytes 884744 | tf_op jit(solution)/shard_map/ppermute | solution.py:840
  31.1 22.6 %collective-permute-start.6 = (bf16[1,48,3072]{2,1,0:T(8,128)(2,1)S(1)}, bf16[1,48,3072]{2,1,0:T(8,128)(2,1)S(1)}, u32[]{:S(2)}, u32[]{:S(2)}) collective-permute-start(bf16[1,48,3072]{2,1,0:T(8,128)(2,1)S(1)} %fusion.2), channel_id=1, source_target_pairs={{0,16},{1,9},{2,18},{3,11},{4,20},{5,13},{6,22},{7,15},{8,24},{9,1... | collective-permute-start | bytes 884744 | tf_op jit(solution)/shard_map/ppermute | solution.py:840
  32.6 21.9 %collective-permute-start.3 = (bf16[4,48,1664]{2,1,0:T(8,128)(2,1)S(1)}, bf16[4,48,1664]{2,1,0:T(8,128)(2,1)S(1)}, u32[]{:S(2)}, u32[]{:S(2)}) collective-permute-start(bf16[4,48,1664]{2,1,0:T(8,128)(2,1)S(1)} %constant_dynamic-update-slice_fusion.8.refs_0_), channel_id=1, source_target_pairs={{0,4},{1,3},{2,6},{3,1},{4,0},{5,7},{6,2},{7,5},{8,12},{9,11},{10,... | collective-permute-start | bytes 1916936 | tf_op jit(solution)/shard_map/ppermute | solution.py:840
  41.4 13.1 %collective-permute-start.5 = (bf16[4,48,1664]{2,1,0:T(8,128)(2,1)S(1)}, bf16[4,48,1664]{2,1,0:T(8,128)(2,1)}, u32[]{:S(2)}, u32[]{:S(2)}) collective-permute-start(bf16[4,48,1664]{2,1,0:T(8,128)(2,1)S(1)} %collective-permute-done.4.refs_1_), channel_id=1, source_target_pairs={{0,4},{1,3},{2,6},{3,1},{4,0},{5,7},{6,2},{7,5},{8,12},{9,11},{10,... | collective-permute-start | bytes 1916936 | tf_op jit(solution)/shard_map/ppermute | solution.py:840
  53.9 4.0 %collective-permute-start.12 = (bf16[4,48,1664]{2,1,0:T(8,128)(2,1)S(1)}, bf16[4,48,1664]{2,1,0:T(8,128)(2,1)}, u32[]{:S(2)}, u32[]{:S(2)}) collective-permute-start(bf16[4,48,1664]{2,1,0:T(8,128)(2,1)S(1)} %collective-permute-done.4.refs_1_), channel_id=1, source_target_pairs={{0,1},{1,0},{2,3},{3,2},{4,5},{5,4},{6,7},{7,6},{8,9},{9,8},{10,11... | collective-permute-start | bytes 1916936 | tf_op jit(solution)/shard_map/ppermute | solution.py:840
  54.4 5.0 %collective-permute-start.13 = (bf16[4,48,1664]{2,1,0:T(8,128)(2,1)S(1)}, bf16[4,48,1664]{2,1,0:T(8,128)(2,1)}, u32[]{:S(2)}, u32[]{:S(2)}) collective-permute-start(bf16[4,48,1664]{2,1,0:T(8,128)(2,1)S(1)} %collective-permute-done.3.refs_2_), channel_id=1, source_target_pairs={{0,1},{1,0},{2,3},{3,2},{4,5},{5,4},{6,7},{7,6},{8,9},{9,8},{10,11... | collective-permute-start | bytes 1916936 | tf_op jit(solution)/shard_map/ppermute | solution.py:840
  54.6 4.9 %collective-permute-start.14 = (bf16[4,48,1664]{2,1,0:T(8,128)(2,1)}, bf16[4,48,1664]{2,1,0:T(8,128)(2,1)}, u32[]{:S(2)}, u32[]{:S(2)}) collective-permute-start(bf16[4,48,1664]{2,1,0:T(8,128)(2,1)} %collective-permute-done.5.refs_3_), channel_id=1, source_target_pairs={{0,1},{1,0},{2,3},{3,2},{4,5},{5,4},{6,7},{7,6},{8,9},{9,8},{10,11... | collective-permute-start | bytes 1916936 | tf_op jit(solution)/shard_map/ppermute | solution.py:840
  55.6 46.6 %collective-permute-start.16 = (bf16[4,48,3072]{2,1,0:T(8,128)(2,1)S(1)}, bf16[4,48,3072]{2,1,0:T(8,128)(2,1)}, u32[]{:S(2)}, u32[]{:S(2)}) collective-permute-start(bf16[4,48,3072]{2,1,0:T(8,128)(2,1)S(1)} %pad_maximum_fusion.refs_0_), channel_id=1, source_target_pairs={{0,1},{1,0},{2,3},{3,2},{4,5},{5,4},{6,7},{7,6},{8,9},{9,8},{10,11... | collective-permute-start | bytes 3538952 | tf_op jit(solution)/shard_map/ppermute | solution.py:840
  56.1 29.4 %collective-permute-start.10 = (bf16[4,48,3072]{2,1,0:T(8,128)(2,1)S(1)}, bf16[4,48,3072]{2,1,0:T(8,128)(2,1)}, u32[]{:S(2)}, u32[]{:S(2)}) collective-permute-start(bf16[4,48,3072]{2,1,0:T(8,128)(2,1)S(1)} %pad_maximum_fusion.refs_0_), channel_id=1, source_target_pairs={{0,4},{1,3},{2,6},{3,1},{4,0},{5,7},{6,2},{7,5},{8,12},{9,11},{10,... | collective-permute-start | bytes 3538952 | tf_op jit(solution)/shard_map/ppermute | solution.py:840
  57.9 27.6 %collective-permute-start.9 = (bf16[4,48,3072]{2,1,0:T(8,128)(2,1)S(1)}, bf16[4,48,3072]{2,1,0:T(8,128)(2,1)}, u32[]{:S(2)}, u32[]{:S(2)}) collective-permute-start(bf16[4,48,3072]{2,1,0:T(8,128)(2,1)S(1)} %pad_maximum_fusion.refs_0_), channel_id=1, source_target_pairs={{0,2},{1,5},{2,0},{3,7},{4,6},{5,1},{6,4},{7,3},{8,10},{9,13},{10,... | collective-permute-start | bytes 3538952 | tf_op jit(solution)/shard_map/ppermute | solution.py:840
  85.5 16.7 %collective-permute-start.17 = (bf16[4,48,3072]{2,1,0:T(8,128)(2,1)}, bf16[4,48,3072]{2,1,0:T(8,128)(2,1)}, u32[]{:S(2)}, u32[]{:S(2)}) collective-permute-start(bf16[4,48,3072]{2,1,0:T(8,128)(2,1)} %collective-permute-done.9.refs_1_), channel_id=1, source_target_pairs={{0,1},{1,0},{2,3},{3,2},{4,5},{5,4},{6,7},{7,6},{8,9},{9,8},{10,11... | collective-permute-start | bytes 3538952 | tf_op jit(solution)/shard_map/ppermute | solution.py:840
  85.6 16.6 %collective-permute-start.15 = (bf16[4,48,3072]{2,1,0:T(8,128)(2,1)}, bf16[4,48,3072]{2,1,0:T(8,128)(2,1)}, u32[]{:S(2)}, u32[]{:S(2)}) collective-permute-start(bf16[4,48,3072]{2,1,0:T(8,128)(2,1)} %collective-permute-done.9.refs_1_), channel_id=1, source_target_pairs={{0,4},{1,3},{2,6},{3,1},{4,0},{5,7},{6,2},{7,5},{8,12},{9,11},{10,... | collective-permute-start | bytes 3538952 | tf_op jit(solution)/shard_map/ppermute | solution.py:840
  86.2 16.0 %collective-permute-start.18 = (bf16[4,48,3072]{2,1,0:T(8,128)(2,1)}, bf16[4,48,3072]{2,1,0:T(8,128)(2,1)}, u32[]{:S(2)}, u32[]{:S(2)}) collective-permute-start(bf16[4,48,3072]{2,1,0:T(8,128)(2,1)} %collective-permute-done.10.refs_2_), channel_id=1, source_target_pairs={{0,1},{1,0},{2,3},{3,2},{4,5},{5,4},{6,7},{7,6},{8,9},{9,8},{10,11... | collective-permute-start | bytes 3538952 | tf_op jit(solution)/shard_map/ppermute | solution.py:840
  154.3 11.2 %collective-permute-start.20 = (bf16[16,48,1536]{2,1,0:T(8,128)(2,1)}, bf16[16,48,1536]{2,1,0:T(8,128)(2,1)}, u32[]{:S(2)}, u32[]{:S(2)}) collective-permute-start(bf16[16,48,1536]{2,1,0:T(8,128)(2,1)} %get-tuple-element.136), channel_id=1, source_target_pairs={{0,1},{1,0},{2,3},{3,2},{4,5},{5,4},{6,7},{7,6},{8,9},{9,8},{10,11... | collective-permute-start | bytes 7077896 | tf_op jit(solution)/shard_map/ppermute | solution.py:840
  168.5 9.3 %collective-permute-start.21 = (bf16[16,48,1920]{2,1,0:T(8,128)(2,1)}, bf16[16,48,1920]{2,1,0:T(8,128)(2,1)}, u32[]{:S(2)}, u32[]{:S(2)}) collective-permute-start(bf16[16,48,1920]{2,1,0:T(8,128)(2,1)} %get-tuple-element.147), channel_id=1, source_target_pairs={{0,1},{1,0},{2,3},{3,2},{4,5},{5,4},{6,7},{7,6},{8,9},{9,8},{10,11... | collective-permute-start | bytes 8847368 | tf_op jit(solution)/shard_map/ppermute | solution.py:840
  168.9 22.2 %collective-permute-start.22 = (bf16[8,48,1536]{2,1,0:T(8,128)(2,1)}, bf16[8,48,1536]{2,1,0:T(8,128)(2,1)}, u32[]{:S(2)}, u32[]{:S(2)}) collective-permute-start(bf16[8,48,1536]{2,1,0:T(8,128)(2,1)} %get-tuple-element.152), channel_id=1, source_target_pairs={{0,4},{1,3},{2,6},{3,1},{4,0},{5,7},{6,2},{7,5},{8,12},{9,11},{10,... | collective-permute-start | bytes 3538952 | tf_op jit(solution)/shard_map/ppermute | solution.py:840
  181.1 25.6 %collective-permute-start.23 = (bf16[8,48,1920]{2,1,0:T(8,128)(2,1)}, bf16[8,48,1920]{2,1,0:T(8,128)(2,1)}, u32[]{:S(2)}, u32[]{:S(2)}) collective-permute-start(bf16[8,48,1920]{2,1,0:T(8,128)(2,1)} %get-tuple-element.160), channel_id=1, source_target_pairs={{0,4},{1,3},{2,6},{3,1},{4,0},{5,7},{6,2},{7,5},{8,12},{9,11},{10,... | collective-permute-start | bytes 4423688 | tf_op jit(solution)/shard_map/ppermute | solution.py:840
  193.6 13.1 %collective-permute-start.24 = (bf16[4,48,1536]{2,1,0:T(8,128)(2,1)}, bf16[4,48,1536]{2,1,0:T(8,128)(2,1)}, u32[]{:S(2)}, u32[]{:S(2)}) collective-permute-start(bf16[4,48,1536]{2,1,0:T(8,128)(2,1)} %get-tuple-element.161), channel_id=1, source_target_pairs={{0,2},{1,5},{2,0},{3,7},{4,6},{5,1},{6,4},{7,3},{8,10},{9,13},{10,... | collective-permute-start | bytes 1769480 | tf_op jit(solution)/shard_map/ppermute | solution.py:840
  209.9 11.8 %collective-permute-start.25 = (bf16[4,48,1920]{2,1,0:T(8,128)(2,1)}, bf16[4,48,1920]{2,1,0:T(8,128)(2,1)}, u32[]{:S(2)}, u32[]{:S(2)}) collective-permute-start(bf16[4,48,1920]{2,1,0:T(8,128)(2,1)} %get-tuple-element.165), channel_id=1, source_target_pairs={{0,2},{1,5},{2,0},{3,7},{4,6},{5,1},{6,4},{7,3},{8,10},{9,13},{10,... | collective-permute-start | bytes 2211848 | tf_op jit(solution)/shard_map/ppermute | solution.py:840
  210.9 9.6 %collective-permute-start.26 = (bf16[2,48,1536]{2,1,0:T(8,128)(2,1)}, bf16[2,48,1536]{2,1,0:T(8,128)(2,1)S(1)}, u32[]{:S(2)}, u32[]{:S(2)}) collective-permute-start(bf16[2,48,1536]{2,1,0:T(8,128)(2,1)} %get-tuple-element.166), channel_id=1, source_target_pairs={{0,8},{1,17},{2,10},{3,19},{4,12},{5,21},{6,14},{7,23},{8,0},{9,25... | collective-permute-start | bytes 884744 | tf_op jit(solution)/shard_map/ppermute | solution.py:840
  221.7 4.3 %collective-permute-start.27 = (bf16[16,48,1280]{2,1,0:T(8,128)(2,1)}, bf16[16,48,1280]{2,1,0:T(8,128)(2,1)}, u32[]{:S(2)}, u32[]{:S(2)}) collective-permute-start(bf16[16,48,1280]{2,1,0:T(8,128)(2,1)} %gate.3), channel_id=1, source_target_pairs={{0,1},{1,0},{2,3},{3,2},{4,5},{5,4},{6,7},{7,6},{8,9},{9,8},{10,11... | collective-permute-start | bytes 5898248 | tf_op jit(solution)/shard_map/ppermute | solution.py:840
  228.7 15.3 %collective-permute-start.28 = (bf16[8,48,1280]{2,1,0:T(8,128)(2,1)}, bf16[8,48,1280]{2,1,0:T(8,128)(2,1)}, u32[]{:S(2)}, u32[]{:S(2)}) collective-permute-start(bf16[8,48,1280]{2,1,0:T(8,128)(2,1)} %get-tuple-element.170), channel_id=1, source_target_pairs={{0,4},{1,3},{2,6},{3,1},{4,0},{5,7},{6,2},{7,5},{8,12},{9,11},{10,... | collective-permute-start | bytes 2949128 | tf_op jit(solution)/shard_map/ppermute | solution.py:840
  230.1 13.1 %collective-permute-start.30 = (bf16[1,48,1536]{2,1,0:T(8,128)(2,1)}, bf16[1,48,1536]{2,1,0:T(8,128)(2,1)}, u32[]{:S(2)}, u32[]{:S(2)}) collective-permute-start(bf16[1,48,1536]{2,1,0:T(8,128)(2,1)} %get-tuple-element.172), channel_id=1, source_target_pairs={{0,16},{1,9},{2,18},{3,11},{4,20},{5,13},{6,22},{7,15},{8,24},{9,1... | collective-permute-start | bytes 442376 | tf_op jit(solution)/shard_map/ppermute | solution.py:840
  232.6 11.4 %collective-permute-start.29 = (bf16[2,48,1920]{2,1,0:T(8,128)(2,1)}, bf16[2,48,1920]{2,1,0:T(8,128)(2,1)S(1)}, u32[]{:S(2)}, u32[]{:S(2)}) collective-permute-start(bf16[2,48,1920]{2,1,0:T(8,128)(2,1)} %get-tuple-element.171), channel_id=1, source_target_pairs={{0,8},{1,17},{2,10},{3,19},{4,12},{5,21},{6,14},{7,23},{8,0},{9,25... | collective-permute-start | bytes 1105928 | tf_op jit(solution)/shard_map/ppermute | solution.py:840
  246.7 9.5 %collective-permute-start.31 = (bf16[4,48,1280]{2,1,0:T(8,128)(2,1)S(1)}, bf16[4,48,1280]{2,1,0:T(8,128)(2,1)S(1)}, u32[]{:S(2)}, u32[]{:S(2)}) collective-permute-start(bf16[4,48,1280]{2,1,0:T(8,128)(2,1)S(1)} %get-tuple-element.175), channel_id=1, source_target_pairs={{0,2},{1,5},{2,0},{3,7},{4,6},{5,1},{6,4},{7,3},{8,10},{9,13},{10,... | collective-permute-start | bytes 1474568 | tf_op jit(solution)/shard_map/ppermute | solution.py:840
  249.6 6.6 %collective-permute-start.32 = (bf16[1,48,1920]{2,1,0:T(8,128)(2,1)S(1)}, bf16[1,48,1920]{2,1,0:T(8,128)(2,1)S(1)}, u32[]{:S(2)}, u32[]{:S(2)}) collective-permute-start(bf16[1,48,1920]{2,1,0:T(8,128)(2,1)S(1)} %get-tuple-element.179), channel_id=1, source_target_pairs={{0,16},{1,9},{2,18},{3,11},{4,20},{5,13},{6,22},{7,15},{8,24},{9,1... | collective-permute-start | bytes 552968 | tf_op jit(solution)/shard_map/ppermute | solution.py:840
  256.8 7.9 %collective-permute-start.33 = (bf16[2,48,1280]{2,1,0:T(8,128)(2,1)S(1)}, bf16[2,48,1280]{2,1,0:T(8,128)(2,1)S(1)}, u32[]{:S(2)}, u32[]{:S(2)}) collective-permute-start(bf16[2,48,1280]{2,1,0:T(8,128)(2,1)S(1)} %get-tuple-element.182), channel_id=1, source_target_pairs={{0,8},{1,17},{2,10},{3,19},{4,12},{5,21},{6,14},{7,23},{8,0},{9,25... | collective-permute-start | bytes 737288 | tf_op jit(solution)/shard_map/ppermute | solution.py:840
  267.1 6.6 %collective-permute-start.34 = (bf16[1,48,1280]{2,1,0:T(8,128)(2,1)S(1)}, bf16[1,48,1280]{2,1,0:T(8,128)(2,1)S(1)}, u32[]{:S(2)}, u32[]{:S(2)}) collective-permute-start(bf16[1,48,1280]{2,1,0:T(8,128)(2,1)S(1)} %get-tuple-element.186), channel_id=1, source_target_pairs={{0,16},{1,9},{2,18},{3,11},{4,20},{5,13},{6,22},{7,15},{8,24},{9,1... | collective-permute-start | bytes 368648 | tf_op jit(solution)/shard_map/ppermute | solution.py:840
  (15 other events, 97.0 us)

commit v3 on v2

--- a/solution.py
+++ b/solution.py
@@ -251,7 +251,7 @@
 
 BLOCK = 256
 WIDTH = 768
-DOWN_STEPS = 8
+DOWN_STEPS = 4
 
 
 def out_weight_copies(proj_w, out_w, sem):

time: 279 us -> 278 us (level)
  no operation moved by 1% of the time
where the time goes in v3:
time: 278 us; the launch traced here: 277 us
  Pallas kernels  168 us (60%)
  waiting for transfers between devices  57.5 us (21%)
  starting transfers between devices  40 us (14%)
  local copies, waits for them, and re-layouts  8.9 us (3%)
    pallas_call x23, Pallas kernels, call(): return pl.pallas_call(body, in_specs=in_specs, **options)(*operands, *deps)  92.2 us
    ppermute x37, waiting for transfers between devices, move(): return lax.ppermute(v, AXES, [(i, i ^ masks[i & 1]) for i in range(SLABS)])  57.5 us
    pallas_call x1, Pallas kernels, feed_forward(): pl.pallas_call(functools.partial(ffn_kernel, meta, len(pieces), blocks),...  47.8 us
    ppermute x37, starting transfers between devices, move(): return lax.ppermute(v, AXES, [(i, i ^ masks[i & 1]) for i in range(SLABS)])  40 us
    pallas_call x1, Pallas kernels, attend(): pl.pallas_call(functools.partial(attend_kernel, meta, len(pieces)), grid=...  17.4 us
    pallas_call x1, Pallas kernels, inner_grads(): pl.pallas_call(inner_grads_kernel, grid=(steps + 1,), in_specs=[whole(D,...  11 us
  transfers between devices with their start and end apart: 37, of which 18 were waited for; matrix products, arithmetic and copies ran while one was open for 1% of the time, Pallas kernels for 38%

profile of v3, /device:TPU:0, one launch (start us, length us, event | category | flops | bytes accessed | tf_op | source)
XLA Modules:
  0.0 276.7 jit_solution(12811093052084093548)
XLA Ops:
  7.8 4.0 %collective-permute-start.1 = (bf16[1,48,1664]{2,1,0:T(8,128)(2,1)S(1)}, bf16[1,48,1664]{2,1,0:T(8,128)(2,1)S(1)}, u32[]{:S(2)}, u32[]{:S(2)}) collective-permute-start(bf16[1,48,1664]{2,1,0:T(8,128)(2,1)S(1)} %fusion.4), channel_id=1, source_target_pairs={{0,16},{1,9},{2,18},{3,11},{4,20},{5,13},{6,22},{7,15},{8,24},{9,1... | collective-permute-start | bytes 479240 | tf_op jit(solution)/shard_map/ppermute | solution.py:840
  11.9 3.7 %collective-permute-done.1 = bf16[1,48,1664]{2,1,0:T(8,128)(2,1)S(1)} collective-permute-done((bf16[1,48,1664]{2,1,0:T(8,128)(2,1)S(1)}, bf16[1,48,1664]{2,1,0:T(8,128)(2,1)S(1)}, u32[]{:S(2)}, u32[]{:S(2)}) %collective-permute-start.1) | collective-permute-done | bytes 159776 | tf_op jit(solution)/shard_map/ppermute | solution.py:840
  15.6 2.5 collective-permute-start.2
  18.1 8.3 %collective-permute-done.2 = bf16[2,48,1664]{2,1,0:T(8,128)(2,1)S(1)} collective-permute-done((bf16[2,48,1664]{2,1,0:T(8,128)(2,1)S(1)}, bf16[2,48,1664]{2,1,0:T(8,128)(2,1)S(1)}, u32[]{:S(2)}, u32[]{:S(2)}) %collective-permute-start.2) | collective-permute-done | bytes 319520 | tf_op jit(solution)/shard_map/ppermute | solution.py:840
  28.2 2.9 %collective-permute-start.8 = (bf16[1,48,3072]{2,1,0:T(8,128)(2,1)S(1)}, bf16[1,48,3072]{2,1,0:T(8,128)(2,1)S(1)}, u32[]{:S(2)}, u32[]{:S(2)}) collective-permute-start(bf16[1,48,3072]{2,1,0:T(8,128)(2,1)S(1)} %fusion.2), channel_id=1, source_target_pairs={{0,24},{1,25},{2,26},{3,27},{4,28},{5,29},{6,30},{7,31},{8,16},{9,... | collective-permute-start | bytes 884744 | tf_op jit(solution)/shard_map/ppermute | solution.py:840
  34.1 7.3 %collective-permute-done.4.refs_1_ = bf16[4,48,1664]{2,1,0:T(8,128)(2,1)S(1)} collective-permute-done((bf16[4,48,1664]{2,1,0:T(8,128)(2,1)S(1)}, bf16[4,48,1664]{2,1,0:T(8,128)(2,1)S(1)}, u32[]{:S(2)}, u32[]{:S(2)}) %collective-permute-start.4) | collective-permute-done | bytes 639008 | tf_op jit(solution)/shard_map/ppermute | solution.py:840
  41.4 2.9 %collective-permute-start.5 = (bf16[4,48,1664]{2,1,0:T(8,128)(2,1)S(1)}, bf16[4,48,1664]{2,1,0:T(8,128)(2,1)}, u32[]{:S(2)}, u32[]{:S(2)}) collective-permute-start(bf16[4,48,1664]{2,1,0:T(8,128)(2,1)S(1)} %collective-permute-done.4.refs_1_), channel_id=1, source_target_pairs={{0,4},{1,3},{2,6},{3,1},{4,0},{5,7},{6,2},{7,5},{8,12},{9,11},{10,... | collective-permute-start | bytes 1916936 | tf_op jit(solution)/shard_map/ppermute | solution.py:840
  45.0 8.7 %collective-permute-done.6 = bf16[1,48,3072]{2,1,0:T(8,128)(2,1)S(1)} collective-permute-done((bf16[1,48,3072]{2,1,0:T(8,128)(2,1)S(1)}, bf16[1,48,3072]{2,1,0:T(8,128)(2,1)S(1)}, u32[]{:S(2)}, u32[]{:S(2)}) %collective-permute-start.6) | collective-permute-done | bytes 294944 | tf_op jit(solution)/shard_map/ppermute | solution.py:840
  59.4 17.4 %attend.1 = (bf16[1024,2304]{1,0:T(8,128)(2,1)}, bf16[1024,768]{1,0:T(8,128)(2,1)}, f32[2,16,512]{2,1,0:T(8,128)}, bf16[768,3328]{1,0:T(8,128)(2,1)}, f32[16,768]{1,0:T(8,128)}) custom-call(s32[2]{0:T(128)} %pad_add_fusion.place.refs_0_, s32[2]{0:T(128)} %refs_0_.3, f32[1024,768]{1,0:T(8,128)} %refs_5_.1, bf16[4,48,1664]{2,1,0:T(8,128)(2,1)} %copy-done.7, ...), custom_call_target="tpu_custom_call" | custom-call | flops 17999998976 | bytes 20971520 | tf_op jit(solution)/shard_map/attend/pallas_call | solution.py:202
  78.5 7.0 %probs.1.refs_4_ = bf16[24,512,512]{2,1,0:T(8,128)(2,1)} custom-call(s32[2]{0:T(128)} %refs_0_.3, bf16[1024,2304]{1,0:T(8,128)(2,1)} %get-tuple-element.117.refs_1_.refs_2_.refs_0_, bf16[1024,2304]{1,0:T(8,128)(2,1)} %get-tuple-element.117.refs_1_.refs_2_.refs_0_, f32[2,16,512]{2,1,0:T(8,128)} %get-tuple-element.118.refs_3_), custom_call_target="tpu_custom_call" | custom-call | flops 8000000000 | bytes 1048576 | tf_op jit(solution)/shard_map/probs/pallas_call | solution.py:67
  86.7 13.2 %window.1 = (bf16[24,512,512]{2,1,0:T(8,128)(2,1)}, f32[1024,768]{1,0:T(8,128)}, f32[1024,128]{1,0:T(8,128)}, bf16[1024,768]{1,0:T(8,128)(2,1)}, bf16[768,1024]{...) custom-call(s32[2]{0:T(128)} %refs_0_.3, ...), custom_call_target="tpu_custom_call", output_to_operand_aliasing={{0}: (4, {})} | custom-call | flops 14000000000 | bytes 1048576 | tf_op jit(solution)/shard_map/window/pallas_call | solution.py:67
  99.9 2.3 collective-permute-done.15.refs_3_
  102.2 3.2 %collective-permute-done.19.refs_7_ = bf16[4,48,3072]{2,1,0:T(8,128)(2,1)} collective-permute-done((bf16[4,48,3072]{2,1,0:T(8,128)(2,1)}, bf16[4,48,3072]{2,1,0:T(8,128)(2,1)}, u32[]{:S(2)}, u32[]{:S(2)}) %collective-permute-start.19) | collective-permute-done | bytes 1179680 | tf_op jit(solution)/shard_map/ppermute | solution.py:840
  105.4 47.8 %feed_forward.1 = (f32[1024,768]{1,0:T(8,128)}, f32[1024,768]{1,0:T(8,128)}, bf16[1024,768]{1,0:T(8,128)(2,1)}, bf16[1024,3072]{1,0:T(8,128)(2,1)}, bf16[1024,76...) custom-call(s32[2]{0:T(128)} %pad_add_fusion.place.refs_0_, ...), custom_call_target="tpu_custom_call" | custom-call | flops 51999997952 | bytes 41943040 | tf_op jit(solution)/shard_map/feed_forward/pallas_call | solution.py:448
  153.4 11.0 %inner_grads.1 = (bf16[16,48,1920]{2,1,0:T(8,128)(2,1)}, bf16[16,48,1920]{2,1,0:T(8,128)(2,1)}) custom-call(bf16[768,1024]{1,0:T(8,128)(2,1)} %get-tuple-element.137.hid_t, bf16[1024,3072]{1,0:T(8,128)(2,1)} %get-tuple-element.138.ib_ref, s32[2]{0:T(128)} %pad_add_fusion.place.refs_0_, bf16[768,1024]{1,0:T(8,128)(2,1)} %get-tuple-element.139.att_in, ...), custom_call_target="tpu_custom_call" | custom-call | flops 4000000000 | bytes 1048576 | tf_op jit(solution)/shard_map/inner_grads/pallas_call | solution.py:518
  164.4 3.0 %add_up.11 = (bf16[8,48,1536]{2,1,0:T(8,128)(2,1)}, bf16[16,48,1920]{2,1,0:T(8,128)(2,1)}, f32[8,128]{1,0:T(8,128)}) custom-call(s32[2]{0:T(128)} %pad_add_fusion.place.refs_0_, bf16[16,48,1536]{2,1,0:T(8,128)(2,1)} %get-tuple-element.135.refs_1_.refs_4_.refs_5_, ...), custom_call_target="tpu_custom_call", output_to_operand_aliasing={{1}: (3, {})} | custom-call | flops 1000 | bytes 1000 | tf_op jit(solution)/shard_map/add_up/pallas_call | solution.py:67
  168.2 8.4 %attend_back_0.1 = (bf16[1024,768]{1,0:T(8,128)(2,1)}, bf16[1024,768]{1,0:T(8,128)(2,1)}, bf16[1024,768]{1,0:T(8,128)(2,1)}) custom-call(bf16[1024,2304]{1,0:T(8,128)(2,1)} %get-tuple-element.117.refs_1_.refs_2_.refs_0_, bf16[1024,2304]{1,0:T(8,128)(2,1)} %get-tuple-element.117.refs_1_.refs_2_.refs_0_, ...), custom_call_target="tpu_custom_call" | custom-call | flops 3000000000 | bytes 1048576 | tf_op jit(solution)/shard_map/attend_back_0/pallas_call | solution.py:67
  176.7 3.3 %add_up.12 = (bf16[8,48,1920]{2,1,0:T(8,128)(2,1)}, f32[8,128]{1,0:T(8,128)}) custom-call(s32[2]{0:T(128)} %pad_add_fusion.place.refs_0_, bf16[16,48,1920]{2,1,0:T(8,128)(2,1)} %get-tuple-element.142.refs_4_.refs_1_, bf16[16,48,1920]{2,1,0:T(8,128)(2,1)} %collective-permute-done.21.refs_2_, bf16[1024,768]{1,0:T(8,128)(2,1)} %get-tuple-element.144.refs_3_.refs_5_), custom_call_target="tpu_custom_call" | custom-call | flops 1000 | bytes 1000 | tf_op jit(solution)/shard_map/add_up/pallas_call | solution.py:67
  181.5 8.4 %attend_back_4.1 = (bf16[1024,768]{1,0:T(8,128)(2,1)}, bf16[1024,768]{1,0:T(8,128)(2,1)}, bf16[1024,768]{1,0:T(8,128)(2,1)}) custom-call(bf16[1024,2304]{1,0:T(8,128)(2,1)} %get-tuple-element.117.refs_1_.refs_2_.refs_0_, bf16[1024,2304]{1,0:T(8,128)(2,1)} %get-tuple-element.117.refs_1_.refs_2_.refs_0_, ...), custom_call_target="tpu_custom_call", output_to_operand_aliasing={{0}: (5, {}), {1}: (6, {}), {2}: (7, {})} | custom-call | flops 3000000000 | bytes 1048576 | tf_op jit(solution)/shard_map/attend_back_4/pallas_call | solution.py:67
  189.9 2.5 add_up.13
  193.4 8.5 %attend_back_8.1 = (bf16[1024,768]{1,0:T(8,128)(2,1)}, bf16[1024,768]{1,0:T(8,128)(2,1)}, bf16[1024,768]{1,0:T(8,128)(2,1)}) custom-call(bf16[1024,2304]{1,0:T(8,128)(2,1)} %get-tuple-element.117.refs_1_.refs_2_.refs_0_, bf16[1024,2304]{1,0:T(8,128)(2,1)} %get-tuple-element.117.refs_1_.refs_2_.refs_0_, ...), custom_call_target="tpu_custom_call", output_to_operand_aliasing={{0}: (5, {}), {1}: (6, {}), {2}: (7, {})} | custom-call | flops 3000000000 | bytes 1048576 | tf_op jit(solution)/shard_map/attend_back_8/pallas_call | solution.py:67
  201.9 3.6 %collective-permute-done.24.refs_7_.refs_8_ = bf16[4,48,1536]{2,1,0:T(8,128)(2,1)} collective-permute-done((bf16[4,48,1536]{2,1,0:T(8,128)(2,1)}, bf16[4,48,1536]{2,1,0:T(8,128)(2,1)}, u32[]{:S(2)}, u32[]{:S(2)}) %collective-permute-start.24) | collective-permute-done | bytes 589856 | tf_op jit(solution)/shard_map/ppermute | solution.py:840
  205.5 3.2 %add_up.14 = (bf16[4,48,1920]{2,1,0:T(8,128)(2,1)}, bf16[2,48,1536]{2,1,0:T(8,128)(2,1)}, f32[8,128]{1,0:T(8,128)}) custom-call(s32[2]{0:T(128)} %pad_add_fusion.place.refs_0_, bf16[16,48,1920]{2,1,0:T(8,128)(2,1)} %get-tuple-element.142.refs_4_.refs_1_, bf16[16,48,1920]{2,1,0:T(8,128)(2,1)} %collective-permute-done.21.refs_2_, ...), custom_call_target="tpu_custom_call" | custom-call | flops 1000 | bytes 1000 | tf_op jit(solution)/shard_map/add_up/pallas_call | solution.py:67
  209.8 9.6 %proj_grads.1 = (bf16[16,48,1280]{2,1,0:T(8,128)(2,1)}, bf16[16,48,1280]{2,1,0:T(8,128)(2,1)}) custom-call(s32[2]{0:T(128)} %pad_add_fusion.place.refs_0_, bf16[768,1024]{1,0:T(8,128)(2,1)} %get-tuple-element.157.refs_1_, f32[6,8,768]{2,1,0:T(8,128)} %get-tuple-element.158.refs_2_, f32[8,3072]{1,0:T(8,128)} %get-tuple-element.159.refs_3_, ...), custom_call_target="tpu_custom_call" | custom-call | flops 4000000000 | bytes 1048576 | tf_op jit(solution)/shard_map/proj_grads/pallas_call | solution.py:67
  220.8 3.6 %add_up.15 = (bf16[2,48,1920]{2,1,0:T(8,128)(2,1)}, f32[2,48,1920]{2,1,0:T(8,128)}, bf16[1,48,1536]{2,1,0:T(8,128)(2,1)}, f32[1,48,1536]{2,1,0:T(8,128)}, f32[8,128]{1,0:T(8,128)}) custom-call(s32[2]{0:T(128)} %pad_add_fusion.place.refs_0_, bf16[16,48,1920]{2,1,0:T(8,128)(2,1)} %get-tuple-element.142.refs_4_.refs_1_, ...), custom_call_target="tpu_custom_call" | custom-call | flops 1000 | bytes 1000 | tf_op jit(solution)/shard_map/add_up/pallas_call | solution.py:67
  224.9 2.7 add_up.16
  228.9 2.6 collective-permute-start.30
  232.3 9.7 %input_back_0.1 = (f32[1024,768]{1,0:T(8,128)}, f32[16,128]{1,0:T(8,128)}) custom-call(f32[1024,768]{1,0:T(8,128)} %get-tuple-element.132.refs_0_, bf16[1024,768]{1,0:T(8,128)(2,1)} %get-tuple-element.154.refs_8_.refs_4_.refs_1_, bf16[1024,768]{1,0:T(8,128)(2,1)} %get-tuple-element.155.refs_5_.refs_2_, bf16[1024,768]{1,0:T(8,128)(2,1)} %get-tuple-element.156.refs_6_.refs_3_, ...), custom_call_target="tpu_custom_call" | custom-call | flops 10000000000 | bytes 1048576 | tf_op jit(solution)/shard_map/input_back_0/pallas_call | solution.py:67
  250.7 4.3 %collective-permute-done.32.refs_1_.refs_4_ = bf16[1,48,1920]{2,1,0:T(8,128)(2,1)S(1)} collective-permute-done((bf16[1,48,1920]{2,1,0:T(8,128)(2,1)S(1)}, bf16[1,48,1920]{2,1,0:T(8,128)(2,1)S(1)}, u32[]{:S(2)}, u32[]{:S(2)}) %collective-permute-start.32) | collective-permute-done | bytes 184352 | tf_op jit(solution)/shard_map/ppermute | solution.py:840
  255.7 2.5 collective-permute-start.33
  258.2 5.5 %collective-permute-done.33.refs_2_ = bf16[2,48,1280]{2,1,0:T(8,128)(2,1)S(1)} collective-permute-done((bf16[2,48,1280]{2,1,0:T(8,128)(2,1)S(1)}, bf16[2,48,1280]{2,1,0:T(8,128)(2,1)S(1)}, u32[]{:S(2)}, u32[]{:S(2)}) %collective-permute-start.33) | collective-permute-done | bytes 245792 | tf_op jit(solution)/shard_map/ppermute | solution.py:840
  268.7 4.2 %collective-permute-done.34.refs_2_ = bf16[1,48,1280]{2,1,0:T(8,128)(2,1)S(1)} collective-permute-done((bf16[1,48,1280]{2,1,0:T(8,128)(2,1)S(1)}, bf16[1,48,1280]{2,1,0:T(8,128)(2,1)S(1)}, u32[]{:S(2)}, u32[]{:S(2)}) %collective-permute-start.34) | collective-permute-done | bytes 122912 | tf_op jit(solution)/shard_map/ppermute | solution.py:840
  (108 shorter events, 47.8 us)
Async XLA Ops:
  7.8 7.8 %collective-permute-start.1 = (bf16[1,48,1664]{2,1,0:T(8,128)(2,1)S(1)}, bf16[1,48,1664]{2,1,0:T(8,128)(2,1)S(1)}, u32[]{:S(2)}, u32[]{:S(2)}) collective-permute-start(bf16[1,48,1664]{2,1,0:T(8,128)(2,1)S(1)} %fusion.4), channel_id=1, source_target_pairs={{0,16},{1,9},{2,18},{3,11},{4,20},{5,13},{6,22},{7,15},{8,24},{9,1... | collective-permute-start | bytes 479240 | tf_op jit(solution)/shard_map/ppermute | solution.py:840
  15.6 10.8 %collective-permute-start.2 = (bf16[2,48,1664]{2,1,0:T(8,128)(2,1)S(1)}, bf16[2,48,1664]{2,1,0:T(8,128)(2,1)S(1)}, u32[]{:S(2)}, u32[]{:S(2)}) collective-permute-start(bf16[2,48,1664]{2,1,0:T(8,128)(2,1)S(1)} %pad_maximum_fusion.1), channel_id=1, source_target_pairs={{0,8},{1,17},{2,10},{3,19},{4,12},{5,21},{6,14},{7,23},{8,0},{9,25... | collective-permute-start | bytes 958472 | tf_op jit(solution)/shard_map/ppermute | solution.py:840
  26.4 14.9 %collective-permute-start.4 = (bf16[4,48,1664]{2,1,0:T(8,128)(2,1)S(1)}, bf16[4,48,1664]{2,1,0:T(8,128)(2,1)S(1)}, u32[]{:S(2)}, u32[]{:S(2)}) collective-permute-start(bf16[4,48,1664]{2,1,0:T(8,128)(2,1)S(1)} %constant_dynamic-update-slice_fusion.8.refs_0_), channel_id=1, source_target_pairs={{0,2},{1,5},{2,0},{3,7},{4,6},{5,1},{6,4},{7,3},{8,10},{9,13},{10,... | collective-permute-start | bytes 1916936 | tf_op jit(solution)/shard_map/ppermute | solution.py:840
  28.2 16.1 %collective-permute-start.8 = (bf16[1,48,3072]{2,1,0:T(8,128)(2,1)S(1)}, bf16[1,48,3072]{2,1,0:T(8,128)(2,1)S(1)}, u32[]{:S(2)}, u32[]{:S(2)}) collective-permute-start(bf16[1,48,3072]{2,1,0:T(8,128)(2,1)S(1)} %fusion.2), channel_id=1, source_target_pairs={{0,24},{1,25},{2,26},{3,27},{4,28},{5,29},{6,30},{7,31},{8,16},{9,... | collective-permute-start | bytes 884744 | tf_op jit(solution)/shard_map/ppermute | solution.py:840
  31.1 13.9 %collective-permute-start.7 = (bf16[1,48,3072]{2,1,0:T(8,128)(2,1)S(1)}, bf16[1,48,3072]{2,1,0:T(8,128)(2,1)S(1)}, u32[]{:S(2)}, u32[]{:S(2)}) collective-permute-start(bf16[1,48,3072]{2,1,0:T(8,128)(2,1)S(1)} %fusion.2), channel_id=1, source_target_pairs={{0,8},{1,17},{2,10},{3,19},{4,12},{5,21},{6,14},{7,23},{8,0},{9,25... | collective-permute-start | bytes 884744 | tf_op jit(solution)/shard_map/ppermute | solution.py:840
  31.1 22.6 %collective-permute-start.6 = (bf16[1,48,3072]{2,1,0:T(8,128)(2,1)S(1)}, bf16[1,48,3072]{2,1,0:T(8,128)(2,1)S(1)}, u32[]{:S(2)}, u32[]{:S(2)}) collective-permute-start(bf16[1,48,3072]{2,1,0:T(8,128)(2,1)S(1)} %fusion.2), channel_id=1, source_target_pairs={{0,16},{1,9},{2,18},{3,11},{4,20},{5,13},{6,22},{7,15},{8,24},{9,1... | collective-permute-start | bytes 884744 | tf_op jit(solution)/shard_map/ppermute | solution.py:840
  32.6 21.9 %collective-permute-start.3 = (bf16[4,48,1664]{2,1,0:T(8,128)(2,1)S(1)}, bf16[4,48,1664]{2,1,0:T(8,128)(2,1)S(1)}, u32[]{:S(2)}, u32[]{:S(2)}) collective-permute-start(bf16[4,48,1664]{2,1,0:T(8,128)(2,1)S(1)} %constant_dynamic-update-slice_fusion.8.refs_0_), channel_id=1, source_target_pairs={{0,4},{1,3},{2,6},{3,1},{4,0},{5,7},{6,2},{7,5},{8,12},{9,11},{10,... | collective-permute-start | bytes 1916936 | tf_op jit(solution)/shard_map/ppermute | solution.py:840
  41.4 13.1 %collective-permute-start.5 = (bf16[4,48,1664]{2,1,0:T(8,128)(2,1)S(1)}, bf16[4,48,1664]{2,1,0:T(8,128)(2,1)}, u32[]{:S(2)}, u32[]{:S(2)}) collective-permute-start(bf16[4,48,1664]{2,1,0:T(8,128)(2,1)S(1)} %collective-permute-done.4.refs_1_), channel_id=1, source_target_pairs={{0,4},{1,3},{2,6},{3,1},{4,0},{5,7},{6,2},{7,5},{8,12},{9,11},{10,... | collective-permute-start | bytes 1916936 | tf_op jit(solution)/shard_map/ppermute | solution.py:840
  53.9 4.0 %collective-permute-start.12 = (bf16[4,48,1664]{2,1,0:T(8,128)(2,1)S(1)}, bf16[4,48,1664]{2,1,0:T(8,128)(2,1)}, u32[]{:S(2)}, u32[]{:S(2)}) collective-permute-start(bf16[4,48,1664]{2,1,0:T(8,128)(2,1)S(1)} %collective-permute-done.4.refs_1_), channel_id=1, source_target_pairs={{0,1},{1,0},{2,3},{3,2},{4,5},{5,4},{6,7},{7,6},{8,9},{9,8},{10,11... | collective-permute-start | bytes 1916936 | tf_op jit(solution)/shard_map/ppermute | solution.py:840
  54.4 5.0 %collective-permute-start.13 = (bf16[4,48,1664]{2,1,0:T(8,128)(2,1)S(1)}, bf16[4,48,1664]{2,1,0:T(8,128)(2,1)}, u32[]{:S(2)}, u32[]{:S(2)}) collective-permute-start(bf16[4,48,1664]{2,1,0:T(8,128)(2,1)S(1)} %collective-permute-done.3.refs_2_), channel_id=1, source_target_pairs={{0,1},{1,0},{2,3},{3,2},{4,5},{5,4},{6,7},{7,6},{8,9},{9,8},{10,11... | collective-permute-start | bytes 1916936 | tf_op jit(solution)/shard_map/ppermute | solution.py:840
  54.6 4.9 %collective-permute-start.14 = (bf16[4,48,1664]{2,1,0:T(8,128)(2,1)}, bf16[4,48,1664]{2,1,0:T(8,128)(2,1)}, u32[]{:S(2)}, u32[]{:S(2)}) collective-permute-start(bf16[4,48,1664]{2,1,0:T(8,128)(2,1)} %collective-permute-done.5.refs_3_), channel_id=1, source_target_pairs={{0,1},{1,0},{2,3},{3,2},{4,5},{5,4},{6,7},{7,6},{8,9},{9,8},{10,11... | collective-permute-start | bytes 1916936 | tf_op jit(solution)/shard_map/ppermute | solution.py:840
  55.6 46.6 %collective-permute-start.16 = (bf16[4,48,3072]{2,1,0:T(8,128)(2,1)S(1)}, bf16[4,48,3072]{2,1,0:T(8,128)(2,1)}, u32[]{:S(2)}, u32[]{:S(2)}) collective-permute-start(bf16[4,48,3072]{2,1,0:T(8,128)(2,1)S(1)} %pad_maximum_fusion.refs_0_), channel_id=1, source_target_pairs={{0,1},{1,0},{2,3},{3,2},{4,5},{5,4},{6,7},{7,6},{8,9},{9,8},{10,11... | collective-permute-start | bytes 3538952 | tf_op jit(solution)/shard_map/ppermute | solution.py:840
  56.1 29.4 %collective-permute-start.10 = (bf16[4,48,3072]{2,1,0:T(8,128)(2,1)S(1)}, bf16[4,48,3072]{2,1,0:T(8,128)(2,1)}, u32[]{:S(2)}, u32[]{:S(2)}) collective-permute-start(bf16[4,48,3072]{2,1,0:T(8,128)(2,1)S(1)} %pad_maximum_fusion.refs_0_), channel_id=1, source_target_pairs={{0,4},{1,3},{2,6},{3,1},{4,0},{5,7},{6,2},{7,5},{8,12},{9,11},{10,... | collective-permute-start | bytes 3538952 | tf_op jit(solution)/shard_map/ppermute | solution.py:840
  57.9 27.6 %collective-permute-start.9 = (bf16[4,48,3072]{2,1,0:T(8,128)(2,1)S(1)}, bf16[4,48,3072]{2,1,0:T(8,128)(2,1)}, u32[]{:S(2)}, u32[]{:S(2)}) collective-permute-start(bf16[4,48,3072]{2,1,0:T(8,128)(2,1)S(1)} %pad_maximum_fusion.refs_0_), channel_id=1, source_target_pairs={{0,2},{1,5},{2,0},{3,7},{4,6},{5,1},{6,4},{7,3},{8,10},{9,13},{10,... | collective-permute-start | bytes 3538952 | tf_op jit(solution)/shard_map/ppermute | solution.py:840
  85.5 16.7 %collective-permute-start.17 = (bf16[4,48,3072]{2,1,0:T(8,128)(2,1)}, bf16[4,48,3072]{2,1,0:T(8,128)(2,1)}, u32[]{:S(2)}, u32[]{:S(2)}) collective-permute-start(bf16[4,48,3072]{2,1,0:T(8,128)(2,1)} %collective-permute-done.9.refs_1_), channel_id=1, source_target_pairs={{0,1},{1,0},{2,3},{3,2},{4,5},{5,4},{6,7},{7,6},{8,9},{9,8},{10,11... | collective-permute-start | bytes 3538952 | tf_op jit(solution)/shard_map/ppermute | solution.py:840
  85.6 16.6 %collective-permute-start.15 = (bf16[4,48,3072]{2,1,0:T(8,128)(2,1)}, bf16[4,48,3072]{2,1,0:T(8,128)(2,1)}, u32[]{:S(2)}, u32[]{:S(2)}) collective-permute-start(bf16[4,48,3072]{2,1,0:T(8,128)(2,1)} %collective-permute-done.9.refs_1_), channel_id=1, source_target_pairs={{0,4},{1,3},{2,6},{3,1},{4,0},{5,7},{6,2},{7,5},{8,12},{9,11},{10,... | collective-permute-start | bytes 3538952 | tf_op jit(solution)/shard_map/ppermute | solution.py:840
  86.2 16.0 %collective-permute-start.18 = (bf16[4,48,3072]{2,1,0:T(8,128)(2,1)}, bf16[4,48,3072]{2,1,0:T(8,128)(2,1)}, u32[]{:S(2)}, u32[]{:S(2)}) collective-permute-start(bf16[4,48,3072]{2,1,0:T(8,128)(2,1)} %collective-permute-done.10.refs_2_), channel_id=1, source_target_pairs={{0,1},{1,0},{2,3},{3,2},{4,5},{5,4},{6,7},{7,6},{8,9},{9,8},{10,11... | collective-permute-start | bytes 3538952 | tf_op jit(solution)/shard_map/ppermute | solution.py:840
  153.2 11.2 %collective-permute-start.20 = (bf16[16,48,1536]{2,1,0:T(8,128)(2,1)}, bf16[16,48,1536]{2,1,0:T(8,128)(2,1)}, u32[]{:S(2)}, u32[]{:S(2)}) collective-permute-start(bf16[16,48,1536]{2,1,0:T(8,128)(2,1)} %get-tuple-element.136), channel_id=1, source_target_pairs={{0,1},{1,0},{2,3},{3,2},{4,5},{5,4},{6,7},{7,6},{8,9},{9,8},{10,11... | collective-permute-start | bytes 7077896 | tf_op jit(solution)/shard_map/ppermute | solution.py:840
  167.3 9.3 %collective-permute-start.21 = (bf16[16,48,1920]{2,1,0:T(8,128)(2,1)}, bf16[16,48,1920]{2,1,0:T(8,128)(2,1)}, u32[]{:S(2)}, u32[]{:S(2)}) collective-permute-start(bf16[16,48,1920]{2,1,0:T(8,128)(2,1)} %get-tuple-element.147), channel_id=1, source_target_pairs={{0,1},{1,0},{2,3},{3,2},{4,5},{5,4},{6,7},{7,6},{8,9},{9,8},{10,11... | collective-permute-start | bytes 8847368 | tf_op jit(solution)/shard_map/ppermute | solution.py:840
  167.7 22.2 %collective-permute-start.22 = (bf16[8,48,1536]{2,1,0:T(8,128)(2,1)}, bf16[8,48,1536]{2,1,0:T(8,128)(2,1)}, u32[]{:S(2)}, u32[]{:S(2)}) collective-permute-start(bf16[8,48,1536]{2,1,0:T(8,128)(2,1)} %get-tuple-element.152), channel_id=1, source_target_pairs={{0,4},{1,3},{2,6},{3,1},{4,0},{5,7},{6,2},{7,5},{8,12},{9,11},{10,... | collective-permute-start | bytes 3538952 | tf_op jit(solution)/shard_map/ppermute | solution.py:840
  180.0 25.5 %collective-permute-start.23 = (bf16[8,48,1920]{2,1,0:T(8,128)(2,1)}, bf16[8,48,1920]{2,1,0:T(8,128)(2,1)}, u32[]{:S(2)}, u32[]{:S(2)}) collective-permute-start(bf16[8,48,1920]{2,1,0:T(8,128)(2,1)} %get-tuple-element.160), channel_id=1, source_target_pairs={{0,4},{1,3},{2,6},{3,1},{4,0},{5,7},{6,2},{7,5},{8,12},{9,11},{10,... | collective-permute-start | bytes 4423688 | tf_op jit(solution)/shard_map/ppermute | solution.py:840
  192.4 13.1 %collective-permute-start.24 = (bf16[4,48,1536]{2,1,0:T(8,128)(2,1)}, bf16[4,48,1536]{2,1,0:T(8,128)(2,1)}, u32[]{:S(2)}, u32[]{:S(2)}) collective-permute-start(bf16[4,48,1536]{2,1,0:T(8,128)(2,1)} %get-tuple-element.161), channel_id=1, source_target_pairs={{0,2},{1,5},{2,0},{3,7},{4,6},{5,1},{6,4},{7,3},{8,10},{9,13},{10,... | collective-permute-start | bytes 1769480 | tf_op jit(solution)/shard_map/ppermute | solution.py:840
  208.8 11.8 %collective-permute-start.25 = (bf16[4,48,1920]{2,1,0:T(8,128)(2,1)}, bf16[4,48,1920]{2,1,0:T(8,128)(2,1)}, u32[]{:S(2)}, u32[]{:S(2)}) collective-permute-start(bf16[4,48,1920]{2,1,0:T(8,128)(2,1)} %get-tuple-element.165), channel_id=1, source_target_pairs={{0,2},{1,5},{2,0},{3,7},{4,6},{5,1},{6,4},{7,3},{8,10},{9,13},{10,... | collective-permute-start | bytes 2211848 | tf_op jit(solution)/shard_map/ppermute | solution.py:840
  209.8 9.6 %collective-permute-start.26 = (bf16[2,48,1536]{2,1,0:T(8,128)(2,1)}, bf16[2,48,1536]{2,1,0:T(8,128)(2,1)S(1)}, u32[]{:S(2)}, u32[]{:S(2)}) collective-permute-start(bf16[2,48,1536]{2,1,0:T(8,128)(2,1)} %get-tuple-element.166), channel_id=1, source_target_pairs={{0,8},{1,17},{2,10},{3,19},{4,12},{5,21},{6,14},{7,23},{8,0},{9,25... | collective-permute-start | bytes 884744 | tf_op jit(solution)/shard_map/ppermute | solution.py:840
  220.5 4.3 %collective-permute-start.27 = (bf16[16,48,1280]{2,1,0:T(8,128)(2,1)}, bf16[16,48,1280]{2,1,0:T(8,128)(2,1)}, u32[]{:S(2)}, u32[]{:S(2)}) collective-permute-start(bf16[16,48,1280]{2,1,0:T(8,128)(2,1)} %gate.3), channel_id=1, source_target_pairs={{0,1},{1,0},{2,3},{3,2},{4,5},{5,4},{6,7},{7,6},{8,9},{9,8},{10,11... | collective-permute-start | bytes 5898248 | tf_op jit(solution)/shard_map/ppermute | solution.py:840
  227.6 15.4 %collective-permute-start.28 = (bf16[8,48,1280]{2,1,0:T(8,128)(2,1)}, bf16[8,48,1280]{2,1,0:T(8,128)(2,1)}, u32[]{:S(2)}, u32[]{:S(2)}) collective-permute-start(bf16[8,48,1280]{2,1,0:T(8,128)(2,1)} %get-tuple-element.170), channel_id=1, source_target_pairs={{0,4},{1,3},{2,6},{3,1},{4,0},{5,7},{6,2},{7,5},{8,12},{9,11},{10,... | collective-permute-start | bytes 2949128 | tf_op jit(solution)/shard_map/ppermute | solution.py:840
  228.9 13.1 %collective-permute-start.30 = (bf16[1,48,1536]{2,1,0:T(8,128)(2,1)}, bf16[1,48,1536]{2,1,0:T(8,128)(2,1)}, u32[]{:S(2)}, u32[]{:S(2)}) collective-permute-start(bf16[1,48,1536]{2,1,0:T(8,128)(2,1)} %get-tuple-element.172), channel_id=1, source_target_pairs={{0,16},{1,9},{2,18},{3,11},{4,20},{5,13},{6,22},{7,15},{8,24},{9,1... | collective-permute-start | bytes 442376 | tf_op jit(solution)/shard_map/ppermute | solution.py:840
  231.5 11.4 %collective-permute-start.29 = (bf16[2,48,1920]{2,1,0:T(8,128)(2,1)}, bf16[2,48,1920]{2,1,0:T(8,128)(2,1)S(1)}, u32[]{:S(2)}, u32[]{:S(2)}) collective-permute-start(bf16[2,48,1920]{2,1,0:T(8,128)(2,1)} %get-tuple-element.171), channel_id=1, source_target_pairs={{0,8},{1,17},{2,10},{3,19},{4,12},{5,21},{6,14},{7,23},{8,0},{9,25... | collective-permute-start | bytes 1105928 | tf_op jit(solution)/shard_map/ppermute | solution.py:840
  245.6 9.4 %collective-permute-start.31 = (bf16[4,48,1280]{2,1,0:T(8,128)(2,1)S(1)}, bf16[4,48,1280]{2,1,0:T(8,128)(2,1)S(1)}, u32[]{:S(2)}, u32[]{:S(2)}) collective-permute-start(bf16[4,48,1280]{2,1,0:T(8,128)(2,1)S(1)} %get-tuple-element.175), channel_id=1, source_target_pairs={{0,2},{1,5},{2,0},{3,7},{4,6},{5,1},{6,4},{7,3},{8,10},{9,13},{10,... | collective-permute-start | bytes 1474568 | tf_op jit(solution)/shard_map/ppermute | solution.py:840
  248.4 6.6 %collective-permute-start.32 = (bf16[1,48,1920]{2,1,0:T(8,128)(2,1)S(1)}, bf16[1,48,1920]{2,1,0:T(8,128)(2,1)S(1)}, u32[]{:S(2)}, u32[]{:S(2)}) collective-permute-start(bf16[1,48,1920]{2,1,0:T(8,128)(2,1)S(1)} %get-tuple-element.179), channel_id=1, source_target_pairs={{0,16},{1,9},{2,18},{3,11},{4,20},{5,13},{6,22},{7,15},{8,24},{9,1... | collective-permute-start | bytes 552968 | tf_op jit(solution)/shard_map/ppermute | solution.py:840
  255.7 8.0 %collective-permute-start.33 = (bf16[2,48,1280]{2,1,0:T(8,128)(2,1)S(1)}, bf16[2,48,1280]{2,1,0:T(8,128)(2,1)S(1)}, u32[]{:S(2)}, u32[]{:S(2)}) collective-permute-start(bf16[2,48,1280]{2,1,0:T(8,128)(2,1)S(1)} %get-tuple-element.182), channel_id=1, source_target_pairs={{0,8},{1,17},{2,10},{3,19},{4,12},{5,21},{6,14},{7,23},{8,0},{9,25... | collective-permute-start | bytes 737288 | tf_op jit(solution)/shard_map/ppermute | solution.py:840
  266.1 6.8 %collective-permute-start.34 = (bf16[1,48,1280]{2,1,0:T(8,128)(2,1)S(1)}, bf16[1,48,1280]{2,1,0:T(8,128)(2,1)S(1)}, u32[]{:S(2)}, u32[]{:S(2)}) collective-permute-start(bf16[1,48,1280]{2,1,0:T(8,128)(2,1)S(1)} %get-tuple-element.186), channel_id=1, source_target_pairs={{0,16},{1,9},{2,18},{3,11},{4,20},{5,13},{6,22},{7,15},{8,24},{9,1... | collective-permute-start | bytes 368648 | tf_op jit(solution)/shard_map/ppermute | solution.py:840
  (15 other events, 96.9 us)

commit v4 on v3

--- a/solution.py
+++ b/solution.py
@@ -921,7 +921,6 @@
         first_then, first_core = move(first, ALONG_XY_THEN), move(first, CORE)
         first_came = move(first, ALONG_XY_FIRST)
         first_last, came_core = move(first_came, ALONG_XY_THEN), move(first_came, CORE)
-        first_then, first_last, second = after(first_then, first_last, second)
         first = [first, first_came, first_then, first_last]
         first += [first_core, came_core, move(first_then, CORE), move(first_last, CORE)]
         second_came, second_then, second_core = move(second, ALONG_XY_FIRST), move(second, ALONG_XY_THEN), move(second, CORE)

time: 278 us -> 278 us (level)
  transfers between devices with their start and end apart: 37 -> 37, of which waited for: 18 -> 17; matrix products, arithmetic and copies ran while one was open for 1% -> 1% of each run, Pallas kernels for 38% -> 38%
where the time goes in v4:
time: 278 us; the launch traced here: 277 us
  Pallas kernels  168 us (60%)
  waiting for transfers between devices  57.7 us (21%)
  starting transfers between devices  39.3 us (14%)
  local copies, waits for them, and re-layouts  9.83 us (4%)
    pallas_call x23, Pallas kernels, call(): return pl.pallas_call(body, in_specs=in_specs, **options)(*operands, *deps)  92.2 us
    ppermute x37, waiting for transfers between devices, move(): return lax.ppermute(v, AXES, [(i, i ^ masks[i & 1]) for i in range(SLABS)])  57.7 us
    pallas_call x1, Pallas kernels, feed_forward(): pl.pallas_call(functools.partial(ffn_kernel, meta, len(pieces), blocks),...  47.8 us
    ppermute x37, starting transfers between devices, move(): return lax.ppermute(v, AXES, [(i, i ^ masks[i & 1]) for i in range(SLABS)])  39.3 us
    pallas_call x1, Pallas kernels, attend(): pl.pallas_call(functools.partial(attend_kernel, meta, len(pieces)), grid=...  17.4 us
    pallas_call x1, Pallas kernels, inner_grads(): pl.pallas_call(inner_grads_kernel, grid=(steps + 1,), in_specs=[whole(D,...  11 us
  transfers between devices with their start and end apart: 37, of which 17 were waited for; matrix products, arithmetic and copies ran while one was open for 1% of the time, Pallas kernels for 38%

profile of v4, /device:TPU:0, one launch (start us, length us, event | category | flops | bytes accessed | tf_op | source)
XLA Modules:
  0.0 277.0 jit_solution(2562815785130028501)
XLA Ops:
  7.8 4.0 %collective-permute-start.1 = (bf16[1,48,1664]{2,1,0:T(8,128)(2,1)S(1)}, bf16[1,48,1664]{2,1,0:T(8,128)(2,1)S(1)}, u32[]{:S(2)}, u32[]{:S(2)}) collective-permute-start(bf16[1,48,1664]{2,1,0:T(8,128)(2,1)S(1)} %fusion.4), channel_id=1, source_target_pairs={{0,16},{1,9},{2,18},{3,11},{4,20},{5,13},{6,22},{7,15},{8,24},{9,1... | collective-permute-start | bytes 479240 | tf_op jit(solution)/shard_map/ppermute | solution.py:840
  11.9 3.7 %collective-permute-done.1 = bf16[1,48,1664]{2,1,0:T(8,128)(2,1)S(1)} collective-permute-done((bf16[1,48,1664]{2,1,0:T(8,128)(2,1)S(1)}, bf16[1,48,1664]{2,1,0:T(8,128)(2,1)S(1)}, u32[]{:S(2)}, u32[]{:S(2)}) %collective-permute-start.1) | collective-permute-done | bytes 159776 | tf_op jit(solution)/shard_map/ppermute | solution.py:840
  15.6 2.5 collective-permute-start.7
  18.1 8.3 %collective-permute-done.7 = bf16[2,48,1664]{2,1,0:T(8,128)(2,1)S(1)} collective-permute-done((bf16[2,48,1664]{2,1,0:T(8,128)(2,1)S(1)}, bf16[2,48,1664]{2,1,0:T(8,128)(2,1)S(1)}, u32[]{:S(2)}, u32[]{:S(2)}) %collective-permute-start.7) | collective-permute-done | bytes 319520 | tf_op jit(solution)/shard_map/ppermute | solution.py:840
  28.8 2.9 %collective-permute-start.4 = (bf16[1,48,3072]{2,1,0:T(8,128)(2,1)S(1)}, bf16[1,48,3072]{2,1,0:T(8,128)(2,1)S(1)}, u32[]{:S(2)}, u32[]{:S(2)}) collective-permute-start(bf16[1,48,3072]{2,1,0:T(8,128)(2,1)S(1)} %fusion.2), channel_id=1, source_target_pairs={{0,24},{1,25},{2,26},{3,27},{4,28},{5,29},{6,30},{7,31},{8,16},{9,... | collective-permute-start | bytes 884744 | tf_op jit(solution)/shard_map/ppermute | solution.py:840
  34.7 6.2 %collective-permute-done.8.refs_1_ = bf16[4,48,1664]{2,1,0:T(8,128)(2,1)} collective-permute-done((bf16[4,48,1664]{2,1,0:T(8,128)(2,1)S(1)}, bf16[4,48,1664]{2,1,0:T(8,128)(2,1)}, u32[]{:S(2)}, u32[]{:S(2)}) %collective-permute-start.8) | collective-permute-done | bytes 639008 | tf_op jit(solution)/shard_map/ppermute | solution.py:840
  40.9 2.9 %collective-permute-start.10 = (bf16[4,48,1664]{2,1,0:T(8,128)(2,1)}, bf16[4,48,1664]{2,1,0:T(8,128)(2,1)S(1)}, u32[]{:S(2)}, u32[]{:S(2)}) collective-permute-start(bf16[4,48,1664]{2,1,0:T(8,128)(2,1)} %collective-permute-done.8.refs_1_), channel_id=1, source_target_pairs={{0,4},{1,3},{2,6},{3,1},{4,0},{5,7},{6,2},{7,5},{8,12},{9,11},{10,... | collective-permute-start | bytes 1916936 | tf_op jit(solution)/shard_map/ppermute | solution.py:840
  43.8 10.5 %collective-permute-done.2 = bf16[1,48,3072]{2,1,0:T(8,128)(2,1)S(1)} collective-permute-done((bf16[1,48,3072]{2,1,0:T(8,128)(2,1)S(1)}, bf16[1,48,3072]{2,1,0:T(8,128)(2,1)S(1)}, u32[]{:S(2)}, u32[]{:S(2)}) %collective-permute-start.2) | collective-permute-done | bytes 294944 | tf_op jit(solution)/shard_map/ppermute | solution.py:840
  57.0 2.2 collective-permute-done.13.refs_6_
  61.5 17.4 %attend.1 = (bf16[1024,2304]{1,0:T(8,128)(2,1)}, bf16[1024,768]{1,0:T(8,128)(2,1)}, f32[2,16,512]{2,1,0:T(8,128)}, bf16[768,3328]{1,0:T(8,128)(2,1)}, f32[16,768]{1,0:T(8,128)}) custom-call(s32[2]{0:T(128)} %pad_add_fusion.place.refs_0_, s32[2]{0:T(128)} %refs_0_.3, f32[1024,768]{1,0:T(8,128)} %refs_5_.1, bf16[4,48,1664]{2,1,0:T(8,128)(2,1)} %copy-done.6, ...), custom_call_target="tpu_custom_call" | custom-call | flops 17999998976 | bytes 20971520 | tf_op jit(solution)/shard_map/attend/pallas_call | solution.py:202
  78.9 7.0 %probs.1.refs_4_ = bf16[24,512,512]{2,1,0:T(8,128)(2,1)} custom-call(s32[2]{0:T(128)} %refs_0_.3, bf16[1024,2304]{1,0:T(8,128)(2,1)} %get-tuple-element.111.refs_1_.refs_2_.refs_0_, bf16[1024,2304]{1,0:T(8,128)(2,1)} %get-tuple-element.111.refs_1_.refs_2_.refs_0_, f32[2,16,512]{2,1,0:T(8,128)} %get-tuple-element.112.refs_3_), custom_call_target="tpu_custom_call" | custom-call | flops 8000000000 | bytes 1048576 | tf_op jit(solution)/shard_map/probs/pallas_call | solution.py:67
  88.7 13.2 %window.1 = (bf16[24,512,512]{2,1,0:T(8,128)(2,1)}, f32[1024,768]{1,0:T(8,128)}, f32[1024,128]{1,0:T(8,128)}, bf16[1024,768]{1,0:T(8,128)(2,1)}, bf16[768,1024]{...) custom-call(s32[2]{0:T(128)} %refs_0_.3, ...), custom_call_target="tpu_custom_call", output_to_operand_aliasing={{0}: (4, {})} | custom-call | flops 14000000000 | bytes 1048576 | tf_op jit(solution)/shard_map/window/pallas_call | solution.py:67
  102.6 3.2 %collective-permute-done.19.refs_7_ = bf16[4,48,3072]{2,1,0:T(8,128)(2,1)} collective-permute-done((bf16[4,48,3072]{2,1,0:T(8,128)(2,1)}, bf16[4,48,3072]{2,1,0:T(8,128)(2,1)}, u32[]{:S(2)}, u32[]{:S(2)}) %collective-permute-start.19) | collective-permute-done | bytes 1179680 | tf_op jit(solution)/shard_map/ppermute | solution.py:840
  105.8 47.8 %feed_forward.1 = (f32[1024,768]{1,0:T(8,128)}, f32[1024,768]{1,0:T(8,128)}, bf16[1024,768]{1,0:T(8,128)(2,1)}, bf16[1024,3072]{1,0:T(8,128)(2,1)}, bf16[1024,76...) custom-call(s32[2]{0:T(128)} %pad_add_fusion.place.refs_0_, ...), custom_call_target="tpu_custom_call" | custom-call | flops 51999997952 | bytes 41943040 | tf_op jit(solution)/shard_map/feed_forward/pallas_call | solution.py:448
  153.8 11.0 %inner_grads.1 = (bf16[16,48,1920]{2,1,0:T(8,128)(2,1)}, bf16[16,48,1920]{2,1,0:T(8,128)(2,1)}) custom-call(bf16[768,1024]{1,0:T(8,128)(2,1)} %get-tuple-element.131.hid_t, bf16[1024,3072]{1,0:T(8,128)(2,1)} %get-tuple-element.132.ib_ref, s32[2]{0:T(128)} %pad_add_fusion.place.refs_0_, bf16[768,1024]{1,0:T(8,128)(2,1)} %get-tuple-element.133.att_in, ...), custom_call_target="tpu_custom_call" | custom-call | flops 4000000000 | bytes 1048576 | tf_op jit(solution)/shard_map/inner_grads/pallas_call | solution.py:518
  164.8 3.0 %add_up.11 = (bf16[8,48,1536]{2,1,0:T(8,128)(2,1)}, bf16[16,48,1920]{2,1,0:T(8,128)(2,1)}, f32[8,128]{1,0:T(8,128)}) custom-call(s32[2]{0:T(128)} %pad_add_fusion.place.refs_0_, bf16[16,48,1536]{2,1,0:T(8,128)(2,1)} %get-tuple-element.129.refs_1_.refs_4_.refs_5_, ...), custom_call_target="tpu_custom_call", output_to_operand_aliasing={{1}: (3, {})} | custom-call | flops 1000 | bytes 1000 | tf_op jit(solution)/shard_map/add_up/pallas_call | solution.py:67
  168.7 8.4 %attend_back_0.1 = (bf16[1024,768]{1,0:T(8,128)(2,1)}, bf16[1024,768]{1,0:T(8,128)(2,1)}, bf16[1024,768]{1,0:T(8,128)(2,1)}) custom-call(bf16[1024,2304]{1,0:T(8,128)(2,1)} %get-tuple-element.111.refs_1_.refs_2_.refs_0_, bf16[1024,2304]{1,0:T(8,128)(2,1)} %get-tuple-element.111.refs_1_.refs_2_.refs_0_, ...), custom_call_target="tpu_custom_call" | custom-call | flops 3000000000 | bytes 1048576 | tf_op jit(solution)/shard_map/attend_back_0/pallas_call | solution.py:67
  177.2 3.3 %add_up.12 = (bf16[8,48,1920]{2,1,0:T(8,128)(2,1)}, f32[8,128]{1,0:T(8,128)}) custom-call(s32[2]{0:T(128)} %pad_add_fusion.place.refs_0_, bf16[16,48,1920]{2,1,0:T(8,128)(2,1)} %get-tuple-element.136.refs_4_.refs_1_, bf16[16,48,1920]{2,1,0:T(8,128)(2,1)} %collective-permute-done.21.refs_2_, bf16[1024,768]{1,0:T(8,128)(2,1)} %get-tuple-element.138.refs_3_.refs_5_), custom_call_target="tpu_custom_call" | custom-call | flops 1000 | bytes 1000 | tf_op jit(solution)/shard_map/add_up/pallas_call | solution.py:67
  181.9 8.4 %attend_back_4.1 = (bf16[1024,768]{1,0:T(8,128)(2,1)}, bf16[1024,768]{1,0:T(8,128)(2,1)}, bf16[1024,768]{1,0:T(8,128)(2,1)}) custom-call(bf16[1024,2304]{1,0:T(8,128)(2,1)} %get-tuple-element.111.refs_1_.refs_2_.refs_0_, bf16[1024,2304]{1,0:T(8,128)(2,1)} %get-tuple-element.111.refs_1_.refs_2_.refs_0_, ...), custom_call_target="tpu_custom_call", output_to_operand_aliasing={{0}: (5, {}), {1}: (6, {}), {2}: (7, {})} | custom-call | flops 3000000000 | bytes 1048576 | tf_op jit(solution)/shard_map/attend_back_4/pallas_call | solution.py:67
  190.4 2.5 add_up.13
  193.7 8.5 %attend_back_8.1 = (bf16[1024,768]{1,0:T(8,128)(2,1)}, bf16[1024,768]{1,0:T(8,128)(2,1)}, bf16[1024,768]{1,0:T(8,128)(2,1)}) custom-call(bf16[1024,2304]{1,0:T(8,128)(2,1)} %get-tuple-element.111.refs_1_.refs_2_.refs_0_, bf16[1024,2304]{1,0:T(8,128)(2,1)} %get-tuple-element.111.refs_1_.refs_2_.refs_0_, ...), custom_call_target="tpu_custom_call", output_to_operand_aliasing={{0}: (5, {}), {1}: (6, {}), {2}: (7, {})} | custom-call | flops 3000000000 | bytes 1048576 | tf_op jit(solution)/shard_map/attend_back_8/pallas_call | solution.py:67
  202.2 3.8 %collective-permute-done.24.refs_7_.refs_8_ = bf16[4,48,1536]{2,1,0:T(8,128)(2,1)} collective-permute-done((bf16[4,48,1536]{2,1,0:T(8,128)(2,1)}, bf16[4,48,1536]{2,1,0:T(8,128)(2,1)}, u32[]{:S(2)}, u32[]{:S(2)}) %collective-permute-start.24) | collective-permute-done | bytes 589856 | tf_op jit(solution)/shard_map/ppermute | solution.py:840
  206.0 3.2 %add_up.14 = (bf16[4,48,1920]{2,1,0:T(8,128)(2,1)}, bf16[2,48,1536]{2,1,0:T(8,128)(2,1)}, f32[8,128]{1,0:T(8,128)}) custom-call(s32[2]{0:T(128)} %pad_add_fusion.place.refs_0_, bf16[16,48,1920]{2,1,0:T(8,128)(2,1)} %get-tuple-element.136.refs_4_.refs_1_, bf16[16,48,1920]{2,1,0:T(8,128)(2,1)} %collective-permute-done.21.refs_2_, ...), custom_call_target="tpu_custom_call" | custom-call | flops 1000 | bytes 1000 | tf_op jit(solution)/shard_map/add_up/pallas_call | solution.py:67
  210.1 9.6 %proj_grads.1 = (bf16[16,48,1280]{2,1,0:T(8,128)(2,1)}, bf16[16,48,1280]{2,1,0:T(8,128)(2,1)}) custom-call(s32[2]{0:T(128)} %pad_add_fusion.place.refs_0_, bf16[768,1024]{1,0:T(8,128)(2,1)} %get-tuple-element.151.refs_1_, f32[6,8,768]{2,1,0:T(8,128)} %get-tuple-element.152.refs_2_, f32[8,3072]{1,0:T(8,128)} %get-tuple-element.153.refs_3_, ...), custom_call_target="tpu_custom_call" | custom-call | flops 4000000000 | bytes 1048576 | tf_op jit(solution)/shard_map/proj_grads/pallas_call | solution.py:67
  221.2 3.6 %add_up.15 = (bf16[2,48,1920]{2,1,0:T(8,128)(2,1)}, f32[2,48,1920]{2,1,0:T(8,128)}, bf16[1,48,1536]{2,1,0:T(8,128)(2,1)}, f32[1,48,1536]{2,1,0:T(8,128)}, f32[8,128]{1,0:T(8,128)}) custom-call(s32[2]{0:T(128)} %pad_add_fusion.place.refs_0_, bf16[16,48,1920]{2,1,0:T(8,128)(2,1)} %get-tuple-element.136.refs_4_.refs_1_, ...), custom_call_target="tpu_custom_call" | custom-call | flops 1000 | bytes 1000 | tf_op jit(solution)/shard_map/add_up/pallas_call | solution.py:67
  225.3 2.7 add_up.16
  229.1 2.5 collective-permute-start.30
  232.3 9.7 %input_back_0.1 = (f32[1024,768]{1,0:T(8,128)}, f32[16,128]{1,0:T(8,128)}) custom-call(f32[1024,768]{1,0:T(8,128)} %get-tuple-element.126.refs_0_, bf16[1024,768]{1,0:T(8,128)(2,1)} %get-tuple-element.148.refs_8_.refs_4_.refs_1_, bf16[1024,768]{1,0:T(8,128)(2,1)} %get-tuple-element.149.refs_5_.refs_2_, bf16[1024,768]{1,0:T(8,128)(2,1)} %get-tuple-element.150.refs_6_.refs_3_, ...), custom_call_target="tpu_custom_call" | custom-call | flops 10000000000 | bytes 1048576 | tf_op jit(solution)/shard_map/input_back_0/pallas_call | solution.py:67
  251.0 4.5 %collective-permute-done.32.refs_1_.refs_4_ = bf16[1,48,1920]{2,1,0:T(8,128)(2,1)S(1)} collective-permute-done((bf16[1,48,1920]{2,1,0:T(8,128)(2,1)S(1)}, bf16[1,48,1920]{2,1,0:T(8,128)(2,1)S(1)}, u32[]{:S(2)}, u32[]{:S(2)}) %collective-permute-start.32) | collective-permute-done | bytes 184352 | tf_op jit(solution)/shard_map/ppermute | solution.py:840
  256.1 2.5 collective-permute-start.33
  258.6 5.5 %collective-permute-done.33.refs_2_ = bf16[2,48,1280]{2,1,0:T(8,128)(2,1)S(1)} collective-permute-done((bf16[2,48,1280]{2,1,0:T(8,128)(2,1)S(1)}, bf16[2,48,1280]{2,1,0:T(8,128)(2,1)S(1)}, u32[]{:S(2)}, u32[]{:S(2)}) %collective-permute-start.33) | collective-permute-done | bytes 245792 | tf_op jit(solution)/shard_map/ppermute | solution.py:840
  269.1 4.0 %collective-permute-done.34.refs_2_ = bf16[1,48,1280]{2,1,0:T(8,128)(2,1)S(1)} collective-permute-done((bf16[1,48,1280]{2,1,0:T(8,128)(2,1)S(1)}, bf16[1,48,1280]{2,1,0:T(8,128)(2,1)S(1)}, u32[]{:S(2)}, u32[]{:S(2)}) %collective-permute-start.34) | collective-permute-done | bytes 122912 | tf_op jit(solution)/shard_map/ppermute | solution.py:840
  (117 shorter events, 47.6 us)
Async XLA Ops:
  7.8 7.8 %collective-permute-start.1 = (bf16[1,48,1664]{2,1,0:T(8,128)(2,1)S(1)}, bf16[1,48,1664]{2,1,0:T(8,128)(2,1)S(1)}, u32[]{:S(2)}, u32[]{:S(2)}) collective-permute-start(bf16[1,48,1664]{2,1,0:T(8,128)(2,1)S(1)} %fusion.4), channel_id=1, source_target_pairs={{0,16},{1,9},{2,18},{3,11},{4,20},{5,13},{6,22},{7,15},{8,24},{9,1... | collective-permute-start | bytes 479240 | tf_op jit(solution)/shard_map/ppermute | solution.py:840
  15.6 10.8 %collective-permute-start.7 = (bf16[2,48,1664]{2,1,0:T(8,128)(2,1)S(1)}, bf16[2,48,1664]{2,1,0:T(8,128)(2,1)S(1)}, u32[]{:S(2)}, u32[]{:S(2)}) collective-permute-start(bf16[2,48,1664]{2,1,0:T(8,128)(2,1)S(1)} %pad_maximum_fusion), channel_id=1, source_target_pairs={{0,8},{1,17},{2,10},{3,19},{4,12},{5,21},{6,14},{7,23},{8,0},{9,25... | collective-permute-start | bytes 958472 | tf_op jit(solution)/shard_map/ppermute | solution.py:840
  26.4 14.4 %collective-permute-start.8 = (bf16[4,48,1664]{2,1,0:T(8,128)(2,1)S(1)}, bf16[4,48,1664]{2,1,0:T(8,128)(2,1)}, u32[]{:S(2)}, u32[]{:S(2)}) collective-permute-start(bf16[4,48,1664]{2,1,0:T(8,128)(2,1)S(1)} %constant_dynamic-update-slice_fusion.12.refs_0_), channel_id=1, source_target_pairs={{0,2},{1,5},{2,0},{3,7},{4,6},{5,1},{6,4},{7,3},{8,10},{9,13},{10,... | collective-permute-start | bytes 1916936 | tf_op jit(solution)/shard_map/ppermute | solution.py:840
  28.8 26.7 %collective-permute-start.4 = (bf16[1,48,3072]{2,1,0:T(8,128)(2,1)S(1)}, bf16[1,48,3072]{2,1,0:T(8,128)(2,1)S(1)}, u32[]{:S(2)}, u32[]{:S(2)}) collective-permute-start(bf16[1,48,3072]{2,1,0:T(8,128)(2,1)S(1)} %fusion.2), channel_id=1, source_target_pairs={{0,24},{1,25},{2,26},{3,27},{4,28},{5,29},{6,30},{7,31},{8,16},{9,... | collective-permute-start | bytes 884744 | tf_op jit(solution)/shard_map/ppermute | solution.py:840
  31.7 22.7 %collective-permute-start.3 = (bf16[1,48,3072]{2,1,0:T(8,128)(2,1)S(1)}, bf16[1,48,3072]{2,1,0:T(8,128)(2,1)S(1)}, u32[]{:S(2)}, u32[]{:S(2)}) collective-permute-start(bf16[1,48,3072]{2,1,0:T(8,128)(2,1)S(1)} %fusion.2), channel_id=1, source_target_pairs={{0,8},{1,17},{2,10},{3,19},{4,12},{5,21},{6,14},{7,23},{8,0},{9,25... | collective-permute-start | bytes 884744 | tf_op jit(solution)/shard_map/ppermute | solution.py:840
  31.7 22.6 %collective-permute-start.2 = (bf16[1,48,3072]{2,1,0:T(8,128)(2,1)S(1)}, bf16[1,48,3072]{2,1,0:T(8,128)(2,1)S(1)}, u32[]{:S(2)}, u32[]{:S(2)}) collective-permute-start(bf16[1,48,3072]{2,1,0:T(8,128)(2,1)S(1)} %fusion.2), channel_id=1, source_target_pairs={{0,16},{1,9},{2,18},{3,11},{4,20},{5,13},{6,22},{7,15},{8,24},{9,1... | collective-permute-start | bytes 884744 | tf_op jit(solution)/shard_map/ppermute | solution.py:840
  33.1 21.7 %collective-permute-start.9 = (bf16[4,48,1664]{2,1,0:T(8,128)(2,1)S(1)}, bf16[4,48,1664]{2,1,0:T(8,128)(2,1)S(1)}, u32[]{:S(2)}, u32[]{:S(2)}) collective-permute-start(bf16[4,48,1664]{2,1,0:T(8,128)(2,1)S(1)} %constant_dynamic-update-slice_fusion.12.refs_0_), channel_id=1, source_target_pairs={{0,4},{1,3},{2,6},{3,1},{4,0},{5,7},{6,2},{7,5},{8,12},{9,11},{10,... | collective-permute-start | bytes 1916936 | tf_op jit(solution)/shard_map/ppermute | solution.py:840
  40.9 14.1 %collective-permute-start.10 = (bf16[4,48,1664]{2,1,0:T(8,128)(2,1)}, bf16[4,48,1664]{2,1,0:T(8,128)(2,1)S(1)}, u32[]{:S(2)}, u32[]{:S(2)}) collective-permute-start(bf16[4,48,1664]{2,1,0:T(8,128)(2,1)} %collective-permute-done.8.refs_1_), channel_id=1, source_target_pairs={{0,4},{1,3},{2,6},{3,1},{4,0},{5,7},{6,2},{7,5},{8,12},{9,11},{10,... | collective-permute-start | bytes 1916936 | tf_op jit(solution)/shard_map/ppermute | solution.py:840
  54.4 6.3 %collective-permute-start.12 = (bf16[4,48,1664]{2,1,0:T(8,128)(2,1)}, bf16[4,48,1664]{2,1,0:T(8,128)(2,1)S(1)}, u32[]{:S(2)}, u32[]{:S(2)}) collective-permute-start(bf16[4,48,1664]{2,1,0:T(8,128)(2,1)} %collective-permute-done.8.refs_1_), channel_id=1, source_target_pairs={{0,1},{1,0},{2,3},{3,2},{4,5},{5,4},{6,7},{7,6},{8,9},{9,8},{10,11... | collective-permute-start | bytes 1916936 | tf_op jit(solution)/shard_map/ppermute | solution.py:840
  54.9 4.3 %collective-permute-start.13 = (bf16[4,48,1664]{2,1,0:T(8,128)(2,1)S(1)}, bf16[4,48,1664]{2,1,0:T(8,128)(2,1)S(1)}, u32[]{:S(2)}, u32[]{:S(2)}) collective-permute-start(bf16[4,48,1664]{2,1,0:T(8,128)(2,1)S(1)} %collective-permute-done.9.refs_2_), channel_id=1, source_target_pairs={{0,1},{1,0},{2,3},{3,2},{4,5},{5,4},{6,7},{7,6},{8,9},{9,8},{10,11... | collective-permute-start | bytes 1916936 | tf_op jit(solution)/shard_map/ppermute | solution.py:840
  55.0 6.6 %collective-permute-start.14 = (bf16[4,48,1664]{2,1,0:T(8,128)(2,1)S(1)}, bf16[4,48,1664]{2,1,0:T(8,128)(2,1)}, u32[]{:S(2)}, u32[]{:S(2)}) collective-permute-start(bf16[4,48,1664]{2,1,0:T(8,128)(2,1)S(1)} %collective-permute-done.10.refs_3_), channel_id=1, source_target_pairs={{0,1},{1,0},{2,3},{3,2},{4,5},{5,4},{6,7},{7,6},{8,9},{9,8},{10,11... | collective-permute-start | bytes 1916936 | tf_op jit(solution)/shard_map/ppermute | solution.py:840
  55.5 47.1 %collective-permute-start.16 = (bf16[4,48,3072]{2,1,0:T(8,128)(2,1)S(1)}, bf16[4,48,3072]{2,1,0:T(8,128)(2,1)}, u32[]{:S(2)}, u32[]{:S(2)}) collective-permute-start(bf16[4,48,3072]{2,1,0:T(8,128)(2,1)S(1)} %constant_dynamic-update-slice_fusion.8.refs_0_), channel_id=1, source_target_pairs={{0,1},{1,0},{2,3},{3,2},{4,5},{5,4},{6,7},{7,6},{8,9},{9,8},{10,11... | collective-permute-start | bytes 3538952 | tf_op jit(solution)/shard_map/ppermute | solution.py:840
  56.4 29.5 %collective-permute-start.6 = (bf16[4,48,3072]{2,1,0:T(8,128)(2,1)S(1)}, bf16[4,48,3072]{2,1,0:T(8,128)(2,1)}, u32[]{:S(2)}, u32[]{:S(2)}) collective-permute-start(bf16[4,48,3072]{2,1,0:T(8,128)(2,1)S(1)} %constant_dynamic-update-slice_fusion.8.refs_0_), channel_id=1, source_target_pairs={{0,4},{1,3},{2,6},{3,1},{4,0},{5,7},{6,2},{7,5},{8,12},{9,11},{10,... | collective-permute-start | bytes 3538952 | tf_op jit(solution)/shard_map/ppermute | solution.py:840
  59.2 26.7 %collective-permute-start.5 = (bf16[4,48,3072]{2,1,0:T(8,128)(2,1)S(1)}, bf16[4,48,3072]{2,1,0:T(8,128)(2,1)}, u32[]{:S(2)}, u32[]{:S(2)}) collective-permute-start(bf16[4,48,3072]{2,1,0:T(8,128)(2,1)S(1)} %constant_dynamic-update-slice_fusion.8.refs_0_), channel_id=1, source_target_pairs={{0,2},{1,5},{2,0},{3,7},{4,6},{5,1},{6,4},{7,3},{8,10},{9,13},{10,... | collective-permute-start | bytes 3538952 | tf_op jit(solution)/shard_map/ppermute | solution.py:840
  85.9 16.7 %collective-permute-start.17 = (bf16[4,48,3072]{2,1,0:T(8,128)(2,1)}, bf16[4,48,3072]{2,1,0:T(8,128)(2,1)}, u32[]{:S(2)}, u32[]{:S(2)}) collective-permute-start(bf16[4,48,3072]{2,1,0:T(8,128)(2,1)} %collective-permute-done.5.refs_1_), channel_id=1, source_target_pairs={{0,1},{1,0},{2,3},{3,2},{4,5},{5,4},{6,7},{7,6},{8,9},{9,8},{10,11... | collective-permute-start | bytes 3538952 | tf_op jit(solution)/shard_map/ppermute | solution.py:840
  86.0 16.6 %collective-permute-start.15 = (bf16[4,48,3072]{2,1,0:T(8,128)(2,1)}, bf16[4,48,3072]{2,1,0:T(8,128)(2,1)}, u32[]{:S(2)}, u32[]{:S(2)}) collective-permute-start(bf16[4,48,3072]{2,1,0:T(8,128)(2,1)} %collective-permute-done.5.refs_1_), channel_id=1, source_target_pairs={{0,4},{1,3},{2,6},{3,1},{4,0},{5,7},{6,2},{7,5},{8,12},{9,11},{10,... | collective-permute-start | bytes 3538952 | tf_op jit(solution)/shard_map/ppermute | solution.py:840
  88.2 14.4 %collective-permute-start.18 = (bf16[4,48,3072]{2,1,0:T(8,128)(2,1)}, bf16[4,48,3072]{2,1,0:T(8,128)(2,1)}, u32[]{:S(2)}, u32[]{:S(2)}) collective-permute-start(bf16[4,48,3072]{2,1,0:T(8,128)(2,1)} %collective-permute-done.6.refs_2_), channel_id=1, source_target_pairs={{0,1},{1,0},{2,3},{3,2},{4,5},{5,4},{6,7},{7,6},{8,9},{9,8},{10,11... | collective-permute-start | bytes 3538952 | tf_op jit(solution)/shard_map/ppermute | solution.py:840
  153.6 11.2 %collective-permute-start.20 = (bf16[16,48,1536]{2,1,0:T(8,128)(2,1)}, bf16[16,48,1536]{2,1,0:T(8,128)(2,1)}, u32[]{:S(2)}, u32[]{:S(2)}) collective-permute-start(bf16[16,48,1536]{2,1,0:T(8,128)(2,1)} %get-tuple-element.130), channel_id=1, source_target_pairs={{0,1},{1,0},{2,3},{3,2},{4,5},{5,4},{6,7},{7,6},{8,9},{9,8},{10,11... | collective-permute-start | bytes 7077896 | tf_op jit(solution)/shard_map/ppermute | solution.py:840
  167.8 9.4 %collective-permute-start.21 = (bf16[16,48,1920]{2,1,0:T(8,128)(2,1)}, bf16[16,48,1920]{2,1,0:T(8,128)(2,1)}, u32[]{:S(2)}, u32[]{:S(2)}) collective-permute-start(bf16[16,48,1920]{2,1,0:T(8,128)(2,1)} %get-tuple-element.141), channel_id=1, source_target_pairs={{0,1},{1,0},{2,3},{3,2},{4,5},{5,4},{6,7},{7,6},{8,9},{9,8},{10,11... | collective-permute-start | bytes 8847368 | tf_op jit(solution)/shard_map/ppermute | solution.py:840
  168.2 22.2 %collective-permute-start.22 = (bf16[8,48,1536]{2,1,0:T(8,128)(2,1)}, bf16[8,48,1536]{2,1,0:T(8,128)(2,1)}, u32[]{:S(2)}, u32[]{:S(2)}) collective-permute-start(bf16[8,48,1536]{2,1,0:T(8,128)(2,1)} %get-tuple-element.146), channel_id=1, source_target_pairs={{0,4},{1,3},{2,6},{3,1},{4,0},{5,7},{6,2},{7,5},{8,12},{9,11},{10,... | collective-permute-start | bytes 3538952 | tf_op jit(solution)/shard_map/ppermute | solution.py:840
  180.5 25.5 %collective-permute-start.23 = (bf16[8,48,1920]{2,1,0:T(8,128)(2,1)}, bf16[8,48,1920]{2,1,0:T(8,128)(2,1)}, u32[]{:S(2)}, u32[]{:S(2)}) collective-permute-start(bf16[8,48,1920]{2,1,0:T(8,128)(2,1)} %get-tuple-element.154), channel_id=1, source_target_pairs={{0,4},{1,3},{2,6},{3,1},{4,0},{5,7},{6,2},{7,5},{8,12},{9,11},{10,... | collective-permute-start | bytes 4423688 | tf_op jit(solution)/shard_map/ppermute | solution.py:840
  192.9 13.1 %collective-permute-start.24 = (bf16[4,48,1536]{2,1,0:T(8,128)(2,1)}, bf16[4,48,1536]{2,1,0:T(8,128)(2,1)}, u32[]{:S(2)}, u32[]{:S(2)}) collective-permute-start(bf16[4,48,1536]{2,1,0:T(8,128)(2,1)} %get-tuple-element.155), channel_id=1, source_target_pairs={{0,2},{1,5},{2,0},{3,7},{4,6},{5,1},{6,4},{7,3},{8,10},{9,13},{10,... | collective-permute-start | bytes 1769480 | tf_op jit(solution)/shard_map/ppermute | solution.py:840
  209.2 11.8 %collective-permute-start.25 = (bf16[4,48,1920]{2,1,0:T(8,128)(2,1)}, bf16[4,48,1920]{2,1,0:T(8,128)(2,1)}, u32[]{:S(2)}, u32[]{:S(2)}) collective-permute-start(bf16[4,48,1920]{2,1,0:T(8,128)(2,1)} %get-tuple-element.159), channel_id=1, source_target_pairs={{0,2},{1,5},{2,0},{3,7},{4,6},{5,1},{6,4},{7,3},{8,10},{9,13},{10,... | collective-permute-start | bytes 2211848 | tf_op jit(solution)/shard_map/ppermute | solution.py:840
  210.1 9.6 %collective-permute-start.26 = (bf16[2,48,1536]{2,1,0:T(8,128)(2,1)}, bf16[2,48,1536]{2,1,0:T(8,128)(2,1)S(1)}, u32[]{:S(2)}, u32[]{:S(2)}) collective-permute-start(bf16[2,48,1536]{2,1,0:T(8,128)(2,1)} %get-tuple-element.160), channel_id=1, source_target_pairs={{0,8},{1,17},{2,10},{3,19},{4,12},{5,21},{6,14},{7,23},{8,0},{9,25... | collective-permute-start | bytes 884744 | tf_op jit(solution)/shard_map/ppermute | solution.py:840
  221.0 4.3 %collective-permute-start.27 = (bf16[16,48,1280]{2,1,0:T(8,128)(2,1)}, bf16[16,48,1280]{2,1,0:T(8,128)(2,1)}, u32[]{:S(2)}, u32[]{:S(2)}) collective-permute-start(bf16[16,48,1280]{2,1,0:T(8,128)(2,1)} %gate.3), channel_id=1, source_target_pairs={{0,1},{1,0},{2,3},{3,2},{4,5},{5,4},{6,7},{7,6},{8,9},{9,8},{10,11... | collective-permute-start | bytes 5898248 | tf_op jit(solution)/shard_map/ppermute | solution.py:840
  228.0 15.1 %collective-permute-start.28 = (bf16[8,48,1280]{2,1,0:T(8,128)(2,1)}, bf16[8,48,1280]{2,1,0:T(8,128)(2,1)}, u32[]{:S(2)}, u32[]{:S(2)}) collective-permute-start(bf16[8,48,1280]{2,1,0:T(8,128)(2,1)} %get-tuple-element.164), channel_id=1, source_target_pairs={{0,4},{1,3},{2,6},{3,1},{4,0},{5,7},{6,2},{7,5},{8,12},{9,11},{10,... | collective-permute-start | bytes 2949128 | tf_op jit(solution)/shard_map/ppermute | solution.py:840
  229.1 12.8 %collective-permute-start.30 = (bf16[1,48,1536]{2,1,0:T(8,128)(2,1)}, bf16[1,48,1536]{2,1,0:T(8,128)(2,1)}, u32[]{:S(2)}, u32[]{:S(2)}) collective-permute-start(bf16[1,48,1536]{2,1,0:T(8,128)(2,1)} %get-tuple-element.166), channel_id=1, source_target_pairs={{0,16},{1,9},{2,18},{3,11},{4,20},{5,13},{6,22},{7,15},{8,24},{9,1... | collective-permute-start | bytes 442376 | tf_op jit(solution)/shard_map/ppermute | solution.py:840
  231.6 11.5 %collective-permute-start.29 = (bf16[2,48,1920]{2,1,0:T(8,128)(2,1)}, bf16[2,48,1920]{2,1,0:T(8,128)(2,1)S(1)}, u32[]{:S(2)}, u32[]{:S(2)}) collective-permute-start(bf16[2,48,1920]{2,1,0:T(8,128)(2,1)} %get-tuple-element.165), channel_id=1, source_target_pairs={{0,8},{1,17},{2,10},{3,19},{4,12},{5,21},{6,14},{7,23},{8,0},{9,25... | collective-permute-start | bytes 1105928 | tf_op jit(solution)/shard_map/ppermute | solution.py:840
  245.8 9.6 %collective-permute-start.31 = (bf16[4,48,1280]{2,1,0:T(8,128)(2,1)S(1)}, bf16[4,48,1280]{2,1,0:T(8,128)(2,1)S(1)}, u32[]{:S(2)}, u32[]{:S(2)}) collective-permute-start(bf16[4,48,1280]{2,1,0:T(8,128)(2,1)S(1)} %get-tuple-element.169), channel_id=1, source_target_pairs={{0,2},{1,5},{2,0},{3,7},{4,6},{5,1},{6,4},{7,3},{8,10},{9,13},{10,... | collective-permute-start | bytes 1474568 | tf_op jit(solution)/shard_map/ppermute | solution.py:840
  248.8 6.6 %collective-permute-start.32 = (bf16[1,48,1920]{2,1,0:T(8,128)(2,1)S(1)}, bf16[1,48,1920]{2,1,0:T(8,128)(2,1)S(1)}, u32[]{:S(2)}, u32[]{:S(2)}) collective-permute-start(bf16[1,48,1920]{2,1,0:T(8,128)(2,1)S(1)} %get-tuple-element.173), channel_id=1, source_target_pairs={{0,16},{1,9},{2,18},{3,11},{4,20},{5,13},{6,22},{7,15},{8,24},{9,1... | collective-permute-start | bytes 552968 | tf_op jit(solution)/shard_map/ppermute | solution.py:840
  256.1 7.9 %collective-permute-start.33 = (bf16[2,48,1280]{2,1,0:T(8,128)(2,1)S(1)}, bf16[2,48,1280]{2,1,0:T(8,128)(2,1)S(1)}, u32[]{:S(2)}, u32[]{:S(2)}) collective-permute-start(bf16[2,48,1280]{2,1,0:T(8,128)(2,1)S(1)} %get-tuple-element.176), channel_id=1, source_target_pairs={{0,8},{1,17},{2,10},{3,19},{4,12},{5,21},{6,14},{7,23},{8,0},{9,25... | collective-permute-start | bytes 737288 | tf_op jit(solution)/shard_map/ppermute | solution.py:840
  266.4 6.7 %collective-permute-start.34 = (bf16[1,48,1280]{2,1,0:T(8,128)(2,1)S(1)}, bf16[1,48,1280]{2,1,0:T(8,128)(2,1)S(1)}, u32[]{:S(2)}, u32[]{:S(2)}) collective-permute-start(bf16[1,48,1280]{2,1,0:T(8,128)(2,1)S(1)} %get-tuple-element.180), channel_id=1, source_target_pairs={{0,16},{1,9},{2,18},{3,11},{4,20},{5,13},{6,22},{7,15},{8,24},{9,1... | collective-permute-start | bytes 368648 | tf_op jit(solution)/shard_map/ppermute | solution.py:840
  (18 other events, 94.7 us)
